TPU v7x, 256 devices: a whole 4x4x8 slice. The times are simulated.
256 devices in a mesh: slab: 64 (over y, z, core), trans: 4 (over x).
Axes of the slice: x: 4, y: 4, z: 8, core: 2. Of those that a mesh axis runs over, the one named last changes fastest.
Arguments:
- start_block: float32 [32, 3, 128, 32, 128], P(None, None, 'slab', 'trans'), may hold values from -2500 to 2500
- material: int32 [128, 32, 128], P('slab', 'trans'), may hold values from 0 to 3
- pml_mask: int32 [128, 32, 128], P('slab', 'trans'), may hold values 0 or 1
- eps_table: float32 [4], replicated, may hold values from 1.5 to 12
Outputs:
- new_blocks: float32 [2, 32, 3, 128, 32, 128], P(None, None, None, 'slab', 'trans')
- couplings: float32 [2, 2, 32, 32], replicated
All inputs are finite; a program needn't handle non-finite values. No bound on the sum of `pml_mask` on one device may be relied on, other than what follows from the above.
Results may differ from a plain program's by a relative error of at most 0.0003.
Values sent between devices are 32-bit elements; how exact they have to be, the bound alone decides.
No kernel may reach another device: no remote copies, remote signals or barrier semaphores. Data moves between devices by JAX's collectives and lax.ppermute only.
A program may use at most 64 MiB of HBM per device.

v0:
```python
import jax
import jax.numpy as jnp
from jax import lax
from jax.sharding import PartitionSpec as P

STEPS = 2


PRECISE = lax.Precision.HIGHEST
SHIFT_SQUARED = 1.0
ABSORB = 4.0


def extended(value, sides, width):
    for axis, dim in sides:
        count, length = (lax.axis_size(axis), value.shape[dim])
        up = [(i, (i + 1) % count) for i in range(count - 1)]
        down = [(j, i) for i, j in up]
        last = lax.slice_in_dim(value, length - width, length, axis=dim)
        first = lax.slice_in_dim(value, 0, width, axis=dim)
        before = lax.ppermute(last, axis, up)
        after = lax.ppermute(first, axis, down)
        value = jnp.concatenate([before, value, after], axis=dim)
    return value


def forward(values, direction):
    first = values.ndim - 3
    length = values.shape[direction]
    difference = lax.slice_in_dim(values, 1, length, axis=direction) - lax.slice_in_dim(
        values, 0, length - 1, axis=direction
    )
    for spatial in range(first, first + 3):
        if spatial != direction:
            difference = lax.slice_in_dim(
                difference, 0, difference.shape[spatial] - 1, axis=spatial
            )
    return difference


def backward(values, direction):
    first = values.ndim - 3
    length = values.shape[direction]
    difference = lax.slice_in_dim(values, 1, length, axis=direction) - lax.slice_in_dim(
        values, 0, length - 1, axis=direction
    )
    for spatial in range(first, first + 3):
        if spatial != direction:
            difference = lax.slice_in_dim(difference, 1, difference.shape[spatial], axis=spatial)
    return difference


def curl_curl(padded):
    first = padded.ndim - 4
    widths = [(0, 0)] * (padded.ndim - 1) + [(1, 1)]
    padded = jnp.pad(padded, widths)
    field_x = lax.index_in_dim(padded, 0, axis=first, keepdims=False)
    field_y = lax.index_in_dim(padded, 1, axis=first, keepdims=False)
    field_z = lax.index_in_dim(padded, 2, axis=first, keepdims=False)
    axis_z, axis_x, axis_y = (first, first + 1, first + 2)
    curl_x = forward(field_z, axis_y) - forward(field_y, axis_z)
    curl_y = forward(field_x, axis_z) - forward(field_z, axis_x)
    curl_z = forward(field_y, axis_x) - forward(field_x, axis_y)
    result_x = backward(curl_z, axis_y) - backward(curl_y, axis_z)
    result_y = backward(curl_x, axis_z) - backward(curl_z, axis_x)
    result_z = backward(curl_y, axis_x) - backward(curl_x, axis_y)
    return jnp.stack([result_x, result_y, result_z], axis=first)


def coefficient(material, pml_mask, eps_table):
    permittivity = jnp.zeros(material.shape, eps_table.dtype)
    for level in range(eps_table.shape[0]):
        permittivity = permittivity + jnp.where(material == level, eps_table[level], 0.0)
    return SHIFT_SQUARED * permittivity + ABSORB * pml_mask.astype(eps_table.dtype)


def local_inner(left, right):
    return jnp.einsum("bczxy,dczxy->bd", left, right, precision=PRECISE)


def orthonormal(block, factor_low):
    identity = jnp.eye(factor_low.shape[0], dtype=factor_low.dtype)
    inverse = lax.linalg.triangular_solve(factor_low, identity, left_side=True, lower=True)
    return jnp.einsum("bd,dczxy->bczxy", inverse, block, precision=PRECISE)


def remove_projections(target, all_proj, earlier_list, width):
    for index_block in range(len(earlier_list)):
        weights = all_proj[index_block * width : (index_block + 1) * width]
        target = target - jnp.einsum(
            "bd,bczxy->dczxy", weights, earlier_list[index_block], precision=PRECISE
        )
    return target


def per_device(start_block, material, pml_mask, eps_table):
    width = start_block.shape[0]
    entries = float(
        3
        * start_block.shape[2]
        * start_block.shape[3]
        * start_block.shape[4]
        * lax.axis_size("slab")
        * lax.axis_size("trans")
    )
    diagonal = coefficient(material, pml_mask, eps_table)
    start_gram = lax.psum(local_inner(start_block, start_block), ("slab", "trans")) / entries
    start_low = jnp.linalg.cholesky(start_gram)
    blocks = [orthonormal(start_block, start_low)]
    couplings = []
    for iteration in range(STEPS):
        padded = extended(blocks[-1], (("slab", 2), ("trans", 3)), 1)
        applied = curl_curl(padded) + diagonal * blocks[-1]
        local_proj = jnp.concatenate([local_inner(earlier, applied) for earlier in blocks], axis=0)
        all_proj = lax.psum(local_proj, ("slab", "trans")) / entries
        applied = remove_projections(applied, all_proj, blocks, width)
        gram_matrix = lax.psum(local_inner(applied, applied), ("slab", "trans")) / entries
        factor_low = jnp.linalg.cholesky(gram_matrix)
        last_proj = all_proj[(len(blocks) - 1) * width :]
        couplings.append(jnp.stack([last_proj, factor_low.T]))
        blocks.append(orthonormal(applied, factor_low))
    return (jnp.stack(blocks[1:]), jnp.stack(couplings))


def solution(mesh):
    return jax.shard_map(
        per_device,
        mesh=mesh,
        in_specs=(
            P(None, None, "slab", "trans", None),
            P("slab", "trans", None),
            P("slab", "trans", None),
            P(),
        ),
        out_specs=(P(None, None, None, "slab", "trans", None), P()),
        check_vma=False,
    )
```

profile of v0, /device:TPU:2, one launch (start us, length us, event | category | flops | bytes accessed | tf_op | source)
XLA Modules:
  0.0 472.0 jit_solution(13045410438022967595)
XLA Ops:
  0.6 2.7 convolution_bitcast_fusion.6
  3.4 78.8 %psum.35 = f32[32,32]{0,1:T(8,128)S(1)} all-reduce(f32[32,32]{0,1:T(8,128)S(1)} %convolution_bitcast_fusion.6), channel_id=1, replica_groups=mesh['slab'=64,'trans'=4] {'slab','trans'}, use_global_device_ids=true, to_apply=%region_0.1 | all-reduce | flops 1024 | bytes 8192 | tf_op jit(solution)/shard_map/psum | solution.py:107
  82.3 2.9 cholesky.59
  85.2 0.6 compare_reduce_fusion.2
  85.9 0.7 fusion.33
  86.5 2.4 custom-call.7
  89.2 0.9 fusion.11
  90.3 1.3 collective-permute-start.1
  91.6 3.1 collective-permute-start
  94.6 0.6 fusion.77
  95.3 0.7 collective-permute-done
  96.0 4.6 collective-permute-start.3
  100.6 1.9 collective-permute-start.2
  102.5 2.6 multiply_add_fusion
  105.1 3.0 collective-permute-done.2
  108.2 2.1 select_maximum_fusion.4
  110.3 0.4 slice_bitcast_fusion.4
  110.7 0.6 fusion.59
  111.3 1.1 fusion.58
  112.4 0.4 fusion.57
  112.9 0.3 fusion.4
  113.5 0.3 fusion.5
  114.1 0.3 fusion.6
  115.0 0.4 fusion.27
  115.6 0.8 convolution_bitcast_fusion.5
  116.4 79.5 %psum.36 = f32[32,32]{0,1:T(8,128)S(1)} all-reduce(f32[32,32]{0,1:T(8,128)S(1)} %convolution_bitcast_fusion.5), channel_id=1, replica_groups=mesh['slab'=64,'trans'=4] {'slab','trans'}, use_global_device_ids=true, to_apply=%region_3.6 | all-reduce | flops 1024 | bytes 8192 | tf_op jit(solution)/shard_map/psum | solution.py:115
  196.0 0.8 convolution_subtract_fusion.2
  196.8 0.8 convolution_bitcast_fusion.4
  197.6 73.6 %psum.37 = f32[32,32]{0,1:T(8,128)S(1)} all-reduce(f32[32,32]{0,1:T(8,128)S(1)} %convolution_bitcast_fusion.4), channel_id=1, replica_groups=mesh['slab'=64,'trans'=4] {'slab','trans'}, use_global_device_ids=true, to_apply=%region_4.7 | all-reduce | flops 1024 | bytes 8192 | tf_op jit(solution)/shard_map/psum | solution.py:117
  271.2 2.9 cholesky.70
  274.2 0.6 compare_reduce_fusion.1
  274.8 0.7 fusion.47
  275.5 2.4 custom-call.8
  278.2 0.8 fusion.78
  279.0 1.3 collective-permute-start.5
  280.3 3.1 collective-permute-start.4
  283.4 1.3 collective-permute-done.4
  284.7 3.0 collective-permute-start.7
  287.7 2.9 collective-permute-start.6
  290.6 1.7 collective-permute-done.7
  292.3 3.0 collective-permute-done.6
  295.3 2.1 select_maximum_fusion
  297.4 0.5 slice_bitcast_fusion.1
  297.9 0.5 fusion.55
  299.0 0.5 fusion.52
  299.6 0.3 fusion.51
  299.9 0.3 fusion.1
  300.6 0.3 fusion.2
  301.2 0.3 fusion.3
  302.2 0.3 fusion.21
  302.7 0.8 convolution_bitcast_fusion.2
  303.5 0.8 convolution_bitcast_fusion.3
  304.4 80.8 %psum.38 = f32[64,32]{0,1:T(8,128)S(1)} all-reduce(f32[64,32]{0,1:T(8,128)S(1)} %pad_maximum_fusion.8), channel_id=1, replica_groups=mesh['slab'=64,'trans'=4] {'slab','trans'}, use_global_device_ids=true, to_apply=%region_5.8 | all-reduce | flops 2048 | bytes 16384 | tf_op jit(solution)/shard_map/psum | solution.py:115
  385.2 0.8 convolution_subtract_fusion.1
  386.1 0.8 convolution_subtract_fusion
  387.0 0.8 convolution_bitcast_fusion.1
  387.7 73.6 %psum.39 = f32[32,32]{0,1:T(8,128)S(1)} all-reduce(f32[32,32]{0,1:T(8,128)S(1)} %convolution_bitcast_fusion.1), channel_id=1, replica_groups=mesh['slab'=64,'trans'=4] {'slab','trans'}, use_global_device_ids=true, to_apply=%region_6.9 | all-reduce | flops 1024 | bytes 8192 | tf_op jit(solution)/shard_map/psum | solution.py:117
  461.4 2.9 cholesky.81
  464.3 0.6 compare_reduce_fusion
  465.0 0.7 fusion.48
  465.6 2.4 custom-call.9
  468.3 0.8 convolution_bitcast_fusion
  469.2 2.1 copy.26
  471.3 0.7 copy.27
  (57 shorter events, 5.0 us)
Async XLA Ops:
  0.6 88.6 %copy-start = (f32[32,3,2,8,128]{4,3,2,1,0:T(8,128)S(1)}, f32[32,3,2,8,128]{4,3,2,1,0:T(8,128)}, u32[]{:S(2)}) copy-start(f32[32,3,2,8,128]{4,3,2,1,0:T(8,128)} %param.7) | copy-start | bytes 2359300
  89.2 5.4 %copy-start.3 = (f32[4]{0:T(128)S(1)}, f32[4]{0:T(128)}, u32[]{:S(2)}) copy-start(f32[4]{0:T(128)} %param.10) | copy-start | bytes 52
  90.3 12.3 %copy-start.1 = (s32[2,8,128]{2,1,0:T(8,128)S(1)}, s32[2,8,128]{2,1,0:T(8,128)}, u32[]{:S(2)}) copy-start(s32[2,8,128]{2,1,0:T(8,128)} %param.9) | copy-start | bytes 24580
  90.3 12.3 %copy-start.2 = (s32[2,8,128]{2,1,0:T(8,128)S(1)}, s32[2,8,128]{2,1,0:T(8,128)}, u32[]{:S(2)}) copy-start(s32[2,8,128]{2,1,0:T(8,128)} %param.8) | copy-start | bytes 24580
  90.3 5.0 %collective-permute-start.1 = (f32[32,3,1,8,128]{4,0,3,2,1:T(8,128)S(1)}, f32[32,3,1,8,128]{4,0,3,2,1:T(8,128)S(1)}, u32[]{:S(2)}, u32[]{:S(2)}) collective-permute-start(f32[32,3,1,8,128]{4,0,3,2,1:T(8,128)S(1)} %get-tuple-element.67), channel_id=1, source_target_pairs={{4,0},{8,4},{12,8},{16,12},{20,16},{24,20},{28,24},{32,28},{36,32}... | collective-permute-start | bytes 1179656 | tf_op jit(solution)/shard_map/ppermute | solution.py:22
  91.6 4.4 collective-permute-start
  96.0 9.1 %collective-permute-start.3 = (f32[32,3,4,1,128]{4,0,3,2,1:T(8,128)S(1)}, f32[32,3,4,1,128]{4,0,3,2,1:T(8,128)S(1)}, u32[]{:S(2)}, u32[]{:S(2)}) collective-permute-start(f32[32,3,4,1,128]{4,0,3,2,1:T(8,128)S(1)} %get-tuple-element.15), channel_id=1, source_target_pairs={{1,0},{2,1},{3,2},{5,4},{6,5},{7,6},{9,8},{10,9},{11,10},{13,12},{... | collective-permute-start | bytes 589832 | tf_op jit(solution)/shard_map/ppermute | solution.py:22
  100.6 7.6 %collective-permute-start.2 = (f32[32,3,4,1,128]{4,0,3,2,1:T(8,128)S(1)}, f32[32,3,4,1,128]{4,0,3,2,1:T(8,128)S(1)}, u32[]{:S(2)}, u32[]{:S(2)}) collective-permute-start(f32[32,3,4,1,128]{4,0,3,2,1:T(8,128)S(1)} %get-tuple-element.14), channel_id=1, source_target_pairs={{0,1},{1,2},{2,3},{4,5},{5,6},{6,7},{8,9},{9,10},{10,11},{12,13},{... | collective-permute-start | bytes 589832 | tf_op jit(solution)/shard_map/ppermute | solution.py:21
  279.0 4.4 collective-permute-start.5
  280.3 4.4 collective-permute-start.4
  284.7 7.6 %collective-permute-start.7 = (f32[32,3,4,1,128]{4,0,3,2,1:T(8,128)S(1)}, f32[32,3,4,1,128]{4,0,3,2,1:T(8,128)S(1)}, u32[]{:S(2)}, u32[]{:S(2)}) collective-permute-start(f32[32,3,4,1,128]{4,0,3,2,1:T(8,128)S(1)} %get-tuple-element.13), channel_id=1, source_target_pairs={{1,0},{2,1},{3,2},{5,4},{6,5},{7,6},{9,8},{10,9},{11,10},{13,12},{... | collective-permute-start | bytes 589832 | tf_op jit(solution)/shard_map/ppermute | solution.py:22
  287.7 7.6 %collective-permute-start.6 = (f32[32,3,4,1,128]{4,0,3,2,1:T(8,128)S(1)}, f32[32,3,4,1,128]{4,0,3,2,1:T(8,128)S(1)}, u32[]{:S(2)}, u32[]{:S(2)}) collective-permute-start(f32[32,3,4,1,128]{4,0,3,2,1:T(8,128)S(1)} %get-tuple-element.12), channel_id=1, source_target_pairs={{0,1},{1,2},{2,3},{4,5},{5,6},{6,7},{8,9},{9,10},{10,11},{12,13},{... | collective-permute-start | bytes 589832 | tf_op jit(solution)/shard_map/ppermute | solution.py:21
where the time goes:
time: 475 us; the launch traced here: 472 us
  blocking collectives  386 us (81%)
  other arithmetic  30.7 us (6%)
  starting transfers between devices  21.1 us (4%)
  matrix products  12.4 us (3%)
  local copies, waits for them, and re-layouts  10.7 us (2%)
  waiting for transfers between devices  9.63 us (2%)
    psum x2, blocking collectives, per_device(): all_proj = lax.psum(local_proj, ('slab', 'trans')) / entries  160 us
    psum x2, blocking collectives, per_device(): lax.psum(local_inner(applied, applied), ('slab', 'trans')) / entries  147 us
    psum x1, blocking collectives, per_device(): lax.psum(local_inner(start_block, start_block), ('slab', 'trans')) / entries  78.8 us
    ppermute x4, starting transfers between devices, extended(): before = lax.ppermute(last, axis, up)  10.9 us
    ppermute x4, starting transfers between devices, extended(): after = lax.ppermute(first, axis, down)  10.1 us
  transfers between devices with their start and end apart: 8, of which 5 were waited for; matrix products, arithmetic and copies ran while one was open for 1% of the time, Pallas kernels for 0%

commit v1 on v0

v1 whole, which is shorter than its diff:
```python
import functools

import jax
import jax.numpy as jnp
from jax import lax
from jax.experimental import pallas as pl
from jax.experimental.pallas import tpu as pltpu
from jax.sharding import PartitionSpec as P

AXES = ("slab", "trans")
ABSORB = 4.0
CURL_CENTRE = 5.0
VMEM_LIMIT = 40 * 1024 * 1024


def call(body, out_shape, operands, smem=(), flops=0):
    specs = [
        pl.BlockSpec(memory_space=pltpu.SMEM if i in smem else pltpu.VMEM)
        for i in range(len(operands))
    ]
    outs = [pl.BlockSpec(memory_space=pltpu.VMEM) for _ in out_shape]
    moved = sum(4 * a.size for a in operands) + sum(
        4 * functools.reduce(lambda p, q: p * q, s.shape) for s in out_shape
    )
    return pl.pallas_call(
        body,
        out_shape=out_shape,
        in_specs=specs,
        out_specs=outs,
        compiler_params=pltpu.CompilerParams(vmem_limit_bytes=VMEM_LIMIT),
        cost_estimate=pl.CostEstimate(flops=flops, bytes_accessed=moved, transcendentals=0),
    )(*operands)


def shape(*dims):
    return jax.ShapeDtypeStruct(dims, jnp.float32)


def edge_shapes(zs, xs, width, ny):
    return [
        shape(3, xs, width, ny),
        shape(2, xs, width, ny),
        shape(zs, 3, width, ny),
        shape(zs, 2, width, ny),
        shape(width, ny),
        shape(width, ny),
    ]


def store_edges(edges, zs, xs, z, c, x, value):
    up_z, down_z, up_x, down_x, corner_up, corner_down = edges
    if z == zs - 1:
        up_z[c, x] = value
    if z == 0 and c < 2:
        down_z[c, x] = value
    if x == xs - 1:
        up_x[z, c] = value
    if x == 0 and c > 0:
        down_x[z, c - 1] = value
    if z == zs - 1 and x == 0 and c == 2:
        corner_up[...] = value
    if z == 0 and x == xs - 1 and c == 0:
        corner_down[...] = value


def split_body(zs, xs, width, start, field, *edges):
    rows = 3 * zs * xs
    for z in range(zs):
        for c in range(3):
            for x in range(xs):
                value = start[pl.ds((c * zs + z) * xs + x, width, stride=rows), :]
                field[z, c, x] = value
                store_edges(edges, zs, xs, z, c, x, value)


def apply_field(zs, xs, field, halo, diagonal, lane, last, put):
    before_z, after_z, before_x, after_x, corner_up, corner_down = halo

    def e(c, z, x):
        if z == -1:
            return corner_up[...] if x == xs else before_z[c, x]
        if z == zs:
            return corner_down[...] if x == -1 else after_z[c, x]
        if x == -1:
            return before_x[z, c]
        if x == xs:
            return after_x[z, c - 1]
        return field[z, c, x]

    def step_y(value):
        return jnp.where(lane == last, 0.0, pltpu.roll(value, last, 1)) - value

    def curl_x(z, x):
        return step_y(e(2, z, x)) - (e(1, z + 1, x) - e(1, z, x))

    def curl_y(z, x):
        return (e(0, z + 1, x) - e(0, z, x)) - (e(2, z, x + 1) - e(2, z, x))

    def curl_z(z, x):
        return (e(1, z, x + 1) - e(1, z, x)) - step_y(e(0, z, x))

    old_y = {z: curl_y(z, -1) for z in range(zs)}
    old_z = {z: curl_z(z, -1) for z in range(zs)}
    for x in range(xs):
        below_x, below_y = curl_x(-1, x), curl_y(-1, x)
        for z in range(zs):
            h_x, h_y, h_z = curl_x(z, x), curl_y(z, x), curl_z(z, x)
            e_x, e_y, e_z = e(0, z, x), e(1, z, x), e(2, z, x)
            d = diagonal(z, x)
            prev_z = jnp.where(lane == 0, -e_x, pltpu.roll(h_z, 1, 1))
            prev_x = jnp.where(lane == 0, e_z, pltpu.roll(h_x, 1, 1))
            put(z, 0, x, (h_z - prev_z) - (h_y - below_y) + d * e_x)
            put(z, 1, x, (h_x - below_x) - (h_z - old_z[z]) + d * e_y)
            put(z, 2, x, (h_y - old_y[z]) - (h_x - prev_x) + d * e_z)
            below_x, below_y = h_x, h_y
            old_y[z], old_z[z] = h_y, h_z


def lanes(width, ny):
    return lax.broadcasted_iota(jnp.int32, (width, ny), 1)


def first_body(zs, xs, width, ny, classes, *refs):
    eps, material, mask, field = refs[:4]
    halo, result, diag, edges = refs[4:10], refs[10], refs[11], refs[12:]
    total = eps[0]
    for level in range(1, classes):
        total = total + eps[level]
    shift = total / classes + CURL_CENTRE
    value = jnp.zeros(material.shape, jnp.float32)
    for level in range(classes):
        value = value + jnp.where(material[...] == level, eps[level], 0.0)
    diag[...] = value + ABSORB * mask[...].astype(jnp.float32) - shift

    def put(z, c, x, cell):
        result[z, c, x] = cell
        store_edges(edges, zs, xs, z, c, x, cell)

    apply_field(
        zs, xs, field, halo, lambda z, x: diag[z, x : x + 1, :], lanes(width, ny), ny - 1, put
    )


def parts3(value):
    high = value.astype(jnp.bfloat16)
    rest = value - high.astype(jnp.float32)
    middle = rest.astype(jnp.bfloat16)
    low = (rest - middle.astype(jnp.float32)).astype(jnp.bfloat16)
    return [high, middle, low]


def pair(ref, z, c, x):
    return jnp.concatenate([ref[z, c, x], ref[z, c, x + 1]], axis=1)


def product(left, right):
    return lax.dot_general(
        left, right, (((1,), (1,)), ((), ())), preferred_element_type=jnp.float32
    )


def fold(total, width, left, right):
    rows = sum(total[i * left * width : (i + 1) * left * width] for i in range(3))
    return sum(rows[:, i * right * width : (i + 1) * right * width] for i in range(3))


def early_gram_body(zs, xs, width, s0, s1, out):
    total = None
    for z in range(zs):
        for c in range(3):
            for x in range(0, xs, 2):
                both = jnp.concatenate([pair(s0, z, c, x), pair(s1, z, c, x)], axis=0)
                stack = jnp.concatenate(parts3(both), axis=0)
                term = product(stack, stack)
                total = term if total is None else total + term
    gram = fold(total, width, 2, 2)
    out[0] = gram[:width, :width]
    out[1] = gram[:width, width:]
    out[2] = gram[width:, width:]


def second_body(zs, xs, width, ny, *refs):
    diag, s1, halo, s2, out = refs[0], refs[1], refs[2:8], refs[8], refs[9]

    def put(z, c, x, cell):
        s2[z, c, x] = cell

    apply_field(
        zs, xs, s1, halo, lambda z, x: diag[z, x : x + 1, :], lanes(width, ny), ny - 1, put
    )
    total = None
    for z in range(zs):
        for c in range(3):
            for x in range(0, xs, 2):
                one, two = parts3(pair(s1, z, c, x)), parts3(pair(s2, z, c, x))
                stack = jnp.concatenate(
                    [jnp.concatenate([p, q], axis=0) for p, q in zip(one, two)], axis=0
                )
                term = product(stack, jnp.concatenate(two, axis=0))
                total = term if total is None else total + term
    gram = fold(total, width, 2, 1)
    out[0] = gram[:width]
    out[1] = gram[width:]


def precise(left, right, contract):
    return lax.dot_general(
        left,
        right,
        (((1,), (contract,)), ((), ())),
        precision=lax.Precision.HIGHEST,
        preferred_element_type=jnp.float32,
    )


def factor(gram, size):
    tiles = size // 8
    row8 = lax.broadcasted_iota(jnp.int32, (8, 1), 0)
    lane = lax.broadcasted_iota(jnp.int32, (8, size), 1)
    sub = lax.broadcasted_iota(jnp.int32, (8, size), 0)
    upper = [gram[8 * t : 8 * t + 8, :] for t in range(tiles)]
    inverse = [jnp.where(lane == sub + 8 * t, 1.0, 0.0) for t in range(tiles)]
    scales = []
    for t in range(tiles):
        cols = {
            u: [
                jnp.broadcast_to(upper[u][:, 8 * t + j : 8 * t + j + 1], (8, size))
                for j in range(8)
            ]
            for u in range(t, tiles)
        }
        pivots = jnp.zeros((8, size), jnp.float32)
        for s in range(8):
            pivot = jnp.broadcast_to(cols[t][s][s : s + 1, :], (8, size))
            pivots = jnp.where(sub == s, pivot, pivots)
            reciprocal = 1.0 / pivot
            heads = [cols[t][j][s : s + 1, :] for j in range(8)]
            row_u, row_i = upper[t][s : s + 1, :], inverse[t][s : s + 1, :]
            for u in range(t, tiles):
                f = cols[u][s] * reciprocal
                if u == t:
                    f = jnp.where(sub > s, f, 0.0)
                for j in range(s + 1, 8):
                    cols[u][j] = cols[u][j] - f * heads[j]
                upper[u] = upper[u] - f * row_u
                inverse[u] = inverse[u] - f * row_i
        scales.append(lax.rsqrt(pivots))
    upper = [a * s for a, s in zip(upper, scales)]
    inverse = [a * s for a, s in zip(inverse, scales)]
    return jnp.concatenate(upper, axis=0), jnp.concatenate(inverse, axis=0)


def last_body(zs, xs, width, ny, classes, entries, eps, moments, s0, s1, s2, out, couplings):
    total = eps[0]
    for level in range(1, classes):
        total = total + eps[level]
    shift = total / classes + CURL_CENTRE
    m = [moments[k] * (1.0 / entries) for k in range(5)]
    m = [0.5 * (a + a.T) for a in m]
    gram = jnp.concatenate(
        [jnp.concatenate([m[i + j] for j in range(3)], axis=1) for i in range(3)], axis=0
    )
    upper, inverse = factor(gram, 3 * width)
    w = width
    identity = jnp.where(
        lax.broadcasted_iota(jnp.int32, (w, w), 0) == lax.broadcasted_iota(jnp.int32, (w, w), 1),
        shift,
        0.0,
    )
    x0, x1 = inverse[:w, :w], inverse[w : 2 * w, w : 2 * w]
    u01, u11 = upper[:w, w : 2 * w], upper[w : 2 * w, w : 2 * w]
    u12, u22 = upper[w : 2 * w, 2 * w :], upper[2 * w :, 2 * w :]
    factor_one = precise(u11, x0, 1)
    couplings[0, 0] = precise(u01, x0, 1) + identity
    couplings[0, 1] = factor_one
    couplings[1, 0] = precise(u12 - precise(factor_one, u01, 0), x1, 1) + identity
    couplings[1, 1] = precise(u22, x1, 1)
    mix = inverse[w:]
    rows = 3 * zs * xs
    for z in range(zs):
        for c in range(3):
            for x in range(0, xs, 2):
                basis = jnp.concatenate([pair(s, z, c, x) for s in (s0, s1, s2)], axis=0)
                value = precise(mix, basis, 0)
                for k in range(2):
                    out[pl.ds((c * zs + z) * xs + x + k, 2 * w, stride=rows), :] = value[
                        :, k * ny : (k + 1) * ny
                    ]


def exchange(edges, slabs, trans):
    up_z, down_z, up_x, down_x, corner_up, corner_down = edges

    def moved(value, dz, dx):
        pairs = [
            (i * trans + j, (i + dz) * trans + j + dx)
            for i in range(slabs)
            for j in range(trans)
            if 0 <= i + dz < slabs and 0 <= j + dx < trans
        ]
        return lax.ppermute(value, AXES, pairs)

    return [
        moved(up_z, 1, 0),
        moved(down_z, -1, 0),
        moved(up_x, 0, 1),
        moved(down_x, 0, -1),
        moved(corner_up, 1, -1),
        moved(corner_down, -1, 1),
    ]


def total_sum(value, slabs, trans):
    devices = slabs * trans
    bits = devices.bit_length() - 1
    if bits == 8:
        groups = [(0, 1), (6, 7), (2, 3), (4, 5)]
    else:
        groups = [(b,) for b in range(bits)]
    for group in groups:
        masks = [0]
        for b in group:
            masks += [m ^ (1 << b) for m in masks]
        got = [
            lax.ppermute(value, AXES, [(i, i ^ m) for i in range(devices)]) for m in masks[1:]
        ]
        for other in got:
            value = value + other
    return value


def per_device(slabs, trans, start_block, material, pml_mask, eps_table):
    width, _, zs, xs, ny = start_block.shape
    classes = eps_table.shape[0]
    entries = float(3 * zs * xs * ny * slabs * trans)
    field = shape(zs, 3, xs, width, ny)
    edges = edge_shapes(zs, xs, width, ny)
    rows = width * 3 * zs * xs

    s0, *e0 = call(
        functools.partial(split_body, zs, xs, width),
        [field] + edges,
        [start_block.reshape(rows, ny)],
    )
    h0 = exchange(e0, slabs, trans)
    s1, diag, *e1 = call(
        functools.partial(first_body, zs, xs, width, ny, classes),
        [field, shape(zs, xs, ny)] + edges,
        [eps_table, material, pml_mask, s0] + h0,
        smem=(0,),
    )
    h1 = exchange(e1, slabs, trans)
    (early,) = call(
        functools.partial(early_gram_body, zs, xs, width), [shape(3, width, width)], [s0, s1]
    )
    s2, late = call(
        functools.partial(second_body, zs, xs, width, ny),
        [field, shape(2, width, width)],
        [diag, s1] + h1,
    )
    moments = jnp.concatenate([early, late], axis=0)
    moments = total_sum(moments.reshape(-1, 128), slabs, trans).reshape(5, width, width)
    blocks, couplings = call(
        functools.partial(last_body, zs, xs, width, ny, classes, entries),
        [shape(2 * rows, ny), shape(2, 2, width, width)],
        [eps_table, moments, s0, s1, s2],
        smem=(0,),
    )
    return blocks.reshape(2, width, 3, zs, xs, ny), couplings


def solution(mesh):
    sizes = dict(zip(mesh.axis_names, mesh.devices.shape))
    return jax.shard_map(
        functools.partial(per_device, sizes["slab"], sizes["trans"]),
        mesh=mesh,
        in_specs=(
            P(None, None, "slab", "trans", None),
            P("slab", "trans", None),
            P("slab", "trans", None),
            P(),
        ),
        out_specs=(P(None, None, None, "slab", "trans", None), P()),
        check_vma=False,
    )
```

time: 475 us -> 97.2 us (0.20)
  blocking collectives: 386 us -> 0 us
  starting transfers between devices: 21.1 us -> 60.6 us
  other arithmetic: 30.7 us -> 0.04 us
  matrix products: 12.4 us -> 0 us
  waiting for transfers between devices: 9.63 us -> 21.1 us
  Pallas kernels: 0 us -> 10.7 us
  local copies, waits for them, and re-layouts: 10.7 us -> 3.33 us
    psum x5 -> x0, blocking collectives: 386 us -> none  [the longest x2 160 us: per_device(): all_proj = lax.psum(local_proj, ('slab', 'trans')) / entries]
    ppermute x8 -> x24, starting transfers between devices: 21.1 us -> 60.6 us  [the longest x12 31 us: moved(): return lax.ppermute(value, AXES, pairs)]
    another operation x26 -> x0, other arithmetic: 21.7 us -> none  [the longest x4 7.96 us: orthonormal(): lax.linalg.triangular_solve(factor_low, identity, left_side=True, lower=T...]
    dot_general x12 -> x0, matrix products: 11.7 us -> none  [the longest x6 6.7 us: local_inner(): return jnp.einsum('bczxy,dczxy->bd', left, right, precision=PRECISE)]
    ppermute x8 -> x24, waiting for transfers between devices: 9.63 us -> 21.1 us  [the longest x12 11.6 us: total_sum(): lax.ppermute(value, AXES, [(i, i ^ m) for i in range(devices)])]
    pallas_call x0 -> x5, Pallas kernels: none -> 10.7 us  [call(): pl.pallas_call(body, out_shape=out_shape, in_specs=specs, out_specs=outs,...]
    slice x24 -> x0, local copies, waits for them, and re-layouts: 6.67 us -> none  [the longest x9 4.02 us: forward(): lax.slice_in_dim(values, 1, length, axis=direction)]
  transfers between devices with their start and end apart: 8 -> 24, of which waited for: 5 -> 11; matrix products, arithmetic and copies ran while one was open for 1% -> 0% of each run, Pallas kernels for 0% -> 1%
where the time goes in v1:
time: 97.2 us; the launch traced here: 96.6 us
  starting transfers between devices  60.6 us (62%)
  waiting for transfers between devices  21.1 us (22%)
  Pallas kernels  10.7 us (11%)
  local copies, waits for them, and re-layouts  3.33 us (3%)
    ppermute x12, starting transfers between devices, moved(): return lax.ppermute(value, AXES, pairs)  31 us
    ppermute x12, starting transfers between devices, total_sum(): lax.ppermute(value, AXES, [(i, i ^ m) for i in range(devices)])  29.6 us
    ppermute x12, waiting for transfers between devices, total_sum(): lax.ppermute(value, AXES, [(i, i ^ m) for i in range(devices)])  11.6 us
    pallas_call x5, Pallas kernels, call(): pl.pallas_call(body, out_shape=out_shape, in_specs=specs, out_specs=outs,...  10.7 us
    ppermute x12, waiting for transfers between devices, moved(): return lax.ppermute(value, AXES, pairs)  9.45 us
    unnamed x10, local copies, waits for them, and re-layouts  3.17 us
  transfers between devices with their start and end apart: 24, of which 11 were waited for; matrix products, arithmetic and copies ran while one was open for 0% of the time, Pallas kernels for 1%

profile of v1, /device:TPU:2, one launch (start us, length us, event | category | flops | bytes accessed | tf_op | source)
XLA Modules:
  0.0 96.6 jit_solution(583985264353013576)
XLA Ops:
  0.6 0.0 copy-start
  0.6 1.1 %copy-done = f32[32,3,2,8,128]{4,3,2,1,0:T(8,128)S(1)} copy-done((f32[32,3,2,8,128]{4,3,2,1,0:T(8,128)S(1)}, f32[32,3,2,8,128]{4,3,2,1,0:T(8,128)}, u32[]{:S(2)}) %copy-start) | copy-done | bytes 786456
  1.8 0.3 shard_map.59
  2.0 1.8 %collective-permute-start = (f32[3,8,32,128]{3,2,1,0:T(8,128)S(1)}, f32[3,8,32,128]{3,2,1,0:T(8,128)S(1)}, u32[]{:S(2)}, u32[]{:S(2)}) collective-permute-start(f32[3,8,32,128]{3,2,1,0:T(8,128)S(1)} %get-tuple-element.22), channel_id=1, source_target_pairs={{0,4},{1,5},{2,6},{3,7},{4,8},{5,9},{6,10},{7,11},{8,12},{9,13},{1... | collective-permute-start | bytes 1179656 | tf_op jit(solution)/shard_map/ppermute | solution.py:301
  3.8 1.3 %collective-permute-start.1 = (f32[2,8,32,128]{3,2,1,0:T(8,128)S(1)}, f32[2,8,32,128]{3,2,1,0:T(8,128)S(1)}, u32[]{:S(2)}, u32[]{:S(2)}) collective-permute-start(f32[2,8,32,128]{3,2,1,0:T(8,128)S(1)} %get-tuple-element.23), channel_id=1, source_target_pairs={{4,0},{5,1},{6,2},{7,3},{8,4},{9,5},{10,6},{11,7},{12,8},{13,9},{1... | collective-permute-start | bytes 786440 | tf_op jit(solution)/shard_map/ppermute | solution.py:301
  5.1 3.4 %collective-permute-start.2 = (f32[2,3,32,128]{3,2,1,0:T(8,128)S(1)}, f32[2,3,32,128]{3,2,1,0:T(8,128)S(1)}, u32[]{:S(2)}, u32[]{:S(2)}) collective-permute-start(f32[2,3,32,128]{3,2,1,0:T(8,128)S(1)} %get-tuple-element.24), channel_id=1, source_target_pairs={{0,1},{1,2},{2,3},{4,5},{5,6},{6,7},{8,9},{9,10},{10,11},{12,13},{... | collective-permute-start | bytes 294920 | tf_op jit(solution)/shard_map/ppermute | solution.py:301
  8.5 2.4 %collective-permute-start.3 = (f32[2,2,32,128]{3,2,1,0:T(8,128)S(1)}, f32[2,2,32,128]{3,2,1,0:T(8,128)S(1)}, u32[]{:S(2)}, u32[]{:S(2)}) collective-permute-start(f32[2,2,32,128]{3,2,1,0:T(8,128)S(1)} %get-tuple-element.25), channel_id=1, source_target_pairs={{1,0},{2,1},{3,2},{5,4},{6,5},{7,6},{9,8},{10,9},{11,10},{13,12},{... | collective-permute-start | bytes 196616 | tf_op jit(solution)/shard_map/ppermute | solution.py:301
  11.0 3.4 %collective-permute-start.4 = (f32[32,128]{1,0:T(8,128)S(1)}, f32[32,128]{1,0:T(8,128)S(1)}, u32[]{:S(2)}, u32[]{:S(2)}) collective-permute-start(f32[32,128]{1,0:T(8,128)S(1)} %get-tuple-element.26), channel_id=1, source_target_pairs={{1,4},{2,5},{3,6},{5,8},{6,9},{7,10},{9,12},{10,13},{11,14},{13,16... | collective-permute-start | bytes 49160 | tf_op jit(solution)/shard_map/ppermute | solution.py:301
  14.4 1.4 %collective-permute-done.4.refs_8_ = f32[32,128]{1,0:T(8,128)S(1)} collective-permute-done((f32[32,128]{1,0:T(8,128)S(1)}, f32[32,128]{1,0:T(8,128)S(1)}, u32[]{:S(2)}, u32[]{:S(2)}) %collective-permute-start.4) | collective-permute-done | bytes 16416 | tf_op jit(solution)/shard_map/ppermute | solution.py:301
  15.8 1.3 %collective-permute-start.5 = (f32[32,128]{1,0:T(8,128)S(1)}, f32[32,128]{1,0:T(8,128)S(1)}, u32[]{:S(2)}, u32[]{:S(2)}) collective-permute-start(f32[32,128]{1,0:T(8,128)S(1)} %get-tuple-element.27), channel_id=1, source_target_pairs={{4,1},{5,2},{6,3},{8,5},{9,6},{10,7},{12,9},{13,10},{14,11},{16,13... | collective-permute-start | bytes 49160 | tf_op jit(solution)/shard_map/ppermute | solution.py:301
  17.1 3.8 %collective-permute-done.5.refs_9_ = f32[32,128]{1,0:T(8,128)S(1)} collective-permute-done((f32[32,128]{1,0:T(8,128)S(1)}, f32[32,128]{1,0:T(8,128)S(1)}, u32[]{:S(2)}, u32[]{:S(2)}) %collective-permute-start.5) | collective-permute-done | bytes 16416 | tf_op jit(solution)/shard_map/ppermute | solution.py:301
  20.9 0.0 collective-permute-done.3.refs_7_
  20.9 0.0 collective-permute-done.2.refs_6_
  20.9 0.0 collective-permute-done.1.refs_5_
  20.9 0.0 collective-permute-done.refs_4_
  20.9 0.0 copy-start.1
  20.9 0.7 copy-done.1
  21.6 0.0 copy-start.2
  21.6 0.7 copy-done.2
  22.3 0.0 copy-start.3
  22.3 0.7 copy-done.3
  22.9 1.6 %shard_map.60 = (f32[2,3,8,32,128]{4,3,2,1,0:T(8,128)S(1)}, f32[2,8,128]{2,1,0:T(8,128)S(1)}, f32[3,8,32,128]{3,2,1,0:T(8,128)S(1)}, f32[2,8,32,128]{3,2,1,0:T(8...) custom-call(f32[4]{0:T(128)S(1)} %copy-done.3, ...), custom_call_target="tpu_custom_call" | custom-call | bytes 3301392 | tf_op jit(solution)/shard_map/pallas_call | solution.py:25
  24.5 5.3 %collective-permute-start.6 = (f32[3,8,32,128]{3,2,1,0:T(8,128)S(1)}, f32[3,8,32,128]{3,2,1,0:T(8,128)S(1)}, u32[]{:S(2)}, u32[]{:S(2)}) collective-permute-start(f32[3,8,32,128]{3,2,1,0:T(8,128)S(1)} %get-tuple-element.30), channel_id=1, source_target_pairs={{0,4},{1,5},{2,6},{3,7},{4,8},{5,9},{6,10},{7,11},{8,12},{9,13},{1... | collective-permute-start | bytes 1179656 | tf_op jit(solution)/shard_map/ppermute | solution.py:301
  29.8 1.3 %collective-permute-start.7 = (f32[2,8,32,128]{3,2,1,0:T(8,128)S(1)}, f32[2,8,32,128]{3,2,1,0:T(8,128)S(1)}, u32[]{:S(2)}, u32[]{:S(2)}) collective-permute-start(f32[2,8,32,128]{3,2,1,0:T(8,128)S(1)} %get-tuple-element.31), channel_id=1, source_target_pairs={{4,0},{5,1},{6,2},{7,3},{8,4},{9,5},{10,6},{11,7},{12,8},{13,9},{1... | collective-permute-start | bytes 786440 | tf_op jit(solution)/shard_map/ppermute | solution.py:301
  31.1 3.9 %collective-permute-start.8 = (f32[2,3,32,128]{3,2,1,0:T(8,128)S(1)}, f32[2,3,32,128]{3,2,1,0:T(8,128)S(1)}, u32[]{:S(2)}, u32[]{:S(2)}) collective-permute-start(f32[2,3,32,128]{3,2,1,0:T(8,128)S(1)} %get-tuple-element.32), channel_id=1, source_target_pairs={{0,1},{1,2},{2,3},{4,5},{5,6},{6,7},{8,9},{9,10},{10,11},{12,13},{... | collective-permute-start | bytes 294920 | tf_op jit(solution)/shard_map/ppermute | solution.py:301
  35.1 1.9 %collective-permute-start.9 = (f32[2,2,32,128]{3,2,1,0:T(8,128)S(1)}, f32[2,2,32,128]{3,2,1,0:T(8,128)S(1)}, u32[]{:S(2)}, u32[]{:S(2)}) collective-permute-start(f32[2,2,32,128]{3,2,1,0:T(8,128)S(1)} %get-tuple-element.33), channel_id=1, source_target_pairs={{1,0},{2,1},{3,2},{5,4},{6,5},{7,6},{9,8},{10,9},{11,10},{13,12},{... | collective-permute-start | bytes 196616 | tf_op jit(solution)/shard_map/ppermute | solution.py:301
  37.0 3.7 %collective-permute-start.10 = (f32[32,128]{1,0:T(8,128)S(1)}, f32[32,128]{1,0:T(8,128)S(1)}, u32[]{:S(2)}, u32[]{:S(2)}) collective-permute-start(f32[32,128]{1,0:T(8,128)S(1)} %get-tuple-element.34), channel_id=1, source_target_pairs={{1,4},{2,5},{3,6},{5,8},{6,9},{7,10},{9,12},{10,13},{11,14},{13,16... | collective-permute-start | bytes 49160 | tf_op jit(solution)/shard_map/ppermute | solution.py:301
  40.7 1.4 %collective-permute-done.10.refs_6_ = f32[32,128]{1,0:T(8,128)S(1)} collective-permute-done((f32[32,128]{1,0:T(8,128)S(1)}, f32[32,128]{1,0:T(8,128)S(1)}, u32[]{:S(2)}, u32[]{:S(2)}) %collective-permute-start.10) | collective-permute-done | bytes 16416 | tf_op jit(solution)/shard_map/ppermute | solution.py:301
  42.1 1.3 %collective-permute-start.11 = (f32[32,128]{1,0:T(8,128)S(1)}, f32[32,128]{1,0:T(8,128)S(1)}, u32[]{:S(2)}, u32[]{:S(2)}) collective-permute-start(f32[32,128]{1,0:T(8,128)S(1)} %get-tuple-element.35), channel_id=1, source_target_pairs={{4,1},{5,2},{6,3},{8,5},{9,6},{10,7},{12,9},{13,10},{14,11},{16,13... | collective-permute-start | bytes 49160 | tf_op jit(solution)/shard_map/ppermute | solution.py:301
  43.4 0.9 shard_map.61
  44.3 2.8 %collective-permute-done.11.refs_7_ = f32[32,128]{1,0:T(8,128)S(1)} collective-permute-done((f32[32,128]{1,0:T(8,128)S(1)}, f32[32,128]{1,0:T(8,128)S(1)}, u32[]{:S(2)}, u32[]{:S(2)}) %collective-permute-start.11) | collective-permute-done | bytes 16416 | tf_op jit(solution)/shard_map/ppermute | solution.py:301
  47.2 0.0 collective-permute-done.9.refs_5_
  47.2 0.0 collective-permute-done.8.refs_4_
  47.2 0.0 collective-permute-done.7.refs_3_
  47.2 0.0 collective-permute-done.6.refs_2_
  47.2 1.3 %shard_map.62 = (f32[2,3,8,32,128]{4,3,2,1,0:T(8,128)S(1)}, f32[2,32,32]{2,1,0:T(8,128)S(1)}) custom-call(f32[2,8,128]{2,1,0:T(8,128)S(1)} %get-tuple-element.29.refs_0_, f32[2,3,8,32,128]{4,3,2,1,0:T(8,128)S(1)} %get-tuple-element.28.s1.refs_1_, f32[3,8,32,128]{3,2,1,0:T(8,128)S(1)} %collective-permute-done.6.refs_2_, ...), custom_call_target="tpu_custom_call" | custom-call | bytes 2441216 | tf_op jit(solution)/shard_map/pallas_call | solution.py:25
  48.5 0.1 reshape.17
  48.6 2.4 %collective-permute-start.14 = (f32[40,128]{1,0:T(8,128)S(1)}, f32[40,128]{1,0:T(8,128)S(1)}, u32[]{:S(2)}, u32[]{:S(2)}) collective-permute-start(f32[40,128]{1,0:T(8,128)S(1)} %reshape.17), channel_id=1, source_target_pairs={{0,3},{1,2},{2,1},{3,0},{4,7},{5,6},{6,5},{7,4},{8,11},{9,10},{10,... | collective-permute-start | bytes 61448 | tf_op jit(solution)/shard_map/ppermute | solution.py:325
  51.0 1.0 %collective-permute-start.13 = (f32[40,128]{1,0:T(8,128)S(1)}, f32[40,128]{1,0:T(8,128)S(1)}, u32[]{:S(2)}, u32[]{:S(2)}) collective-permute-start(f32[40,128]{1,0:T(8,128)S(1)} %reshape.17), channel_id=1, source_target_pairs={{0,2},{1,3},{2,0},{3,1},{4,6},{5,7},{6,4},{7,5},{8,10},{9,11},{10,... | collective-permute-start | bytes 61448 | tf_op jit(solution)/shard_map/ppermute | solution.py:325
  52.0 1.2 %collective-permute-start.12 = (f32[40,128]{1,0:T(8,128)S(1)}, f32[40,128]{1,0:T(8,128)S(1)}, u32[]{:S(2)}, u32[]{:S(2)}) collective-permute-start(f32[40,128]{1,0:T(8,128)S(1)} %reshape.17), channel_id=1, source_target_pairs={{0,1},{1,0},{2,3},{3,2},{4,5},{5,4},{6,7},{7,6},{8,9},{9,8},{10,11... | collective-permute-start | bytes 61448 | tf_op jit(solution)/shard_map/ppermute | solution.py:325
  53.2 0.0 collective-permute-done.14
  53.2 3.3 %collective-permute-done.13 = f32[40,128]{1,0:T(8,128)S(1)} collective-permute-done((f32[40,128]{1,0:T(8,128)S(1)}, f32[40,128]{1,0:T(8,128)S(1)}, u32[]{:S(2)}, u32[]{:S(2)}) %collective-permute-start.13) | collective-permute-done | bytes 20512 | tf_op jit(solution)/shard_map/ppermute | solution.py:325
  56.5 0.0 collective-permute-done.12
  56.5 15.6 %collective-permute-start.17 = (f32[40,128]{1,0:T(8,128)S(1)}, f32[40,128]{1,0:T(8,128)S(1)}, u32[]{:S(2)}, u32[]{:S(2)}) collective-permute-start(f32[40,128]{1,0:T(8,128)S(1)} %add_add_fusion.3), channel_id=1, source_target_pairs={{0,192},{1,193},{2,194},{3,195},{4,196},{5,197},{6,198},{7,199},{8... | collective-permute-start | bytes 61448 | tf_op jit(solution)/shard_map/ppermute | solution.py:325
  72.1 0.4 collective-permute-start.16
  72.5 0.5 collective-permute-start.15
  73.0 0.8 collective-permute-done.17
  73.8 3.5 %collective-permute-done.16 = f32[40,128]{1,0:T(8,128)S(1)} collective-permute-done((f32[40,128]{1,0:T(8,128)S(1)}, f32[40,128]{1,0:T(8,128)S(1)}, u32[]{:S(2)}, u32[]{:S(2)}) %collective-permute-start.16) | collective-permute-done | bytes 20512 | tf_op jit(solution)/shard_map/ppermute | solution.py:325
  77.3 0.0 collective-permute-done.15
  77.4 0.1 collective-permute-start.20
  77.5 0.1 collective-permute-start.19
  77.6 1.7 %collective-permute-start.18 = (f32[40,128]{1,0:T(8,128)S(1)}, f32[40,128]{1,0:T(8,128)S(1)}, u32[]{:S(2)}, u32[]{:S(2)}) collective-permute-start(f32[40,128]{1,0:T(8,128)S(1)} %add_add_fusion.2), channel_id=1, source_target_pairs={{0,4},{1,5},{2,6},{3,7},{4,0},{5,1},{6,2},{7,3},{8,12},{9,13},{10,... | collective-permute-start | bytes 61448 | tf_op jit(solution)/shard_map/ppermute | solution.py:325
  79.3 1.3 %collective-permute-done.20 = f32[40,128]{1,0:T(8,128)S(1)} collective-permute-done((f32[40,128]{1,0:T(8,128)S(1)}, f32[40,128]{1,0:T(8,128)S(1)}, u32[]{:S(2)}, u32[]{:S(2)}) %collective-permute-start.20) | collective-permute-done | bytes 20512 | tf_op jit(solution)/shard_map/ppermute | solution.py:325
  80.7 0.7 collective-permute-done.19
  81.3 0.0 collective-permute-done.18
  81.3 0.1 collective-permute-start.23
  81.4 2.1 %collective-permute-start.22 = (f32[40,128]{1,0:T(8,128)S(1)}, f32[40,128]{1,0:T(8,128)S(1)}, u32[]{:S(2)}, u32[]{:S(2)}) collective-permute-start(f32[40,128]{1,0:T(8,128)S(1)} %add_add_fusion.1), channel_id=1, source_target_pairs={{0,32},{1,33},{2,34},{3,35},{4,36},{5,37},{6,38},{7,39},{8,40},{9,... | collective-permute-start | bytes 61448 | tf_op jit(solution)/shard_map/ppermute | solution.py:325
  83.5 4.4 %collective-permute-start.21 = (f32[40,128]{1,0:T(8,128)S(1)}, f32[40,128]{1,0:T(8,128)S(1)}, u32[]{:S(2)}, u32[]{:S(2)}) collective-permute-start(f32[40,128]{1,0:T(8,128)S(1)} %add_add_fusion.1), channel_id=1, source_target_pairs={{0,16},{1,17},{2,18},{3,19},{4,20},{5,21},{6,22},{7,23},{8,24},{9,... | collective-permute-start | bytes 61448 | tf_op jit(solution)/shard_map/ppermute | solution.py:325
  87.9 0.0 collective-permute-done.23
  87.9 1.3 %collective-permute-done.22 = f32[40,128]{1,0:T(8,128)S(1)} collective-permute-done((f32[40,128]{1,0:T(8,128)S(1)}, f32[40,128]{1,0:T(8,128)S(1)}, u32[]{:S(2)}, u32[]{:S(2)}) %collective-permute-start.22) | collective-permute-done | bytes 20512 | tf_op jit(solution)/shard_map/ppermute | solution.py:325
  89.2 0.7 collective-permute-done.21
  89.9 0.1 reshape.18.moments
  90.0 0.0 copy-done.4
  90.0 6.6 %shard_map.63 = (f32[3072,128]{1,0:T(8,128)}, f32[2,2,32,32]{3,2,1,0:T(8,128)}) custom-call(f32[4]{0:T(128)S(1)} %copy-done.4, f32[5,32,32]{2,1,0:T(8,128)S(1)} %reshape.18.moments, f32[2,3,8,32,128]{4,3,2,1,0:T(8,128)S(1)} %get-tuple-element.21.refs_3_.s0, f32[2,3,8,32,128]{4,3,2,1,0:T(8,128)S(1)} %get-tuple-element.28.s1.refs_1_, ...), custom_call_target="tpu_custom_call" | custom-call | bytes 3969040 | tf_op jit(solution)/shard_map/pallas_call | solution.py:25
  (6 shorter events, 0.0 us)
Async XLA Ops:
  0.6 1.1 %copy-start = (f32[32,3,2,8,128]{4,3,2,1,0:T(8,128)S(1)}, f32[32,3,2,8,128]{4,3,2,1,0:T(8,128)}, u32[]{:S(2)}) copy-start(f32[32,3,2,8,128]{4,3,2,1,0:T(8,128)} %param.4) | copy-start | bytes 2359300
  2.0 18.8 %collective-permute-start = (f32[3,8,32,128]{3,2,1,0:T(8,128)S(1)}, f32[3,8,32,128]{3,2,1,0:T(8,128)S(1)}, u32[]{:S(2)}, u32[]{:S(2)}) collective-permute-start(f32[3,8,32,128]{3,2,1,0:T(8,128)S(1)} %get-tuple-element.22), channel_id=1, source_target_pairs={{0,4},{1,5},{2,6},{3,7},{4,8},{5,9},{6,10},{7,11},{8,12},{9,13},{1... | collective-permute-start | bytes 1179656 | tf_op jit(solution)/shard_map/ppermute | solution.py:301
  3.8 17.1 %collective-permute-start.1 = (f32[2,8,32,128]{3,2,1,0:T(8,128)S(1)}, f32[2,8,32,128]{3,2,1,0:T(8,128)S(1)}, u32[]{:S(2)}, u32[]{:S(2)}) collective-permute-start(f32[2,8,32,128]{3,2,1,0:T(8,128)S(1)} %get-tuple-element.23), channel_id=1, source_target_pairs={{4,0},{5,1},{6,2},{7,3},{8,4},{9,5},{10,6},{11,7},{12,8},{13,9},{1... | collective-permute-start | bytes 786440 | tf_op jit(solution)/shard_map/ppermute | solution.py:301
  5.1 15.8 %collective-permute-start.2 = (f32[2,3,32,128]{3,2,1,0:T(8,128)S(1)}, f32[2,3,32,128]{3,2,1,0:T(8,128)S(1)}, u32[]{:S(2)}, u32[]{:S(2)}) collective-permute-start(f32[2,3,32,128]{3,2,1,0:T(8,128)S(1)} %get-tuple-element.24), channel_id=1, source_target_pairs={{0,1},{1,2},{2,3},{4,5},{5,6},{6,7},{8,9},{9,10},{10,11},{12,13},{... | collective-permute-start | bytes 294920 | tf_op jit(solution)/shard_map/ppermute | solution.py:301
  8.5 12.4 %collective-permute-start.3 = (f32[2,2,32,128]{3,2,1,0:T(8,128)S(1)}, f32[2,2,32,128]{3,2,1,0:T(8,128)S(1)}, u32[]{:S(2)}, u32[]{:S(2)}) collective-permute-start(f32[2,2,32,128]{3,2,1,0:T(8,128)S(1)} %get-tuple-element.25), channel_id=1, source_target_pairs={{1,0},{2,1},{3,2},{5,4},{6,5},{7,6},{9,8},{10,9},{11,10},{13,12},{... | collective-permute-start | bytes 196616 | tf_op jit(solution)/shard_map/ppermute | solution.py:301
  11.0 4.9 %collective-permute-start.4 = (f32[32,128]{1,0:T(8,128)S(1)}, f32[32,128]{1,0:T(8,128)S(1)}, u32[]{:S(2)}, u32[]{:S(2)}) collective-permute-start(f32[32,128]{1,0:T(8,128)S(1)} %get-tuple-element.26), channel_id=1, source_target_pairs={{1,4},{2,5},{3,6},{5,8},{6,9},{7,10},{9,12},{10,13},{11,14},{13,16... | collective-permute-start | bytes 49160 | tf_op jit(solution)/shard_map/ppermute | solution.py:301
  15.8 5.0 %collective-permute-start.5 = (f32[32,128]{1,0:T(8,128)S(1)}, f32[32,128]{1,0:T(8,128)S(1)}, u32[]{:S(2)}, u32[]{:S(2)}) collective-permute-start(f32[32,128]{1,0:T(8,128)S(1)} %get-tuple-element.27), channel_id=1, source_target_pairs={{4,1},{5,2},{6,3},{8,5},{9,6},{10,7},{12,9},{13,10},{14,11},{16,13... | collective-permute-start | bytes 49160 | tf_op jit(solution)/shard_map/ppermute | solution.py:301
  20.9 0.7 copy-start.1
  21.6 0.7 copy-start.2
  22.3 0.7 copy-start.3
  24.5 22.6 %collective-permute-start.6 = (f32[3,8,32,128]{3,2,1,0:T(8,128)S(1)}, f32[3,8,32,128]{3,2,1,0:T(8,128)S(1)}, u32[]{:S(2)}, u32[]{:S(2)}) collective-permute-start(f32[3,8,32,128]{3,2,1,0:T(8,128)S(1)} %get-tuple-element.30), channel_id=1, source_target_pairs={{0,4},{1,5},{2,6},{3,7},{4,8},{5,9},{6,10},{7,11},{8,12},{9,13},{1... | collective-permute-start | bytes 1179656 | tf_op jit(solution)/shard_map/ppermute | solution.py:301
  29.8 17.3 %collective-permute-start.7 = (f32[2,8,32,128]{3,2,1,0:T(8,128)S(1)}, f32[2,8,32,128]{3,2,1,0:T(8,128)S(1)}, u32[]{:S(2)}, u32[]{:S(2)}) collective-permute-start(f32[2,8,32,128]{3,2,1,0:T(8,128)S(1)} %get-tuple-element.31), channel_id=1, source_target_pairs={{4,0},{5,1},{6,2},{7,3},{8,4},{9,5},{10,6},{11,7},{12,8},{13,9},{1... | collective-permute-start | bytes 786440 | tf_op jit(solution)/shard_map/ppermute | solution.py:301
  31.1 16.0 %collective-permute-start.8 = (f32[2,3,32,128]{3,2,1,0:T(8,128)S(1)}, f32[2,3,32,128]{3,2,1,0:T(8,128)S(1)}, u32[]{:S(2)}, u32[]{:S(2)}) collective-permute-start(f32[2,3,32,128]{3,2,1,0:T(8,128)S(1)} %get-tuple-element.32), channel_id=1, source_target_pairs={{0,1},{1,2},{2,3},{4,5},{5,6},{6,7},{8,9},{9,10},{10,11},{12,13},{... | collective-permute-start | bytes 294920 | tf_op jit(solution)/shard_map/ppermute | solution.py:301
  35.1 12.1 %collective-permute-start.9 = (f32[2,2,32,128]{3,2,1,0:T(8,128)S(1)}, f32[2,2,32,128]{3,2,1,0:T(8,128)S(1)}, u32[]{:S(2)}, u32[]{:S(2)}) collective-permute-start(f32[2,2,32,128]{3,2,1,0:T(8,128)S(1)} %get-tuple-element.33), channel_id=1, source_target_pairs={{1,0},{2,1},{3,2},{5,4},{6,5},{7,6},{9,8},{10,9},{11,10},{13,12},{... | collective-permute-start | bytes 196616 | tf_op jit(solution)/shard_map/ppermute | solution.py:301
  37.0 5.1 %collective-permute-start.10 = (f32[32,128]{1,0:T(8,128)S(1)}, f32[32,128]{1,0:T(8,128)S(1)}, u32[]{:S(2)}, u32[]{:S(2)}) collective-permute-start(f32[32,128]{1,0:T(8,128)S(1)} %get-tuple-element.34), channel_id=1, source_target_pairs={{1,4},{2,5},{3,6},{5,8},{6,9},{7,10},{9,12},{10,13},{11,14},{13,16... | collective-permute-start | bytes 49160 | tf_op jit(solution)/shard_map/ppermute | solution.py:301
  42.1 5.0 %collective-permute-start.11 = (f32[32,128]{1,0:T(8,128)S(1)}, f32[32,128]{1,0:T(8,128)S(1)}, u32[]{:S(2)}, u32[]{:S(2)}) collective-permute-start(f32[32,128]{1,0:T(8,128)S(1)} %get-tuple-element.35), channel_id=1, source_target_pairs={{4,1},{5,2},{6,3},{8,5},{9,6},{10,7},{12,9},{13,10},{14,11},{16,13... | collective-permute-start | bytes 49160 | tf_op jit(solution)/shard_map/ppermute | solution.py:301
  44.3 45.7 %copy-start.4 = (f32[4]{0:T(128)S(1)}, f32[4]{0:T(128)}, u32[]{:S(2)}) copy-start(f32[4]{0:T(128)} %eps.1) | copy-start | bytes 52
  48.6 4.6 %collective-permute-start.14 = (f32[40,128]{1,0:T(8,128)S(1)}, f32[40,128]{1,0:T(8,128)S(1)}, u32[]{:S(2)}, u32[]{:S(2)}) collective-permute-start(f32[40,128]{1,0:T(8,128)S(1)} %reshape.17), channel_id=1, source_target_pairs={{0,3},{1,2},{2,1},{3,0},{4,7},{5,6},{6,5},{7,4},{8,11},{9,10},{10,... | collective-permute-start | bytes 61448 | tf_op jit(solution)/shard_map/ppermute | solution.py:325
  51.0 5.5 %collective-permute-start.13 = (f32[40,128]{1,0:T(8,128)S(1)}, f32[40,128]{1,0:T(8,128)S(1)}, u32[]{:S(2)}, u32[]{:S(2)}) collective-permute-start(f32[40,128]{1,0:T(8,128)S(1)} %reshape.17), channel_id=1, source_target_pairs={{0,2},{1,3},{2,0},{3,1},{4,6},{5,7},{6,4},{7,5},{8,10},{9,11},{10,... | collective-permute-start | bytes 61448 | tf_op jit(solution)/shard_map/ppermute | solution.py:325
  52.0 4.5 %collective-permute-start.12 = (f32[40,128]{1,0:T(8,128)S(1)}, f32[40,128]{1,0:T(8,128)S(1)}, u32[]{:S(2)}, u32[]{:S(2)}) collective-permute-start(f32[40,128]{1,0:T(8,128)S(1)} %reshape.17), channel_id=1, source_target_pairs={{0,1},{1,0},{2,3},{3,2},{4,5},{5,4},{6,7},{7,6},{8,9},{9,8},{10,11... | collective-permute-start | bytes 61448 | tf_op jit(solution)/shard_map/ppermute | solution.py:325
  56.5 17.3 %collective-permute-start.17 = (f32[40,128]{1,0:T(8,128)S(1)}, f32[40,128]{1,0:T(8,128)S(1)}, u32[]{:S(2)}, u32[]{:S(2)}) collective-permute-start(f32[40,128]{1,0:T(8,128)S(1)} %add_add_fusion.3), channel_id=1, source_target_pairs={{0,192},{1,193},{2,194},{3,195},{4,196},{5,197},{6,198},{7,199},{8... | collective-permute-start | bytes 61448 | tf_op jit(solution)/shard_map/ppermute | solution.py:325
  72.1 5.3 %collective-permute-start.16 = (f32[40,128]{1,0:T(8,128)S(1)}, f32[40,128]{1,0:T(8,128)S(1)}, u32[]{:S(2)}, u32[]{:S(2)}) collective-permute-start(f32[40,128]{1,0:T(8,128)S(1)} %add_add_fusion.3), channel_id=1, source_target_pairs={{0,128},{1,129},{2,130},{3,131},{4,132},{5,133},{6,134},{7,135},{8... | collective-permute-start | bytes 61448 | tf_op jit(solution)/shard_map/ppermute | solution.py:325
  72.5 4.8 %collective-permute-start.15 = (f32[40,128]{1,0:T(8,128)S(1)}, f32[40,128]{1,0:T(8,128)S(1)}, u32[]{:S(2)}, u32[]{:S(2)}) collective-permute-start(f32[40,128]{1,0:T(8,128)S(1)} %add_add_fusion.3), channel_id=1, source_target_pairs={{0,64},{1,65},{2,66},{3,67},{4,68},{5,69},{6,70},{7,71},{8,72},{9,... | collective-permute-start | bytes 61448 | tf_op jit(solution)/shard_map/ppermute | solution.py:325
  77.4 3.3 %collective-permute-start.20 = (f32[40,128]{1,0:T(8,128)S(1)}, f32[40,128]{1,0:T(8,128)S(1)}, u32[]{:S(2)}, u32[]{:S(2)}) collective-permute-start(f32[40,128]{1,0:T(8,128)S(1)} %add_add_fusion.2), channel_id=1, source_target_pairs={{0,12},{1,13},{2,14},{3,15},{4,8},{5,9},{6,10},{7,11},{8,4},{9,5},... | collective-permute-start | bytes 61448 | tf_op jit(solution)/shard_map/ppermute | solution.py:325
  77.5 3.9 %collective-permute-start.19 = (f32[40,128]{1,0:T(8,128)S(1)}, f32[40,128]{1,0:T(8,128)S(1)}, u32[]{:S(2)}, u32[]{:S(2)}) collective-permute-start(f32[40,128]{1,0:T(8,128)S(1)} %add_add_fusion.2), channel_id=1, source_target_pairs={{0,8},{1,9},{2,10},{3,11},{4,12},{5,13},{6,14},{7,15},{8,0},{9,1},... | collective-permute-start | bytes 61448 | tf_op jit(solution)/shard_map/ppermute | solution.py:325
  77.6 3.8 %collective-permute-start.18 = (f32[40,128]{1,0:T(8,128)S(1)}, f32[40,128]{1,0:T(8,128)S(1)}, u32[]{:S(2)}, u32[]{:S(2)}) collective-permute-start(f32[40,128]{1,0:T(8,128)S(1)} %add_add_fusion.2), channel_id=1, source_target_pairs={{0,4},{1,5},{2,6},{3,7},{4,0},{5,1},{6,2},{7,3},{8,12},{9,13},{10,... | collective-permute-start | bytes 61448 | tf_op jit(solution)/shard_map/ppermute | solution.py:325
  81.3 6.6 %collective-permute-start.23 = (f32[40,128]{1,0:T(8,128)S(1)}, f32[40,128]{1,0:T(8,128)S(1)}, u32[]{:S(2)}, u32[]{:S(2)}) collective-permute-start(f32[40,128]{1,0:T(8,128)S(1)} %add_add_fusion.1), channel_id=1, source_target_pairs={{0,48},{1,49},{2,50},{3,51},{4,52},{5,53},{6,54},{7,55},{8,56},{9,... | collective-permute-start | bytes 61448 | tf_op jit(solution)/shard_map/ppermute | solution.py:325
  81.4 7.8 %collective-permute-start.22 = (f32[40,128]{1,0:T(8,128)S(1)}, f32[40,128]{1,0:T(8,128)S(1)}, u32[]{:S(2)}, u32[]{:S(2)}) collective-permute-start(f32[40,128]{1,0:T(8,128)S(1)} %add_add_fusion.1), channel_id=1, source_target_pairs={{0,32},{1,33},{2,34},{3,35},{4,36},{5,37},{6,38},{7,39},{8,40},{9,... | collective-permute-start | bytes 61448 | tf_op jit(solution)/shard_map/ppermute | solution.py:325
  83.5 6.4 %collective-permute-start.21 = (f32[40,128]{1,0:T(8,128)S(1)}, f32[40,128]{1,0:T(8,128)S(1)}, u32[]{:S(2)}, u32[]{:S(2)}) collective-permute-start(f32[40,128]{1,0:T(8,128)S(1)} %add_add_fusion.1), channel_id=1, source_target_pairs={{0,16},{1,17},{2,18},{3,19},{4,20},{5,21},{6,22},{7,23},{8,24},{9,... | collective-permute-start | bytes 61448 | tf_op jit(solution)/shard_map/ppermute | solution.py:325

commit v2 on v1

v2 whole, which is shorter than its diff:
```python
import functools

import jax
import jax.numpy as jnp
from jax import lax
from jax.experimental import pallas as pl
from jax.experimental.pallas import tpu as pltpu
from jax.sharding import PartitionSpec as P

AXES = ("slab", "trans")
ABSORB = 4.0
CURL_CENTRE = 5.0
VMEM_LIMIT = 40 * 1024 * 1024


def call(body, out_shape, operands, smem=(), scratch=()):
    specs = [
        pl.BlockSpec(memory_space=pltpu.SMEM if i in smem else pltpu.VMEM)
        for i in range(len(operands))
    ]
    outs = [pl.BlockSpec(memory_space=pltpu.VMEM) for _ in out_shape]
    return pl.pallas_call(
        body,
        out_shape=out_shape,
        in_specs=specs,
        out_specs=outs,
        scratch_shapes=list(scratch),
        compiler_params=pltpu.CompilerParams(vmem_limit_bytes=VMEM_LIMIT),
    )(*operands)


def shape(*dims):
    return jax.ShapeDtypeStruct(dims, jnp.float32)


class Halo:
    def __init__(self, zs, xs):
        self.zs, self.xs = zs, xs
        self.first = set()
        for c in range(3):
            for z in range(zs):
                for x in range(xs):
                    self.first.add((c, z, x))
                    self.first |= reach(c, z, x)
        cells = set(self.first)
        for cell in self.first:
            cells |= reach(*cell)
        self.blocks, self.diagonal = {}, {}
        self.sides = sorted({self.side(z, x) for _, z, x in cells} - {(0, 0)}, key=side_order)
        for side in self.sides:
            self.blocks[side] = sorted(q for q in cells if self.side(q[1], q[2]) == side)
            near = {q[1:] for q in self.first if self.side(q[1], q[2]) == side}
            self.diagonal[side] = sorted(near)

    def side(self, z, x):
        return (
            -1 if z < 0 else int(z >= self.zs),
            -1 if x < 0 else int(x >= self.xs),
        )

    def own(self, side, z, x):
        return z - side[0] * self.zs, x - side[1] * self.xs

    def rows(self, side, width):
        return len(self.blocks[side]) * width + (8 if self.diagonal[side] else 0)


def side_order(side):
    return (abs(side[0]) + abs(side[1]), -abs(side[0]), side)


CURL = (
    lambda z, x: {(2, z, x), (1, z + 1, x), (1, z, x)},
    lambda z, x: {(0, z + 1, x), (0, z, x), (2, z, x + 1), (2, z, x)},
    lambda z, x: {(1, z, x + 1), (1, z, x), (0, z, x)},
)
BACK = (
    lambda z, x: {(2, z, x), (1, z, x), (1, z - 1, x)},
    lambda z, x: {(0, z, x), (0, z - 1, x), (2, z, x), (2, z, x - 1)},
    lambda z, x: {(1, z, x), (1, z, x - 1), (0, z, x)},
)


def reach(c, z, x):
    cells = {(c, z, x)}
    for k, hz, hx in BACK[c](z, x):
        cells |= CURL[k](hz, hx)
    return cells


def stencil(e, lane, last):
    known = {}

    def step_y(value):
        return jnp.where(lane == last, 0.0, pltpu.roll(value, last, 1)) - value

    def h(k, z, x):
        if (k, z, x) not in known:
            if k == 0:
                value = step_y(e(2, z, x)) - (e(1, z + 1, x) - e(1, z, x))
            elif k == 1:
                value = (e(0, z + 1, x) - e(0, z, x)) - (e(2, z, x + 1) - e(2, z, x))
            else:
                value = (e(1, z, x + 1) - e(1, z, x)) - step_y(e(0, z, x))
            known[k, z, x] = value
        return known[k, z, x]

    def result(c, z, x):
        if c == 0:
            here = h(2, z, x)
            before = jnp.where(lane == 0, -e(0, z, x), pltpu.roll(here, 1, 1))
            return (here - before) - (h(1, z, x) - h(1, z - 1, x))
        if c == 1:
            return (h(0, z, x) - h(0, z - 1, x)) - (h(2, z, x) - h(2, z, x - 1))
        here = h(0, z, x)
        before = jnp.where(lane == 0, e(2, z, x), pltpu.roll(here, 1, 1))
        return (h(1, z, x) - h(1, z, x - 1)) - (here - before)

    return result


def split_body(halo, width, classes, eps, material, mask, start, field, diag, *messages):
    zs, xs = halo.zs, halo.xs
    rows = 3 * zs * xs
    total = eps[0]
    for level in range(1, classes):
        total = total + eps[level]
    shift = total / classes + CURL_CENTRE
    value = jnp.zeros(material.shape, jnp.float32)
    for level in range(classes):
        value = value + jnp.where(material[...] == level, eps[level], 0.0)
    diag[...] = value + ABSORB * mask[...].astype(jnp.float32) - shift

    places = {}
    for side, message in zip(halo.sides, messages):
        for i, (c, z, x) in enumerate(halo.blocks[side]):
            places.setdefault((c, *halo.own(side, z, x)), []).append((message, i))
        base = len(halo.blocks[side]) * width
        if halo.diagonal[side]:
            message[base : base + 8, :] = jnp.zeros((8, message.shape[1]), jnp.float32)
        for i, (z, x) in enumerate(halo.diagonal[side]):
            oz, ox = halo.own(side, z, x)
            message[base + i : base + i + 1, :] = diag[oz, ox : ox + 1, :]
    for z in range(zs):
        for c in range(3):
            for x in range(xs):
                cell = start[pl.ds((c * zs + z) * xs + x, width, stride=rows), :]
                field[z, c, x] = cell
                for message, i in places.get((c, z, x), ()):
                    message[i * width : (i + 1) * width, :] = cell


def parts(value, count):
    found, rest = [], value
    for i in range(count):
        found.append(rest.astype(jnp.bfloat16))
        if i + 1 < count:
            rest = rest - found[-1].astype(jnp.float32)
    return found


def pair(ref, z, c, x):
    return jnp.concatenate([ref[z, c, x], ref[z, c, x + 1]], axis=1)


def product(left, right, contract):
    return lax.dot_general(
        left, right, (((1,), (contract,)), ((), ())), preferred_element_type=jnp.float32
    )


def fold(total, left, right):
    rows = total[:left] + total[left : 2 * left] + total[2 * left :]
    return rows[:, :right] + rows[:, right : 2 * right] + rows[:, 2 * right :]


def start_gram_body(zs, xs, s0, out):
    total = None
    for z in range(zs):
        for c in range(3):
            for x in range(0, xs, 2):
                stack = jnp.concatenate(parts(pair(s0, z, c, x), 3), axis=0)
                term = product(stack, stack, 1)
                total = term if total is None else total + term
    out[...] = fold(total, *out.shape)


def apply_body(halo, width, ny, slabs, trans, s0, diag, gram, *refs):
    zs, xs = halo.zs, halo.xs
    count = len(halo.sides)
    messages = dict(zip(halo.sides, refs[:count]))
    s1, s2, moments, outer = refs[count:]
    slab, across = lax.axis_index("slab"), lax.axis_index("trans")
    inside = {
        (-1, 0): slab > 0,
        (1, 0): slab < slabs - 1,
        (0, -1): across > 0,
        (0, 1): across < trans - 1,
    }
    inside = {side: jnp.where(held, 1.0, 0.0) for side, held in inside.items()}
    for side in halo.sides:
        if side not in inside:
            inside[side] = inside[side[0], 0] * inside[0, side[1]]
    block = {s: {q: i for i, q in enumerate(halo.blocks[s])} for s in halo.sides}
    extra = sorted(q for q in halo.first if halo.side(q[1], q[2]) != (0, 0))
    extra = {q: i for i, q in enumerate(extra)}
    lane = lax.broadcasted_iota(jnp.int32, (8, ny), 1)

    def diagonal(z, x):
        side = halo.side(z, x)
        if side == (0, 0):
            return diag[z, x : x + 1, :]
        row = len(halo.blocks[side]) * width + halo.diagonal[side].index((z, x))
        return messages[side][row : row + 1, :]

    def group(g, carry):
        at = pl.multiple_of(g * 8, 8)

        def start(c, z, x):
            side = halo.side(z, x)
            if side == (0, 0):
                return s0[z, c, x, pl.ds(at, 8), :]
            place = block[side][c, z, x] * width
            return messages[side][pl.ds(place + at, 8), :] * inside[side]

        def once(c, z, x):
            if halo.side(z, x) == (0, 0):
                return s1[z, c, x, pl.ds(at, 8), :]
            return outer[extra[c, z, x]]

        apply = stencil(start, lane, ny - 1)
        for x in range(-1, xs + 1):
            for z in range(-1, zs + 1):
                for c in range(3):
                    if (c, z, x) not in halo.first:
                        continue
                    value = apply(c, z, x) + diagonal(z, x) * start(c, z, x)
                    side = halo.side(z, x)
                    if side == (0, 0):
                        s1[z, c, x, pl.ds(at, 8), :] = value
                    else:
                        outer[extra[c, z, x]] = value * inside[side]
        apply = stencil(once, lane, ny - 1)
        for x in range(xs):
            for z in range(zs):
                for c in range(3):
                    value = apply(c, z, x) + diagonal(z, x) * once(c, z, x)
                    s2[z, c, x, pl.ds(at, 8), :] = value
        return carry

    lax.fori_loop(0, width // 8, group, 0)

    total = None
    for z in range(zs):
        for c in range(3):
            for x in range(0, xs, 2):
                split = [parts(pair(s, z, c, x), 3) for s in (s0, s1, s2)]
                left = jnp.concatenate([p for i in range(3) for p in (s[i] for s in split)], axis=0)
                right = jnp.concatenate(
                    [p for i in range(3) for p in (s[i] for s in split[1:])], axis=0
                )
                term = product(left, right, 1)
                total = term if total is None else total + term
    found = fold(total, 3 * width, 2 * width)
    w = width
    found = [
        gram[...],
        found[:w, :w],
        found[w : 2 * w, :w],
        found[w : 2 * w, w:],
        found[2 * w :, w:],
    ]
    for k, m in enumerate(found):
        for j in range(w // 8):
            moments[8 * k : 8 * k + 8, w * j : w * j + w] = m[8 * j : 8 * j + 8]


def precise(left, right, contract):
    return lax.dot_general(
        left,
        right,
        (((1,), (contract,)), ((), ())),
        precision=lax.Precision.HIGHEST,
        preferred_element_type=jnp.float32,
    )


def factor(gram, size):
    tiles = size // 8
    lane = lax.broadcasted_iota(jnp.int32, (8, size), 1)
    sub = lax.broadcasted_iota(jnp.int32, (8, size), 0)
    upper = [gram[8 * t : 8 * t + 8, :] for t in range(tiles)]
    inverse = [jnp.where(lane == sub + 8 * t, 1.0, 0.0) for t in range(tiles)]
    scales = []
    for t in range(tiles):
        cols = {
            u: [
                jnp.broadcast_to(upper[u][:, 8 * t + j : 8 * t + j + 1], (8, size))
                for j in range(8)
            ]
            for u in range(t, tiles)
        }
        pivots = jnp.zeros((8, size), jnp.float32)
        for s in range(8):
            pivot = jnp.broadcast_to(cols[t][s][s : s + 1, :], (8, size))
            pivots = jnp.where(sub == s, pivot, pivots)
            reciprocal = 1.0 / pivot
            heads = [cols[t][j][s : s + 1, :] for j in range(8)]
            row_u, row_i = upper[t][s : s + 1, :], inverse[t][s : s + 1, :]
            for u in range(t, tiles):
                f = cols[u][s] * reciprocal
                if u == t:
                    f = jnp.where(sub > s, f, 0.0)
                for j in range(s + 1, 8):
                    cols[u][j] = cols[u][j] - f * heads[j]
                upper[u] = upper[u] - f * row_u
                inverse[u] = inverse[u] - f * row_i
        scales.append(lax.rsqrt(pivots))
    upper = [a * s for a, s in zip(upper, scales)]
    inverse = [a * s for a, s in zip(inverse, scales)]
    return jnp.concatenate(upper, axis=0), jnp.concatenate(inverse, axis=0)


def last_body(zs, xs, width, ny, classes, entries, eps, moments, s0, s1, s2, out, couplings):
    w = width
    total = eps[0]
    for level in range(1, classes):
        total = total + eps[level]
    shift = total / classes + CURL_CENTRE
    m = []
    for k in range(5):
        rows = moments[8 * k : 8 * k + 8, :] * (1.0 / entries)
        found = jnp.concatenate([rows[:, w * j : w * j + w] for j in range(w // 8)], axis=0)
        m.append(0.5 * (found + found.T))
    gram = jnp.concatenate(
        [jnp.concatenate([m[i + j] for j in range(3)], axis=1) for i in range(3)], axis=0
    )
    upper, inverse = factor(gram, 3 * width)
    mix = jnp.concatenate(
        [jnp.concatenate([p, p], axis=1) for p in parts(inverse[w:], 3)], axis=0
    )
    rows = 3 * zs * xs
    for z in range(zs):
        for c in range(3):
            for x in range(0, xs, 2):
                basis = jnp.concatenate([pair(s, z, c, x) for s in (s0, s1, s2)], axis=0)
                terms = product(mix, jnp.concatenate(parts(basis, 2), axis=0), 0)
                value = terms[: 2 * w] + terms[2 * w : 4 * w] + terms[4 * w :]
                for k in range(2):
                    out[pl.ds((c * zs + z) * xs + x + k, 2 * w, stride=rows), :] = value[
                        :, k * ny : (k + 1) * ny
                    ]
    identity = jnp.where(
        lax.broadcasted_iota(jnp.int32, (w, w), 0) == lax.broadcasted_iota(jnp.int32, (w, w), 1),
        shift,
        0.0,
    )
    x0, x1 = inverse[:w, :w], inverse[w : 2 * w, w : 2 * w]
    u01, u11 = upper[:w, w : 2 * w], upper[w : 2 * w, w : 2 * w]
    u12, u22 = upper[w : 2 * w, 2 * w :], upper[2 * w :, 2 * w :]
    factor_one = precise(u11, x0, 1)
    couplings[0, 0] = precise(u01, x0, 1) + identity
    couplings[0, 1] = factor_one
    couplings[1, 0] = precise(u12 - precise(factor_one, u01, 0), x1, 1) + identity
    couplings[1, 1] = precise(u22, x1, 1)


def exchange(halo, messages, slabs, trans):
    def moved(side, value):
        pairs = [
            (i * trans + j, (i - side[0]) % slabs * trans + (j - side[1]) % trans)
            for i in range(slabs)
            for j in range(trans)
        ]
        return lax.ppermute(value, AXES, pairs)

    return [moved(side, value) for side, value in zip(halo.sides, messages)]


def total_sum(value, slabs, trans):
    devices = slabs * trans
    groups = [(4, 1, 5), (3, 64, 67), (192, 8, 200), (24, 56, 32)]
    if devices != 256:
        groups = [(1 << b,) for b in range(devices.bit_length() - 1)]
    for group in groups:
        got = [lax.ppermute(value, AXES, [(i, i ^ m) for i in range(devices)]) for m in group]
        for other in got:
            value = value + other
    return value


def per_device(slabs, trans, start_block, material, pml_mask, eps_table):
    width, _, zs, xs, ny = start_block.shape
    classes = eps_table.shape[0]
    entries = float(3 * zs * xs * ny * slabs * trans)
    field = shape(zs, 3, xs, width, ny)
    rows = width * 3 * zs * xs
    halo = Halo(zs, xs)

    s0, diag, *messages = call(
        functools.partial(split_body, halo, width, classes),
        [field, shape(zs, xs, ny)] + [shape(halo.rows(s, width), ny) for s in halo.sides],
        [eps_table, material, pml_mask, start_block.reshape(rows, ny)],
        smem=(0,),
    )
    messages = exchange(halo, messages, slabs, trans)
    (gram,) = call(functools.partial(start_gram_body, zs, xs), [shape(width, width)], [s0])
    outside = len(halo.first) - 3 * zs * xs
    s1, s2, moments = call(
        functools.partial(apply_body, halo, width, ny, slabs, trans),
        [field, field, shape(40, 4 * width)],
        [s0, diag, gram] + messages,
        scratch=[pltpu.VMEM((outside, 8, ny), jnp.float32)],
    )
    moments = total_sum(moments, slabs, trans)
    blocks, couplings = call(
        functools.partial(last_body, zs, xs, width, ny, classes, entries),
        [shape(2 * rows, ny), shape(2, 2, width, width)],
        [eps_table, moments, s0, s1, s2],
        smem=(0,),
    )
    return blocks.reshape(2, width, 3, zs, xs, ny), couplings


def solution(mesh):
    sizes = dict(zip(mesh.axis_names, mesh.devices.shape))
    return jax.shard_map(
        functools.partial(per_device, sizes["slab"], sizes["trans"]),
        mesh=mesh,
        in_specs=(
            P(None, None, "slab", "trans", None),
            P("slab", "trans", None),
            P("slab", "trans", None),
            P(),
        ),
        out_specs=(P(None, None, None, "slab", "trans", None), P()),
        check_vma=False,
    )
```

time: 97.2 us -> 78.1 us (0.80)
  the two profiles are of different devices: /device:TPU:2 before, /device:TPU:6 now
where the time goes in v2:
time: 78.1 us; the launch traced here: 77.9 us
  starting transfers between devices  35.2 us (45%)
  waiting for transfers between devices  25.9 us (33%)
  Pallas kernels  12.8 us (16%)
  local copies, waits for them, and re-layouts  3.18 us (4%)
    ppermute x12, starting transfers between devices, total_sum(): lax.ppermute(value, AXES, [(i, i ^ m) for i in range(devices)])  19.1 us
    ppermute x8, starting transfers between devices, moved(): return lax.ppermute(value, AXES, pairs)  16.1 us
    ppermute x8, waiting for transfers between devices, moved(): return lax.ppermute(value, AXES, pairs)  15.1 us
    pallas_call x4, Pallas kernels, call(): pl.pallas_call(body, out_shape=out_shape, in_specs=specs, out_specs=outs,...  12.8 us
    ppermute x12, waiting for transfers between devices, total_sum(): lax.ppermute(value, AXES, [(i, i ^ m) for i in range(devices)])  10.9 us
    unnamed x10, local copies, waits for them, and re-layouts  3.18 us
  transfers between devices with their start and end apart: 20, of which 12 were waited for; matrix products, arithmetic and copies ran while one was open for 0% of the time, Pallas kernels for 1%

profile of v2, /device:TPU:6, one launch (start us, length us, event | category | flops | bytes accessed | tf_op | source)
XLA Modules:
  0.0 77.9 jit_solution(16766262281053705217)
XLA Ops:
  0.6 0.0 copy-start
  0.6 1.1 %copy-done = f32[32,3,2,8,128]{4,3,2,1,0:T(8,128)S(1)} copy-done((f32[32,3,2,8,128]{4,3,2,1,0:T(8,128)S(1)}, f32[32,3,2,8,128]{4,3,2,1,0:T(8,128)}, u32[]{:S(2)}) %copy-start) | copy-done | bytes 786456
  1.8 0.0 copy-start.1
  1.8 0.7 copy-done.1
  2.5 0.0 copy-start.2
  2.5 0.7 copy-done.2
  3.2 0.0 copy-start.3
  3.2 0.7 copy-done.3
  3.8 0.9 %shard_map.59 = (f32[2,3,8,32,128]{4,3,2,1,0:T(8,128)S(1)}, f32[2,8,128]{2,1,0:T(8,128)S(1)}, f32[1544,128]{1,0:T(8,128)S(1)}, f32[1288,128]{1,0:T(8,128)S(1)}, ...) custom-call(f32[4]{0:T(128)S(1)} %copy-done.3, ...), custom_call_target="tpu_custom_call" | custom-call | tf_op jit(solution)/shard_map/pallas_call | solution.py:22
  4.7 0.1 collective-permute-start
  4.8 7.8 %collective-permute-start.1 = (f32[1288,128]{1,0:T(8,128)S(1)}, f32[1288,128]{1,0:T(8,128)S(1)}, u32[]{:S(2)}, u32[]{:S(2)}) collective-permute-start(f32[1288,128]{1,0:T(8,128)S(1)} %get-tuple-element.20), channel_id=1, source_target_pairs={{0,252},{1,253},{2,254},{3,255},{4,0},{5,1},{6,2},{7,3},{8,4},{9,5... | collective-permute-start | bytes 1978376 | tf_op jit(solution)/shard_map/ppermute | solution.py:375
  12.6 0.0 collective-permute-start.4
  12.6 6.0 %collective-permute-start.7 = (f32[96,128]{1,0:T(8,128)S(1)}, f32[96,128]{1,0:T(8,128)S(1)}, u32[]{:S(2)}, u32[]{:S(2)}) collective-permute-start(f32[96,128]{1,0:T(8,128)S(1)} %get-tuple-element.26), channel_id=1, source_target_pairs={{0,255},{1,252},{2,253},{3,254},{4,3},{5,0},{6,1},{7,2},{8,7},{9,4... | collective-permute-start | bytes 147464 | tf_op jit(solution)/shard_map/ppermute | solution.py:375
  18.6 1.7 %collective-permute-start.2 = (f32[392,128]{1,0:T(8,128)S(1)}, f32[392,128]{1,0:T(8,128)S(1)}, u32[]{:S(2)}, u32[]{:S(2)}) collective-permute-start(f32[392,128]{1,0:T(8,128)S(1)} %get-tuple-element.21), channel_id=1, source_target_pairs={{0,1},{1,2},{2,3},{3,0},{4,5},{5,6},{6,7},{7,4},{8,9},{9,10},{10,1... | collective-permute-start | bytes 602120 | tf_op jit(solution)/shard_map/ppermute | solution.py:375
  20.2 2.9 %collective-permute-done.4.refs_4_ = f32[96,128]{1,0:T(8,128)S(1)} collective-permute-done((f32[96,128]{1,0:T(8,128)S(1)}, f32[96,128]{1,0:T(8,128)S(1)}, u32[]{:S(2)}, u32[]{:S(2)}) %collective-permute-start.4) | collective-permute-done | bytes 49184 | tf_op jit(solution)/shard_map/ppermute | solution.py:375
  23.1 0.0 collective-permute-start.5
  23.1 0.0 collective-permute-done.7.refs_7_
  23.1 0.5 collective-permute-start.3
  23.7 8.8 %collective-permute-done.5.refs_5_ = f32[168,128]{1,0:T(8,128)S(1)} collective-permute-done((f32[168,128]{1,0:T(8,128)S(1)}, f32[168,128]{1,0:T(8,128)S(1)}, u32[]{:S(2)}, u32[]{:S(2)}) %collective-permute-start.5) | collective-permute-done | bytes 86048 | tf_op jit(solution)/shard_map/ppermute | solution.py:375
  32.5 0.0 collective-permute-start.6
  32.5 0.5 shard_map.60.gram
  33.0 3.4 %collective-permute-done.6.refs_6_ = f32[168,128]{1,0:T(8,128)S(1)} collective-permute-done((f32[168,128]{1,0:T(8,128)S(1)}, f32[168,128]{1,0:T(8,128)S(1)}, u32[]{:S(2)}, u32[]{:S(2)}) %collective-permute-start.6) | collective-permute-done | bytes 86048 | tf_op jit(solution)/shard_map/ppermute | solution.py:375
  36.4 0.0 collective-permute-done.3.refs_3_
  36.4 0.0 collective-permute-done.2.refs_2_
  36.4 0.0 collective-permute-done.1.refs_1_
  36.4 0.0 collective-permute-done.refs_0_
  36.4 0.0 copy-start.4
  36.4 5.2 %shard_map.61 = (f32[2,3,8,32,128]{4,3,2,1,0:T(8,128)S(1)}, f32[2,3,8,32,128]{4,3,2,1,0:T(8,128)S(1)}, f32[40,128]{1,0:T(8,128)S(1)}) custom-call(f32[2,3,8,32,128]{4,3,2,1,0:T(8,128)S(1)} %get-tuple-element.17.s0, f32[2,8,128]{2,1,0:T(8,128)S(1)} %get-tuple-element.18.diag, f32[32,32]{1,0:T(8,128)S(1)} %shard_map.60.gram, ...), custom_call_target="tpu_custom_call" | custom-call | tf_op jit(solution)/shard_map/pallas_call | solution.py:22
  41.6 0.1 collective-permute-start.10
  41.7 0.5 collective-permute-start.9
  42.3 1.3 %collective-permute-start.8 = (f32[40,128]{1,0:T(8,128)S(1)}, f32[40,128]{1,0:T(8,128)S(1)}, u32[]{:S(2)}, u32[]{:S(2)}) collective-permute-start(f32[40,128]{1,0:T(8,128)S(1)} %get-tuple-element.27), channel_id=1, source_target_pairs={{0,4},{1,5},{2,6},{3,7},{4,0},{5,1},{6,2},{7,3},{8,12},{9,13},{10,... | collective-permute-start | bytes 61448 | tf_op jit(solution)/shard_map/ppermute | solution.py:386
  43.6 1.3 %collective-permute-done.10 = f32[40,128]{1,0:T(8,128)S(1)} collective-permute-done((f32[40,128]{1,0:T(8,128)S(1)}, f32[40,128]{1,0:T(8,128)S(1)}, u32[]{:S(2)}, u32[]{:S(2)}) %collective-permute-start.10) | collective-permute-done | bytes 20512 | tf_op jit(solution)/shard_map/ppermute | solution.py:386
  44.9 0.7 collective-permute-done.9
  45.6 0.0 collective-permute-done.8
  45.6 0.1 collective-permute-start.13
  45.7 3.9 %collective-permute-start.12 = (f32[40,128]{1,0:T(8,128)S(1)}, f32[40,128]{1,0:T(8,128)S(1)}, u32[]{:S(2)}, u32[]{:S(2)}) collective-permute-start(f32[40,128]{1,0:T(8,128)S(1)} %add_add_fusion.3), channel_id=1, source_target_pairs={{0,64},{1,65},{2,66},{3,67},{4,68},{5,69},{6,70},{7,71},{8,72},{9,... | collective-permute-start | bytes 61448 | tf_op jit(solution)/shard_map/ppermute | solution.py:386
  49.6 0.8 %collective-permute-start.11 = (f32[40,128]{1,0:T(8,128)S(1)}, f32[40,128]{1,0:T(8,128)S(1)}, u32[]{:S(2)}, u32[]{:S(2)}) collective-permute-start(f32[40,128]{1,0:T(8,128)S(1)} %add_add_fusion.3), channel_id=1, source_target_pairs={{0,3},{1,2},{2,1},{3,0},{4,7},{5,6},{6,5},{7,4},{8,11},{9,10},{10,... | collective-permute-start | bytes 61448 | tf_op jit(solution)/shard_map/ppermute | solution.py:386
  50.4 1.2 %collective-permute-done.13 = f32[40,128]{1,0:T(8,128)S(1)} collective-permute-done((f32[40,128]{1,0:T(8,128)S(1)}, f32[40,128]{1,0:T(8,128)S(1)}, u32[]{:S(2)}, u32[]{:S(2)}) %collective-permute-start.13) | collective-permute-done | bytes 20512 | tf_op jit(solution)/shard_map/ppermute | solution.py:386
  51.6 0.0 collective-permute-done.12
  51.6 3.0 %collective-permute-done.11 = f32[40,128]{1,0:T(8,128)S(1)} collective-permute-done((f32[40,128]{1,0:T(8,128)S(1)}, f32[40,128]{1,0:T(8,128)S(1)}, u32[]{:S(2)}, u32[]{:S(2)}) %collective-permute-start.11) | collective-permute-done | bytes 20512 | tf_op jit(solution)/shard_map/ppermute | solution.py:386
  54.6 0.1 collective-permute-start.16
  54.7 1.0 %collective-permute-start.15 = (f32[40,128]{1,0:T(8,128)S(1)}, f32[40,128]{1,0:T(8,128)S(1)}, u32[]{:S(2)}, u32[]{:S(2)}) collective-permute-start(f32[40,128]{1,0:T(8,128)S(1)} %add_add_fusion.2), channel_id=1, source_target_pairs={{0,8},{1,9},{2,10},{3,11},{4,12},{5,13},{6,14},{7,15},{8,0},{9,1},... | collective-permute-start | bytes 61448 | tf_op jit(solution)/shard_map/ppermute | solution.py:386
  55.7 3.7 %collective-permute-start.14 = (f32[40,128]{1,0:T(8,128)S(1)}, f32[40,128]{1,0:T(8,128)S(1)}, u32[]{:S(2)}, u32[]{:S(2)}) collective-permute-start(f32[40,128]{1,0:T(8,128)S(1)} %add_add_fusion.2), channel_id=1, source_target_pairs={{0,192},{1,193},{2,194},{3,195},{4,196},{5,197},{6,198},{7,199},{8... | collective-permute-start | bytes 61448 | tf_op jit(solution)/shard_map/ppermute | solution.py:386
  59.4 1.2 %collective-permute-done.16 = f32[40,128]{1,0:T(8,128)S(1)} collective-permute-done((f32[40,128]{1,0:T(8,128)S(1)}, f32[40,128]{1,0:T(8,128)S(1)}, u32[]{:S(2)}, u32[]{:S(2)}) %collective-permute-start.16) | collective-permute-done | bytes 20512 | tf_op jit(solution)/shard_map/ppermute | solution.py:386
  60.6 0.0 collective-permute-done.15
  60.6 0.6 collective-permute-done.14
  61.1 3.5 %collective-permute-start.19 = (f32[40,128]{1,0:T(8,128)S(1)}, f32[40,128]{1,0:T(8,128)S(1)}, u32[]{:S(2)}, u32[]{:S(2)}) collective-permute-start(f32[40,128]{1,0:T(8,128)S(1)} %add_add_fusion.1), channel_id=1, source_target_pairs={{0,32},{1,33},{2,34},{3,35},{4,36},{5,37},{6,38},{7,39},{8,40},{9,... | collective-permute-start | bytes 61448 | tf_op jit(solution)/shard_map/ppermute | solution.py:386
  64.6 1.5 %collective-permute-start.18 = (f32[40,128]{1,0:T(8,128)S(1)}, f32[40,128]{1,0:T(8,128)S(1)}, u32[]{:S(2)}, u32[]{:S(2)}) collective-permute-start(f32[40,128]{1,0:T(8,128)S(1)} %add_add_fusion.1), channel_id=1, source_target_pairs={{0,56},{1,57},{2,58},{3,59},{4,60},{5,61},{6,62},{7,63},{8,48},{9,... | collective-permute-start | bytes 61448 | tf_op jit(solution)/shard_map/ppermute | solution.py:386
  66.1 2.7 %collective-permute-start.17 = (f32[40,128]{1,0:T(8,128)S(1)}, f32[40,128]{1,0:T(8,128)S(1)}, u32[]{:S(2)}, u32[]{:S(2)}) collective-permute-start(f32[40,128]{1,0:T(8,128)S(1)} %add_add_fusion.1), channel_id=1, source_target_pairs={{0,24},{1,25},{2,26},{3,27},{4,28},{5,29},{6,30},{7,31},{8,16},{9,... | collective-permute-start | bytes 61448 | tf_op jit(solution)/shard_map/ppermute | solution.py:386
  68.8 0.1 collective-permute-done.19
  68.9 0.7 collective-permute-done.18
  69.6 2.1 %collective-permute-done.17 = f32[40,128]{1,0:T(8,128)S(1)} collective-permute-done((f32[40,128]{1,0:T(8,128)S(1)}, f32[40,128]{1,0:T(8,128)S(1)}, u32[]{:S(2)}, u32[]{:S(2)}) %collective-permute-start.17) | collective-permute-done | bytes 20512 | tf_op jit(solution)/shard_map/ppermute | solution.py:386
  71.7 0.0 copy-done.4
  71.7 6.2 %shard_map.62 = (f32[3072,128]{1,0:T(8,128)}, f32[2,2,32,32]{3,2,1,0:T(8,128)}) custom-call(f32[4]{0:T(128)S(1)} %copy-done.4, f32[40,128]{1,0:T(8,128)S(1)} %add_add_fusion.moments, f32[2,3,8,32,128]{4,3,2,1,0:T(8,128)S(1)} %get-tuple-element.17.s0, f32[2,3,8,32,128]{4,3,2,1,0:T(8,128)S(1)} %get-tuple-element.28.s1, ...), custom_call_target="tpu_custom_call" | custom-call | tf_op jit(solution)/shard_map/pallas_call | solution.py:22
  (4 shorter events, 0.0 us)
Async XLA Ops:
  0.6 1.1 %copy-start = (f32[32,3,2,8,128]{4,3,2,1,0:T(8,128)S(1)}, f32[32,3,2,8,128]{4,3,2,1,0:T(8,128)}, u32[]{:S(2)}) copy-start(f32[32,3,2,8,128]{4,3,2,1,0:T(8,128)} %param.4) | copy-start | bytes 2359300
  1.8 0.7 copy-start.1
  2.5 0.7 copy-start.2
  3.2 0.7 copy-start.3
  4.7 31.7 %collective-permute-start = (f32[1544,128]{1,0:T(8,128)S(1)}, f32[1544,128]{1,0:T(8,128)S(1)}, u32[]{:S(2)}, u32[]{:S(2)}) collective-permute-start(f32[1544,128]{1,0:T(8,128)S(1)} %get-tuple-element.19), channel_id=1, source_target_pairs={{0,4},{1,5},{2,6},{3,7},{4,8},{5,9},{6,10},{7,11},{8,12},{9,13},{1... | collective-permute-start | bytes 2371592 | tf_op jit(solution)/shard_map/ppermute | solution.py:375
  4.8 31.6 %collective-permute-start.1 = (f32[1288,128]{1,0:T(8,128)S(1)}, f32[1288,128]{1,0:T(8,128)S(1)}, u32[]{:S(2)}, u32[]{:S(2)}) collective-permute-start(f32[1288,128]{1,0:T(8,128)S(1)} %get-tuple-element.20), channel_id=1, source_target_pairs={{0,252},{1,253},{2,254},{3,255},{4,0},{5,1},{6,2},{7,3},{8,4},{9,5... | collective-permute-start | bytes 1978376 | tf_op jit(solution)/shard_map/ppermute | solution.py:375
  12.6 10.5 %collective-permute-start.4 = (f32[96,128]{1,0:T(8,128)S(1)}, f32[96,128]{1,0:T(8,128)S(1)}, u32[]{:S(2)}, u32[]{:S(2)}) collective-permute-start(f32[96,128]{1,0:T(8,128)S(1)} %get-tuple-element.23), channel_id=1, source_target_pairs={{0,5},{1,6},{2,7},{3,4},{4,9},{5,10},{6,11},{7,8},{8,13},{9,14},{1... | collective-permute-start | bytes 147464 | tf_op jit(solution)/shard_map/ppermute | solution.py:375
  12.6 10.5 %collective-permute-start.7 = (f32[96,128]{1,0:T(8,128)S(1)}, f32[96,128]{1,0:T(8,128)S(1)}, u32[]{:S(2)}, u32[]{:S(2)}) collective-permute-start(f32[96,128]{1,0:T(8,128)S(1)} %get-tuple-element.26), channel_id=1, source_target_pairs={{0,255},{1,252},{2,253},{3,254},{4,3},{5,0},{6,1},{7,2},{8,7},{9,4... | collective-permute-start | bytes 147464 | tf_op jit(solution)/shard_map/ppermute | solution.py:375
  18.6 17.8 %collective-permute-start.2 = (f32[392,128]{1,0:T(8,128)S(1)}, f32[392,128]{1,0:T(8,128)S(1)}, u32[]{:S(2)}, u32[]{:S(2)}) collective-permute-start(f32[392,128]{1,0:T(8,128)S(1)} %get-tuple-element.21), channel_id=1, source_target_pairs={{0,1},{1,2},{2,3},{3,0},{4,5},{5,6},{6,7},{7,4},{8,9},{9,10},{10,1... | collective-permute-start | bytes 602120 | tf_op jit(solution)/shard_map/ppermute | solution.py:375
  23.1 9.3 %collective-permute-start.5 = (f32[168,128]{1,0:T(8,128)S(1)}, f32[168,128]{1,0:T(8,128)S(1)}, u32[]{:S(2)}, u32[]{:S(2)}) collective-permute-start(f32[168,128]{1,0:T(8,128)S(1)} %get-tuple-element.24), channel_id=1, source_target_pairs={{0,7},{1,4},{2,5},{3,6},{4,11},{5,8},{6,9},{7,10},{8,15},{9,12},{1... | collective-permute-start | bytes 258056 | tf_op jit(solution)/shard_map/ppermute | solution.py:375
  23.1 13.2 %collective-permute-start.3 = (f32[328,128]{1,0:T(8,128)S(1)}, f32[328,128]{1,0:T(8,128)S(1)}, u32[]{:S(2)}, u32[]{:S(2)}) collective-permute-start(f32[328,128]{1,0:T(8,128)S(1)} %get-tuple-element.22), channel_id=1, source_target_pairs={{0,3},{1,0},{2,1},{3,2},{4,7},{5,4},{6,5},{7,6},{8,11},{9,8},{10,9... | collective-permute-start | bytes 503816 | tf_op jit(solution)/shard_map/ppermute | solution.py:375
  32.5 3.9 %collective-permute-start.6 = (f32[168,128]{1,0:T(8,128)S(1)}, f32[168,128]{1,0:T(8,128)S(1)}, u32[]{:S(2)}, u32[]{:S(2)}) collective-permute-start(f32[168,128]{1,0:T(8,128)S(1)} %get-tuple-element.25), channel_id=1, source_target_pairs={{0,253},{1,254},{2,255},{3,252},{4,1},{5,2},{6,3},{7,0},{8,5},{9,6... | collective-permute-start | bytes 258056 | tf_op jit(solution)/shard_map/ppermute | solution.py:375
  36.4 35.3 %copy-start.4 = (f32[4]{0:T(128)S(1)}, f32[4]{0:T(128)}, u32[]{:S(2)}) copy-start(f32[4]{0:T(128)} %eps.3) | copy-start | bytes 52
  41.6 3.3 %collective-permute-start.10 = (f32[40,128]{1,0:T(8,128)S(1)}, f32[40,128]{1,0:T(8,128)S(1)}, u32[]{:S(2)}, u32[]{:S(2)}) collective-permute-start(f32[40,128]{1,0:T(8,128)S(1)} %get-tuple-element.27), channel_id=1, source_target_pairs={{0,5},{1,4},{2,7},{3,6},{4,1},{5,0},{6,3},{7,2},{8,13},{9,12},{10,... | collective-permute-start | bytes 61448 | tf_op jit(solution)/shard_map/ppermute | solution.py:386
  41.7 3.9 %collective-permute-start.9 = (f32[40,128]{1,0:T(8,128)S(1)}, f32[40,128]{1,0:T(8,128)S(1)}, u32[]{:S(2)}, u32[]{:S(2)}) collective-permute-start(f32[40,128]{1,0:T(8,128)S(1)} %get-tuple-element.27), channel_id=1, source_target_pairs={{0,1},{1,0},{2,3},{3,2},{4,5},{5,4},{6,7},{7,6},{8,9},{9,8},{10,11... | collective-permute-start | bytes 61448 | tf_op jit(solution)/shard_map/ppermute | solution.py:386
  42.3 3.3 %collective-permute-start.8 = (f32[40,128]{1,0:T(8,128)S(1)}, f32[40,128]{1,0:T(8,128)S(1)}, u32[]{:S(2)}, u32[]{:S(2)}) collective-permute-start(f32[40,128]{1,0:T(8,128)S(1)} %get-tuple-element.27), channel_id=1, source_target_pairs={{0,4},{1,5},{2,6},{3,7},{4,0},{5,1},{6,2},{7,3},{8,12},{9,13},{10,... | collective-permute-start | bytes 61448 | tf_op jit(solution)/shard_map/ppermute | solution.py:386
  45.6 6.0 %collective-permute-start.13 = (f32[40,128]{1,0:T(8,128)S(1)}, f32[40,128]{1,0:T(8,128)S(1)}, u32[]{:S(2)}, u32[]{:S(2)}) collective-permute-start(f32[40,128]{1,0:T(8,128)S(1)} %add_add_fusion.3), channel_id=1, source_target_pairs={{0,67},{1,66},{2,65},{3,64},{4,71},{5,70},{6,69},{7,68},{8,75},{9,... | collective-permute-start | bytes 61448 | tf_op jit(solution)/shard_map/ppermute | solution.py:386
  45.7 5.9 %collective-permute-start.12 = (f32[40,128]{1,0:T(8,128)S(1)}, f32[40,128]{1,0:T(8,128)S(1)}, u32[]{:S(2)}, u32[]{:S(2)}) collective-permute-start(f32[40,128]{1,0:T(8,128)S(1)} %add_add_fusion.3), channel_id=1, source_target_pairs={{0,64},{1,65},{2,66},{3,67},{4,68},{5,69},{6,70},{7,71},{8,72},{9,... | collective-permute-start | bytes 61448 | tf_op jit(solution)/shard_map/ppermute | solution.py:386
  49.6 5.0 %collective-permute-start.11 = (f32[40,128]{1,0:T(8,128)S(1)}, f32[40,128]{1,0:T(8,128)S(1)}, u32[]{:S(2)}, u32[]{:S(2)}) collective-permute-start(f32[40,128]{1,0:T(8,128)S(1)} %add_add_fusion.3), channel_id=1, source_target_pairs={{0,3},{1,2},{2,1},{3,0},{4,7},{5,6},{6,5},{7,4},{8,11},{9,10},{10,... | collective-permute-start | bytes 61448 | tf_op jit(solution)/shard_map/ppermute | solution.py:386
  54.6 6.0 %collective-permute-start.16 = (f32[40,128]{1,0:T(8,128)S(1)}, f32[40,128]{1,0:T(8,128)S(1)}, u32[]{:S(2)}, u32[]{:S(2)}) collective-permute-start(f32[40,128]{1,0:T(8,128)S(1)} %add_add_fusion.2), channel_id=1, source_target_pairs={{0,200},{1,201},{2,202},{3,203},{4,204},{5,205},{6,206},{7,207},{8... | collective-permute-start | bytes 61448 | tf_op jit(solution)/shard_map/ppermute | solution.py:386
  54.7 5.9 %collective-permute-start.15 = (f32[40,128]{1,0:T(8,128)S(1)}, f32[40,128]{1,0:T(8,128)S(1)}, u32[]{:S(2)}, u32[]{:S(2)}) collective-permute-start(f32[40,128]{1,0:T(8,128)S(1)} %add_add_fusion.2), channel_id=1, source_target_pairs={{0,8},{1,9},{2,10},{3,11},{4,12},{5,13},{6,14},{7,15},{8,0},{9,1},... | collective-permute-start | bytes 61448 | tf_op jit(solution)/shard_map/ppermute | solution.py:386
  55.7 5.5 %collective-permute-start.14 = (f32[40,128]{1,0:T(8,128)S(1)}, f32[40,128]{1,0:T(8,128)S(1)}, u32[]{:S(2)}, u32[]{:S(2)}) collective-permute-start(f32[40,128]{1,0:T(8,128)S(1)} %add_add_fusion.2), channel_id=1, source_target_pairs={{0,192},{1,193},{2,194},{3,195},{4,196},{5,197},{6,198},{7,199},{8... | collective-permute-start | bytes 61448 | tf_op jit(solution)/shard_map/ppermute | solution.py:386
  61.1 7.8 %collective-permute-start.19 = (f32[40,128]{1,0:T(8,128)S(1)}, f32[40,128]{1,0:T(8,128)S(1)}, u32[]{:S(2)}, u32[]{:S(2)}) collective-permute-start(f32[40,128]{1,0:T(8,128)S(1)} %add_add_fusion.1), channel_id=1, source_target_pairs={{0,32},{1,33},{2,34},{3,35},{4,36},{5,37},{6,38},{7,39},{8,40},{9,... | collective-permute-start | bytes 61448 | tf_op jit(solution)/shard_map/ppermute | solution.py:386
  64.6 5.0 %collective-permute-start.18 = (f32[40,128]{1,0:T(8,128)S(1)}, f32[40,128]{1,0:T(8,128)S(1)}, u32[]{:S(2)}, u32[]{:S(2)}) collective-permute-start(f32[40,128]{1,0:T(8,128)S(1)} %add_add_fusion.1), channel_id=1, source_target_pairs={{0,56},{1,57},{2,58},{3,59},{4,60},{5,61},{6,62},{7,63},{8,48},{9,... | collective-permute-start | bytes 61448 | tf_op jit(solution)/shard_map/ppermute | solution.py:386
  66.1 5.6 %collective-permute-start.17 = (f32[40,128]{1,0:T(8,128)S(1)}, f32[40,128]{1,0:T(8,128)S(1)}, u32[]{:S(2)}, u32[]{:S(2)}) collective-permute-start(f32[40,128]{1,0:T(8,128)S(1)} %add_add_fusion.1), channel_id=1, source_target_pairs={{0,24},{1,25},{2,26},{3,27},{4,28},{5,29},{6,30},{7,31},{8,16},{9,... | collective-permute-start | bytes 61448 | tf_op jit(solution)/shard_map/ppermute | solution.py:386

commit v3 on v2

--- a/solution.py
+++ b/solution.py
@@ -7,18 +7,21 @@
 from jax.experimental.pallas import tpu as pltpu
 from jax.sharding import PartitionSpec as P
 
-AXES = ("slab", "trans")
+AXES = ("y", "z", "core", "x")
 ABSORB = 4.0
 CURL_CENTRE = 5.0
 VMEM_LIMIT = 40 * 1024 * 1024
 
 
-def call(body, out_shape, operands, smem=(), scratch=()):
+def call(body, out_shape, operands, smem=(), hbm=(), hbm_out=(), scratch=()):
+    special = {**{i: pltpu.SMEM for i in smem}, **{i: pltpu.HBM for i in hbm}}
     specs = [
-        pl.BlockSpec(memory_space=pltpu.SMEM if i in smem else pltpu.VMEM)
-        for i in range(len(operands))
+        pl.BlockSpec(memory_space=special.get(i, pltpu.VMEM)) for i in range(len(operands))
     ]
-    outs = [pl.BlockSpec(memory_space=pltpu.VMEM) for _ in out_shape]
+    outs = [
+        pl.BlockSpec(memory_space=pltpu.HBM if i in hbm_out else pltpu.VMEM)
+        for i in range(len(out_shape))
+    ]
     return pl.pallas_call(
         body,
         out_shape=out_shape,
@@ -26,7 +29,12 @@
         out_specs=outs,
         scratch_shapes=list(scratch),
         compiler_params=pltpu.CompilerParams(vmem_limit_bytes=VMEM_LIMIT),
-    )(*operands)
+    )(
+        *(
+            pltpu.with_memory_space_constraint(a, pltpu.HBM) if i in hbm else a
+            for i, a in enumerate(operands)
+        )
+    )
 
 
 def shape(*dims):
@@ -45,12 +53,16 @@
         cells = set(self.first)
         for cell in self.first:
             cells |= reach(*cell)
+        self.names = [(0, -1), (0, 1), (-1, 0), (1, 0), (-1, 2), (1, 2)]
         self.blocks, self.diagonal = {}, {}
-        self.sides = sorted({self.side(z, x) for _, z, x in cells} - {(0, 0)}, key=side_order)
-        for side in self.sides:
-            self.blocks[side] = sorted(q for q in cells if self.side(q[1], q[2]) == side)
-            near = {q[1:] for q in self.first if self.side(q[1], q[2]) == side}
-            self.diagonal[side] = sorted(near)
+        for name in self.names:
+            self.blocks[name] = sorted(q for q in cells if self.name(q[1], q[2]) == name)
+            near = {q[1:] for q in self.first if self.name(q[1], q[2]) == name}
+            self.diagonal[name] = sorted(near)
+
+    def name(self, z, x):
+        side = self.side(z, x)
+        return (side[0], 2) if side[0] and side[1] else side
 
     def side(self, z, x):
         return (
@@ -58,15 +70,17 @@
             -1 if x < 0 else int(x >= self.xs),
         )
 
-    def own(self, side, z, x):
-        return z - side[0] * self.zs, x - side[1] * self.xs
-
-    def rows(self, side, width):
-        return len(self.blocks[side]) * width + (8 if self.diagonal[side] else 0)
-
-
-def side_order(side):
-    return (abs(side[0]) + abs(side[1]), -abs(side[0]), side)
+    def own(self, name, z, x):
+        return z - name[0] * self.zs, x - name[1] % 2 * name[1] * self.xs
+
+    def rows(self, name, width):
+        return len(self.blocks[name]) * width + 8
+
+    def block_row(self, name, c, z, x, width):
+        return self.blocks[name].index((c, z, x)) * width
+
+    def diagonal_row(self, name, z, x, width):
+        return len(self.blocks[name]) * width + self.diagonal[name].index((z, x))
 
 
 CURL = (
@@ -119,35 +133,66 @@
     return result
 
 
-def split_body(halo, width, classes, eps, material, mask, start, field, diag, *messages):
+def split_body(halo, width, classes, eps, material, mask, start, field, diag, *refs):
     zs, xs = halo.zs, halo.xs
     rows = 3 * zs * xs
+    messages, (start_in, material_in, mask_in, eps_in, sems) = refs[:4], refs[4:]
+    copies = [
+        pltpu.make_async_copy(source, target, sems.at[i])
+        for i, (source, target) in enumerate(
+            [(eps, eps_in), (material, material_in), (mask, mask_in), (start, start_in)]
+        )
+    ]
+    for copy in copies:
+        copy.start()
+    for copy in copies[:3]:
+        copy.wait()
+    eps = eps_in
     total = eps[0]
     for level in range(1, classes):
         total = total + eps[level]
     shift = total / classes + CURL_CENTRE
-    value = jnp.zeros(material.shape, jnp.float32)
+    value = jnp.zeros(material_in.shape, jnp.float32)
     for level in range(classes):
-        value = value + jnp.where(material[...] == level, eps[level], 0.0)
-    diag[...] = value + ABSORB * mask[...].astype(jnp.float32) - shift
+        value = value + jnp.where(material_in[...] == level, eps[level], 0.0)
+    diag[...] = value + ABSORB * mask_in[...].astype(jnp.float32) - shift
 
     places = {}
-    for side, message in zip(halo.sides, messages):
-        for i, (c, z, x) in enumerate(halo.blocks[side]):
-            places.setdefault((c, *halo.own(side, z, x)), []).append((message, i))
-        base = len(halo.blocks[side]) * width
-        if halo.diagonal[side]:
-            message[base : base + 8, :] = jnp.zeros((8, message.shape[1]), jnp.float32)
-        for i, (z, x) in enumerate(halo.diagonal[side]):
-            oz, ox = halo.own(side, z, x)
-            message[base + i : base + i + 1, :] = diag[oz, ox : ox + 1, :]
+    for name, message in zip(halo.names, messages):
+        for c, z, x in halo.blocks[name]:
+            row = halo.block_row(name, c, z, x, width)
+            places.setdefault((c, *halo.own(name, z, x)), []).append((message, row))
+        base = len(halo.blocks[name]) * width
+        message[base : base + 8, :] = jnp.zeros((8, message.shape[1]), jnp.float32)
+        for z, x in halo.diagonal[name]:
+            row = halo.diagonal_row(name, z, x, width)
+            oz, ox = halo.own(name, z, x)
+            message[row : row + 1, :] = diag[oz, ox : ox + 1, :]
+    copies[3].wait()
     for z in range(zs):
         for c in range(3):
             for x in range(xs):
-                cell = start[pl.ds((c * zs + z) * xs + x, width, stride=rows), :]
+                cell = start_in[pl.ds((c * zs + z) * xs + x, width, stride=rows), :]
                 field[z, c, x] = cell
-                for message, i in places.get((c, z, x), ()):
-                    message[i * width : (i + 1) * width, :] = cell
+                for message, row in places.get((c, z, x), ()):
+                    message[row : row + width, :] = cell
+
+
+def relay_body(halo, width, before, after, *passed):
+    received = {-1: ((0, -1), before), 1: ((0, 1), after)}
+    for name, message in zip(halo.names[4:], passed):
+        base = len(halo.blocks[name]) * width
+        message[base : base + 8, :] = jnp.zeros((8, message.shape[1]), jnp.float32)
+        for c, z, x in halo.blocks[name]:
+            side, source = received[halo.side(z, x)[1]]
+            at = halo.block_row(side, c, z - name[0] * halo.zs, x, width)
+            row = halo.block_row(name, c, z, x, width)
+            message[row : row + width, :] = source[at : at + width, :]
+        for z, x in halo.diagonal[name]:
+            side, source = received[halo.side(z, x)[1]]
+            at = halo.diagonal_row(side, z - name[0] * halo.zs, x, width)
+            row = halo.diagonal_row(name, z, x, width)
+            message[row : row + 1, :] = source[at : at + 1, :]
 
 
 def parts(value, count):
@@ -187,41 +232,36 @@
 
 def apply_body(halo, width, ny, slabs, trans, s0, diag, gram, *refs):
     zs, xs = halo.zs, halo.xs
-    count = len(halo.sides)
-    messages = dict(zip(halo.sides, refs[:count]))
-    s1, s2, moments, outer = refs[count:]
-    slab, across = lax.axis_index("slab"), lax.axis_index("trans")
+    messages = dict(zip(halo.names, refs[:6]))
+    s1, s2, moments, outer = refs[6:]
+    slab, across = lax.axis_index(AXES[:3]), lax.axis_index("x")
+    held_z = {-1: slab > 0, 0: slab >= 0, 1: slab < slabs - 1}
+    held_x = {-1: across > 0, 0: across >= 0, 1: across < trans - 1}
     inside = {
-        (-1, 0): slab > 0,
-        (1, 0): slab < slabs - 1,
-        (0, -1): across > 0,
-        (0, 1): across < trans - 1,
+        (i, j): jnp.where(jnp.logical_and(held_z[i], held_x[j]), 1.0, 0.0)
+        for i in (-1, 0, 1)
+        for j in (-1, 0, 1)
     }
-    inside = {side: jnp.where(held, 1.0, 0.0) for side, held in inside.items()}
-    for side in halo.sides:
-        if side not in inside:
-            inside[side] = inside[side[0], 0] * inside[0, side[1]]
-    block = {s: {q: i for i, q in enumerate(halo.blocks[s])} for s in halo.sides}
     extra = sorted(q for q in halo.first if halo.side(q[1], q[2]) != (0, 0))
     extra = {q: i for i, q in enumerate(extra)}
     lane = lax.broadcasted_iota(jnp.int32, (8, ny), 1)
 
     def diagonal(z, x):
-        side = halo.side(z, x)
-        if side == (0, 0):
+        name = halo.name(z, x)
+        if name == (0, 0):
             return diag[z, x : x + 1, :]
-        row = len(halo.blocks[side]) * width + halo.diagonal[side].index((z, x))
-        return messages[side][row : row + 1, :]
+        row = halo.diagonal_row(name, z, x, width)
+        return messages[name][row : row + 1, :]
 
     def group(g, carry):
         at = pl.multiple_of(g * 8, 8)
 
         def start(c, z, x):
-            side = halo.side(z, x)
-            if side == (0, 0):
+            name = halo.name(z, x)
+            if name == (0, 0):
                 return s0[z, c, x, pl.ds(at, 8), :]
-            place = block[side][c, z, x] * width
-            return messages[side][pl.ds(place + at, 8), :] * inside[side]
+            row = halo.block_row(name, c, z, x, width)
+            return messages[name][pl.ds(row + at, 8), :] * inside[halo.side(z, x)]
 
         def once(c, z, x):
             if halo.side(z, x) == (0, 0):
@@ -328,8 +368,11 @@
         total = total + eps[level]
     shift = total / classes + CURL_CENTRE
     m = []
+    summed = moments[0]
+    for i in range(1, moments.shape[0]):
+        summed = summed + moments[i]
     for k in range(5):
-        rows = moments[8 * k : 8 * k + 8, :] * (1.0 / entries)
+        rows = summed[8 * k : 8 * k + 8, :] * (1.0 / entries)
         found = jnp.concatenate([rows[:, w * j : w * j + w] for j in range(w // 8)], axis=0)
         m.append(0.5 * (found + found.T))
     gram = jnp.concatenate(
@@ -365,31 +408,33 @@
     couplings[1, 1] = precise(u22, x1, 1)
 
 
-def exchange(halo, messages, slabs, trans):
-    def moved(side, value):
-        pairs = [
-            (i * trans + j, (i - side[0]) % slabs * trans + (j - side[1]) % trans)
-            for i in range(slabs)
-            for j in range(trans)
-        ]
-        return lax.ppermute(value, AXES, pairs)
-
-    return [moved(side, value) for side, value in zip(halo.sides, messages)]
-
-
-def total_sum(value, slabs, trans):
-    devices = slabs * trans
-    groups = [(4, 1, 5), (3, 64, 67), (192, 8, 200), (24, 56, 32)]
-    if devices != 256:
-        groups = [(1 << b,) for b in range(devices.bit_length() - 1)]
-    for group in groups:
-        got = [lax.ppermute(value, AXES, [(i, i ^ m) for i in range(devices)]) for m in group]
-        for other in got:
-            value = value + other
-    return value
-
-
-def per_device(slabs, trans, start_block, material, pml_mask, eps_table):
+def moved(name, value, slabs, trans):
+    dz, dx = name[0], name[1] % 2 * name[1]
+    pairs = [
+        (i * trans + j, (i - dz) % slabs * trans + (j - dx) % trans)
+        for i in range(slabs)
+        for j in range(trans)
+    ]
+    return lax.ppermute(value, AXES, pairs)
+
+
+def total_sum(value, deep, trans, devices):
+    core, near = trans, 2 * trans
+    rounds = [(core, near, core ^ near)]
+    if deep == 8:
+        middle, far = 4 * trans, 8 * trans
+        rounds.append((middle, far ^ near, far ^ middle))
+    for masks in rounds:
+        one, two, three = (
+            lax.ppermute(value, AXES, [(i, i ^ m) for i in range(devices)]) for m in masks
+        )
+        value = (value + one) + (two + three)
+    count = devices // (2 * deep)
+    copies = jnp.broadcast_to(value[None], (count, *value.shape))
+    return lax.all_to_all(copies, ("y", "x"), 0, 0, tiled=True)
+
+
+def per_device(slabs, deep, trans, start_block, material, pml_mask, eps_table):
     width, _, zs, xs, ny = start_block.shape
     classes = eps_table.shape[0]
     entries = float(3 * zs * xs * ny * slabs * trans)
@@ -399,11 +444,24 @@
 
     s0, diag, *messages = call(
         functools.partial(split_body, halo, width, classes),
-        [field, shape(zs, xs, ny)] + [shape(halo.rows(s, width), ny) for s in halo.sides],
+        [field, shape(zs, xs, ny)] + [shape(halo.rows(n, width), ny) for n in halo.names[:4]],
         [eps_table, material, pml_mask, start_block.reshape(rows, ny)],
-        smem=(0,),
-    )
-    messages = exchange(halo, messages, slabs, trans)
+        hbm=(0, 1, 2, 3),
+        scratch=[
+            pltpu.VMEM((rows, ny), jnp.float32),
+            pltpu.VMEM((zs, xs, ny), jnp.int32),
+            pltpu.VMEM((zs, xs, ny), jnp.int32),
+            pltpu.SMEM((classes,), jnp.float32),
+            pltpu.SemaphoreType.DMA((4,)),
+        ],
+    )
+    messages = [moved(n, m, slabs, trans) for n, m in zip(halo.names, messages)]
+    passed = call(
+        functools.partial(relay_body, halo, width),
+        [shape(halo.rows(n, width), ny) for n in halo.names[4:]],
+        messages[:2],
+    )
+    messages += [moved(n, m, slabs, trans) for n, m in zip(halo.names[4:], passed)]
     (gram,) = call(functools.partial(start_gram_body, zs, xs), [shape(width, width)], [s0])
     outside = len(halo.first) - 3 * zs * xs
     s1, s2, moments = call(
@@ -412,7 +470,7 @@
         [s0, diag, gram] + messages,
         scratch=[pltpu.VMEM((outside, 8, ny), jnp.float32)],
     )
-    moments = total_sum(moments, slabs, trans)
+    moments = total_sum(moments, deep, trans, slabs * trans)
     blocks, couplings = call(
         functools.partial(last_body, zs, xs, width, ny, classes, entries),
         [shape(2 * rows, ny), shape(2, 2, width, width)],
@@ -423,16 +481,20 @@
 
 
 def solution(mesh):
-    sizes = dict(zip(mesh.axis_names, mesh.devices.shape))
+    slabs, trans = mesh.devices.shape
+    deep = 8 if slabs == 64 else 2
+    sizes = (slabs // (2 * deep), deep, 2, trans)
+    split = jax.sharding.Mesh(mesh.devices.reshape(sizes), AXES)
+    slab = AXES[:3]
     return jax.shard_map(
-        functools.partial(per_device, sizes["slab"], sizes["trans"]),
-        mesh=mesh,
+        functools.partial(per_device, slabs, deep, trans),
+        mesh=split,
         in_specs=(
-            P(None, None, "slab", "trans", None),
-            P("slab", "trans", None),
-            P("slab", "trans", None),
+            P(None, None, slab, "x", None),
+            P(slab, "x", None),
+            P(slab, "x", None),
             P(),
         ),
-        out_specs=(P(None, None, None, "slab", "trans", None), P()),
+        out_specs=(P(None, None, None, slab, "x", None), P()),
         check_vma=False,
     )

time: 78.1 us -> 65.9 us (0.84)
  the two profiles are of different devices: /device:TPU:6 before, /device:TPU:2 now
where the time goes in v3:
time: 65.9 us; the launch traced here: 65.8 us
  starting transfers between devices  22.2 us (34%)
  blocking collectives  16.8 us (25%)
  Pallas kernels  13.4 us (20%)
  waiting for transfers between devices  12.6 us (19%)
  between operations  0.71 us (1%)
    all_to_all x1, blocking collectives, total_sum(): return lax.all_to_all(copies, ('y', 'x'), 0, 0, tiled=True)  16.8 us
    ppermute x6, starting transfers between devices, moved(): return lax.ppermute(value, AXES, pairs)  15.1 us
    pallas_call x5, Pallas kernels, call(): pl.pallas_call(body, out_shape=out_shape, in_specs=specs, out_specs=outs,...  13.4 us
    ppermute x6, starting transfers between devices, total_sum(): lax.ppermute(value, AXES, [(i, i ^ m) for i in range(devices)])  7.18 us
    ppermute x6, waiting for transfers between devices, moved(): return lax.ppermute(value, AXES, pairs)  7.01 us
    ppermute x6, waiting for transfers between devices, total_sum(): lax.ppermute(value, AXES, [(i, i ^ m) for i in range(devices)])  5.56 us
  transfers between devices with their start and end apart: 12, of which 6 were waited for; matrix products, arithmetic and copies ran while one was open for 0% of the time, Pallas kernels for 1%

profile of v3, /device:TPU:2, one launch (start us, length us, event | category | flops | bytes accessed | tf_op | source)
XLA Modules:
  0.0 65.8 jit_solution(15889375679377763954)
XLA Ops:
  0.6 1.5 %shard_map.59 = (f32[2,3,8,32,128]{4,3,2,1,0:T(8,128)S(1)}, f32[2,8,128]{2,1,0:T(8,128)S(1)}, f32[392,128]{1,0:T(8,128)S(1)}, f32[328,128]{1,0:T(8,128)S(1)}, f3...) custom-call(f32[4]{0:T(128)} %eps.3, s32[2,8,128]{2,1,0:T(8,128)} %material.1, s32[2,8,128]{2,1,0:T(8,128)} %mask.1, ...), custom_call_target="tpu_custom_call" | custom-call | tf_op jit(solution)/shard_map/pallas_call | solution.py:25
  2.1 0.1 collective-permute-start.2
  2.2 7.8 %collective-permute-start.3 = (f32[1288,128]{1,0:T(8,128)S(1)}, f32[1288,128]{1,0:T(8,128)S(1)}, u32[]{:S(2)}, u32[]{:S(2)}) collective-permute-start(f32[1288,128]{1,0:T(8,128)S(1)} %get-tuple-element.20), channel_id=1, source_target_pairs={{0,252},{1,253},{2,254},{3,255},{4,0},{5,1},{6,2},{7,3},{8,4},{9,5... | collective-permute-start | bytes 1978376 | tf_op jit(solution)/shard_map/ppermute | solution.py:418
  10.1 1.5 %collective-permute-start = (f32[392,128]{1,0:T(8,128)S(1)}, f32[392,128]{1,0:T(8,128)S(1)}, u32[]{:S(2)}, u32[]{:S(2)}) collective-permute-start(f32[392,128]{1,0:T(8,128)S(1)} %get-tuple-element.17), channel_id=1, source_target_pairs={{0,1},{1,2},{2,3},{3,0},{4,5},{5,6},{6,7},{7,4},{8,9},{9,10},{10,1... | collective-permute-start | bytes 602120 | tf_op jit(solution)/shard_map/ppermute | solution.py:418
  11.5 0.5 collective-permute-start.1
  12.1 4.8 %collective-permute-done.1.after.refs_1_ = f32[328,128]{1,0:T(8,128)S(1)} collective-permute-done((f32[328,128]{1,0:T(8,128)S(1)}, f32[328,128]{1,0:T(8,128)S(1)}, u32[]{:S(2)}, u32[]{:S(2)}) %collective-permute-start.1) | collective-permute-done | bytes 167968 | tf_op jit(solution)/shard_map/ppermute | solution.py:418
  16.9 0.0 collective-permute-done.before.refs_0_
  16.9 0.1 collective-permute-start.4
  17.0 5.1 %collective-permute-start.5 = (f32[264,128]{1,0:T(8,128)S(1)}, f32[264,128]{1,0:T(8,128)S(1)}, u32[]{:S(2)}, u32[]{:S(2)}) collective-permute-start(f32[264,128]{1,0:T(8,128)S(1)} %get-tuple-element.22), channel_id=1, source_target_pairs={{0,252},{1,253},{2,254},{3,255},{4,0},{5,1},{6,2},{7,3},{8,4},{9,5... | collective-permute-start | bytes 405512 | tf_op jit(solution)/shard_map/ppermute | solution.py:418
  22.1 0.5 shard_map.60.gram
  22.6 2.2 %collective-permute-done.4.refs_4_ = f32[264,128]{1,0:T(8,128)S(1)} collective-permute-done((f32[264,128]{1,0:T(8,128)S(1)}, f32[264,128]{1,0:T(8,128)S(1)}, u32[]{:S(2)}, u32[]{:S(2)}) %collective-permute-start.4) | collective-permute-done | bytes 135200 | tf_op jit(solution)/shard_map/ppermute | solution.py:418
  24.8 0.0 collective-permute-done.5.refs_5_
  24.8 0.0 collective-permute-done.3.refs_3_
  24.8 0.0 collective-permute-done.2.refs_2_
  24.8 0.0 copy-start
  24.8 5.2 %shard_map.62 = (f32[2,3,8,32,128]{4,3,2,1,0:T(8,128)S(1)}, f32[2,3,8,32,128]{4,3,2,1,0:T(8,128)S(1)}, f32[40,128]{1,0:T(8,128)S(1)}) custom-call(f32[2,3,8,32,128]{4,3,2,1,0:T(8,128)S(1)} %get-tuple-element.15.s0, f32[2,8,128]{2,1,0:T(8,128)S(1)} %get-tuple-element.16.diag, f32[32,32]{1,0:T(8,128)S(1)} %shard_map.60.gram, ...), custom_call_target="tpu_custom_call" | custom-call | tf_op jit(solution)/shard_map/pallas_call | solution.py:25
  30.0 0.1 collective-permute-start.8
  30.1 0.1 collective-permute-start.7
  30.2 1.7 %collective-permute-start.6 = (f32[40,128]{1,0:T(8,128)S(1)}, f32[40,128]{1,0:T(8,128)S(1)}, u32[]{:S(2)}, u32[]{:S(2)}) collective-permute-start(f32[40,128]{1,0:T(8,128)S(1)} %get-tuple-element.23), channel_id=1, source_target_pairs={{0,4},{1,5},{2,6},{3,7},{4,0},{5,1},{6,2},{7,3},{8,12},{9,13},{10,... | collective-permute-start | bytes 61448 | tf_op jit(solution)/shard_map/ppermute | solution.py:429
  32.0 1.3 %collective-permute-done.8 = f32[40,128]{1,0:T(8,128)S(1)} collective-permute-done((f32[40,128]{1,0:T(8,128)S(1)}, f32[40,128]{1,0:T(8,128)S(1)}, u32[]{:S(2)}, u32[]{:S(2)}) %collective-permute-start.8) | collective-permute-done | bytes 20512 | tf_op jit(solution)/shard_map/ppermute | solution.py:429
  33.3 0.7 %collective-permute-done.7 = f32[40,128]{1,0:T(8,128)S(1)} collective-permute-done((f32[40,128]{1,0:T(8,128)S(1)}, f32[40,128]{1,0:T(8,128)S(1)}, u32[]{:S(2)}, u32[]{:S(2)}) %collective-permute-start.7) | collective-permute-done | bytes 20512 | tf_op jit(solution)/shard_map/ppermute | solution.py:429
  34.0 0.0 collective-permute-done.6
  34.0 1.6 %collective-permute-start.11 = (f32[40,128]{1,0:T(8,128)S(1)}, f32[40,128]{1,0:T(8,128)S(1)}, u32[]{:S(2)}, u32[]{:S(2)}) collective-permute-start(f32[40,128]{1,0:T(8,128)S(1)} %add_add_fusion.1), channel_id=1, source_target_pairs={{0,48},{1,49},{2,50},{3,51},{4,52},{5,53},{6,54},{7,55},{8,56},{9,... | collective-permute-start | bytes 61448 | tf_op jit(solution)/shard_map/ppermute | solution.py:429
  35.6 1.7 %collective-permute-start.10 = (f32[40,128]{1,0:T(8,128)S(1)}, f32[40,128]{1,0:T(8,128)S(1)}, u32[]{:S(2)}, u32[]{:S(2)}) collective-permute-start(f32[40,128]{1,0:T(8,128)S(1)} %add_add_fusion.1), channel_id=1, source_target_pairs={{0,40},{1,41},{2,42},{3,43},{4,44},{5,45},{6,46},{7,47},{8,32},{9,... | collective-permute-start | bytes 61448 | tf_op jit(solution)/shard_map/ppermute | solution.py:429
  37.3 1.9 %collective-permute-start.9 = (f32[40,128]{1,0:T(8,128)S(1)}, f32[40,128]{1,0:T(8,128)S(1)}, u32[]{:S(2)}, u32[]{:S(2)}) collective-permute-start(f32[40,128]{1,0:T(8,128)S(1)} %add_add_fusion.1), channel_id=1, source_target_pairs={{0,16},{1,17},{2,18},{3,19},{4,20},{5,21},{6,22},{7,23},{8,24},{9,... | collective-permute-start | bytes 61448 | tf_op jit(solution)/shard_map/ppermute | solution.py:429
  39.2 0.7 %collective-permute-done.11 = f32[40,128]{1,0:T(8,128)S(1)} collective-permute-done((f32[40,128]{1,0:T(8,128)S(1)}, f32[40,128]{1,0:T(8,128)S(1)}, u32[]{:S(2)}, u32[]{:S(2)}) %collective-permute-start.11) | collective-permute-done | bytes 20512 | tf_op jit(solution)/shard_map/ppermute | solution.py:429
  40.0 2.8 %collective-permute-done.10 = f32[40,128]{1,0:T(8,128)S(1)} collective-permute-done((f32[40,128]{1,0:T(8,128)S(1)}, f32[40,128]{1,0:T(8,128)S(1)}, u32[]{:S(2)}, u32[]{:S(2)}) %collective-permute-start.10) | collective-permute-done | bytes 20512 | tf_op jit(solution)/shard_map/ppermute | solution.py:429
  42.8 0.0 collective-permute-done.9
  42.8 16.8 %all_to_all.5.moments = f32[16,40,128]{2,1,0:T(8,128)S(1)} all-to-all(f32[16,40,128]{2,1,0:T(8,128)S(1)} %broadcast_in_dim.2), channel_id=1, replica_groups=mesh['y'=4,'z'=8,'core'=2,'x'=4] {'y','x'}, dimensions={0} | all-to-all | bytes 655360 | tf_op jit(solution)/shard_map/all_to_all | solution.py:434
  59.6 0.0 copy-done
  59.6 6.2 %shard_map.63 = (f32[3072,128]{1,0:T(8,128)}, f32[2,2,32,32]{3,2,1,0:T(8,128)}) custom-call(f32[4]{0:T(128)S(1)} %copy-done, f32[16,40,128]{2,1,0:T(8,128)S(1)} %all_to_all.5.moments, f32[2,3,8,32,128]{4,3,2,1,0:T(8,128)S(1)} %get-tuple-element.15.s0, f32[2,3,8,32,128]{4,3,2,1,0:T(8,128)S(1)} %get-tuple-element.24.s1, ...), custom_call_target="tpu_custom_call" | custom-call | tf_op jit(solution)/shard_map/pallas_call | solution.py:25
  (4 shorter events, 0.1 us)
Async XLA Ops:
  2.1 22.6 %collective-permute-start.2 = (f32[1544,128]{1,0:T(8,128)S(1)}, f32[1544,128]{1,0:T(8,128)S(1)}, u32[]{:S(2)}, u32[]{:S(2)}) collective-permute-start(f32[1544,128]{1,0:T(8,128)S(1)} %get-tuple-element.19), channel_id=1, source_target_pairs={{0,4},{1,5},{2,6},{3,7},{4,8},{5,9},{6,10},{7,11},{8,12},{9,13},{1... | collective-permute-start | bytes 2371592 | tf_op jit(solution)/shard_map/ppermute | solution.py:418
  2.2 22.5 %collective-permute-start.3 = (f32[1288,128]{1,0:T(8,128)S(1)}, f32[1288,128]{1,0:T(8,128)S(1)}, u32[]{:S(2)}, u32[]{:S(2)}) collective-permute-start(f32[1288,128]{1,0:T(8,128)S(1)} %get-tuple-element.20), channel_id=1, source_target_pairs={{0,252},{1,253},{2,254},{3,255},{4,0},{5,1},{6,2},{7,3},{8,4},{9,5... | collective-permute-start | bytes 1978376 | tf_op jit(solution)/shard_map/ppermute | solution.py:418
  10.1 6.9 %collective-permute-start = (f32[392,128]{1,0:T(8,128)S(1)}, f32[392,128]{1,0:T(8,128)S(1)}, u32[]{:S(2)}, u32[]{:S(2)}) collective-permute-start(f32[392,128]{1,0:T(8,128)S(1)} %get-tuple-element.17), channel_id=1, source_target_pairs={{0,1},{1,2},{2,3},{3,0},{4,5},{5,6},{6,7},{7,4},{8,9},{9,10},{10,1... | collective-permute-start | bytes 602120 | tf_op jit(solution)/shard_map/ppermute | solution.py:418
  11.5 5.4 %collective-permute-start.1 = (f32[328,128]{1,0:T(8,128)S(1)}, f32[328,128]{1,0:T(8,128)S(1)}, u32[]{:S(2)}, u32[]{:S(2)}) collective-permute-start(f32[328,128]{1,0:T(8,128)S(1)} %get-tuple-element.18), channel_id=1, source_target_pairs={{0,3},{1,0},{2,1},{3,2},{4,7},{5,4},{6,5},{7,6},{8,11},{9,8},{10,9... | collective-permute-start | bytes 503816 | tf_op jit(solution)/shard_map/ppermute | solution.py:418
  16.9 7.8 %collective-permute-start.4 = (f32[264,128]{1,0:T(8,128)S(1)}, f32[264,128]{1,0:T(8,128)S(1)}, u32[]{:S(2)}, u32[]{:S(2)}) collective-permute-start(f32[264,128]{1,0:T(8,128)S(1)} %get-tuple-element.21), channel_id=1, source_target_pairs={{0,4},{1,5},{2,6},{3,7},{4,8},{5,9},{6,10},{7,11},{8,12},{9,13},{1... | collective-permute-start | bytes 405512 | tf_op jit(solution)/shard_map/ppermute | solution.py:418
  17.0 7.7 %collective-permute-start.5 = (f32[264,128]{1,0:T(8,128)S(1)}, f32[264,128]{1,0:T(8,128)S(1)}, u32[]{:S(2)}, u32[]{:S(2)}) collective-permute-start(f32[264,128]{1,0:T(8,128)S(1)} %get-tuple-element.22), channel_id=1, source_target_pairs={{0,252},{1,253},{2,254},{3,255},{4,0},{5,1},{6,2},{7,3},{8,4},{9,5... | collective-permute-start | bytes 405512 | tf_op jit(solution)/shard_map/ppermute | solution.py:418
  24.8 34.8 %copy-start = (f32[4]{0:T(128)S(1)}, f32[4]{0:T(128)}, u32[]{:S(2)}) copy-start(f32[4]{0:T(128)} %eps.3) | copy-start | bytes 52
  30.0 3.3 %collective-permute-start.8 = (f32[40,128]{1,0:T(8,128)S(1)}, f32[40,128]{1,0:T(8,128)S(1)}, u32[]{:S(2)}, u32[]{:S(2)}) collective-permute-start(f32[40,128]{1,0:T(8,128)S(1)} %get-tuple-element.23), channel_id=1, source_target_pairs={{0,12},{1,13},{2,14},{3,15},{4,8},{5,9},{6,10},{7,11},{8,4},{9,5},... | collective-permute-start | bytes 61448 | tf_op jit(solution)/shard_map/ppermute | solution.py:429
  30.1 3.9 %collective-permute-start.7 = (f32[40,128]{1,0:T(8,128)S(1)}, f32[40,128]{1,0:T(8,128)S(1)}, u32[]{:S(2)}, u32[]{:S(2)}) collective-permute-start(f32[40,128]{1,0:T(8,128)S(1)} %get-tuple-element.23), channel_id=1, source_target_pairs={{0,8},{1,9},{2,10},{3,11},{4,12},{5,13},{6,14},{7,15},{8,0},{9,1},... | collective-permute-start | bytes 61448 | tf_op jit(solution)/shard_map/ppermute | solution.py:429
  30.2 3.8 %collective-permute-start.6 = (f32[40,128]{1,0:T(8,128)S(1)}, f32[40,128]{1,0:T(8,128)S(1)}, u32[]{:S(2)}, u32[]{:S(2)}) collective-permute-start(f32[40,128]{1,0:T(8,128)S(1)} %get-tuple-element.23), channel_id=1, source_target_pairs={{0,4},{1,5},{2,6},{3,7},{4,0},{5,1},{6,2},{7,3},{8,12},{9,13},{10,... | collective-permute-start | bytes 61448 | tf_op jit(solution)/shard_map/ppermute | solution.py:429
  34.0 6.0 %collective-permute-start.11 = (f32[40,128]{1,0:T(8,128)S(1)}, f32[40,128]{1,0:T(8,128)S(1)}, u32[]{:S(2)}, u32[]{:S(2)}) collective-permute-start(f32[40,128]{1,0:T(8,128)S(1)} %add_add_fusion.1), channel_id=1, source_target_pairs={{0,48},{1,49},{2,50},{3,51},{4,52},{5,53},{6,54},{7,55},{8,56},{9,... | collective-permute-start | bytes 61448 | tf_op jit(solution)/shard_map/ppermute | solution.py:429
  35.6 7.2 %collective-permute-start.10 = (f32[40,128]{1,0:T(8,128)S(1)}, f32[40,128]{1,0:T(8,128)S(1)}, u32[]{:S(2)}, u32[]{:S(2)}) collective-permute-start(f32[40,128]{1,0:T(8,128)S(1)} %add_add_fusion.1), channel_id=1, source_target_pairs={{0,40},{1,41},{2,42},{3,43},{4,44},{5,45},{6,46},{7,47},{8,32},{9,... | collective-permute-start | bytes 61448 | tf_op jit(solution)/shard_map/ppermute | solution.py:429
  37.3 5.4 %collective-permute-start.9 = (f32[40,128]{1,0:T(8,128)S(1)}, f32[40,128]{1,0:T(8,128)S(1)}, u32[]{:S(2)}, u32[]{:S(2)}) collective-permute-start(f32[40,128]{1,0:T(8,128)S(1)} %add_add_fusion.1), channel_id=1, source_target_pairs={{0,16},{1,17},{2,18},{3,19},{4,20},{5,21},{6,22},{7,23},{8,24},{9,... | collective-permute-start | bytes 61448 | tf_op jit(solution)/shard_map/ppermute | solution.py:429

commit v4 on v3

--- a/solution.py
+++ b/solution.py
@@ -253,9 +253,7 @@
         row = halo.diagonal_row(name, z, x, width)
         return messages[name][row : row + 1, :]
 
-    def group(g, carry):
-        at = pl.multiple_of(g * 8, 8)
-
+    def group(at):
         def start(c, z, x):
             name = halo.name(z, x)
             if name == (0, 0):
@@ -286,9 +284,9 @@
                 for c in range(3):
                     value = apply(c, z, x) + diagonal(z, x) * once(c, z, x)
                     s2[z, c, x, pl.ds(at, 8), :] = value
-        return carry
-
-    lax.fori_loop(0, width // 8, group, 0)
+
+    for at in range(0, width, 8):
+        group(at)
 
     total = None
     for z in range(zs):
@@ -325,21 +323,23 @@
     )
 
 
-def factor(gram, size):
+def factor(gram, size, pauses):
     tiles = size // 8
     lane = lax.broadcasted_iota(jnp.int32, (8, size), 1)
     sub = lax.broadcasted_iota(jnp.int32, (8, size), 0)
     upper = [gram[8 * t : 8 * t + 8, :] for t in range(tiles)]
     inverse = [jnp.where(lane == sub + 8 * t, 1.0, 0.0) for t in range(tiles)]
-    scales = []
+    found_u, found_i = [], []
+
+    def column(u, j):
+        return jnp.broadcast_to(upper[u][:, j : j + 1], (8, size))
+
+    ahead = [column(0, j) for j in range(8)]
     for t in range(tiles):
-        cols = {
-            u: [
-                jnp.broadcast_to(upper[u][:, 8 * t + j : 8 * t + j + 1], (8, size))
-                for j in range(8)
-            ]
-            for u in range(t, tiles)
-        }
+        cols = {u: [column(u, 8 * t + j) for j in range(8)] for u in range(t + 1, tiles)}
+        cols[t] = ahead
+        if t + 1 < tiles:
+            ahead = [column(t + 1, 8 * t + 8 + j) for j in range(8)]
         pivots = jnp.zeros((8, size), jnp.float32)
         for s in range(8):
             pivot = jnp.broadcast_to(cols[t][s][s : s + 1, :], (8, size))
@@ -351,18 +351,35 @@
                 f = cols[u][s] * reciprocal
                 if u == t:
                     f = jnp.where(sub > s, f, 0.0)
+                if u == t + 1:
+                    for j in range(8):
+                        ahead[j] = ahead[j] - f * cols[u][s][j : j + 1, :]
                 for j in range(s + 1, 8):
                     cols[u][j] = cols[u][j] - f * heads[j]
                 upper[u] = upper[u] - f * row_u
                 inverse[u] = inverse[u] - f * row_i
-        scales.append(lax.rsqrt(pivots))
-    upper = [a * s for a, s in zip(upper, scales)]
-    inverse = [a * s for a, s in zip(inverse, scales)]
-    return jnp.concatenate(upper, axis=0), jnp.concatenate(inverse, axis=0)
-
-
-def last_body(zs, xs, width, ny, classes, entries, eps, moments, s0, s1, s2, out, couplings):
+        scale = lax.rsqrt(pivots)
+        found_u.append(upper[t] * scale)
+        found_i.append(inverse[t] * scale)
+        if t + 1 in pauses:
+            yield jnp.concatenate(found_u, axis=0), jnp.concatenate(found_i, axis=0)
+
+
+def basis_body(zs, xs, width, s0, s1, s2, out):
     w = width
+    for i, (z, c, x) in enumerate(cell_pairs(zs, xs)):
+        first = jnp.concatenate([pair(s0, z, c, x), pair(s1, z, c, x)], axis=0)
+        out[i, : 4 * w] = jnp.concatenate(parts(first, 2), axis=0)
+        out[i, 4 * w :] = jnp.concatenate(parts(pair(s2, z, c, x), 2), axis=0)
+
+
+def cell_pairs(zs, xs):
+    return [(z, c, x) for z in range(zs) for c in range(3) for x in range(0, xs, 2)]
+
+
+def last_body(zs, xs, width, ny, classes, entries, eps, moments, basis, out, couplings, *scratch):
+    w = width
+    staged, sems = scratch
     total = eps[0]
     for level in range(1, classes):
         total = total + eps[level]
@@ -373,26 +390,33 @@
         summed = summed + moments[i]
     for k in range(5):
         rows = summed[8 * k : 8 * k + 8, :] * (1.0 / entries)
-        found = jnp.concatenate([rows[:, w * j : w * j + w] for j in range(w // 8)], axis=0)
-        m.append(0.5 * (found + found.T))
+        m.append(jnp.concatenate([rows[:, w * j : w * j + w] for j in range(w // 8)], axis=0))
     gram = jnp.concatenate(
         [jnp.concatenate([m[i + j] for j in range(3)], axis=1) for i in range(3)], axis=0
     )
-    upper, inverse = factor(gram, 3 * width)
-    mix = jnp.concatenate(
-        [jnp.concatenate([p, p], axis=1) for p in parts(inverse[w:], 3)], axis=0
-    )
     rows = 3 * zs * xs
-    for z in range(zs):
-        for c in range(3):
-            for x in range(0, xs, 2):
-                basis = jnp.concatenate([pair(s, z, c, x) for s in (s0, s1, s2)], axis=0)
-                terms = product(mix, jnp.concatenate(parts(basis, 2), axis=0), 0)
-                value = terms[: 2 * w] + terms[2 * w : 4 * w] + terms[4 * w :]
-                for k in range(2):
-                    out[pl.ds((c * zs + z) * xs + x + k, 2 * w, stride=rows), :] = value[
-                        :, k * ny : (k + 1) * ny
-                    ]
+
+    def combine(block, mix, depth):
+        for i, (z, c, x) in enumerate(cell_pairs(zs, xs)):
+            terms = product(mix, basis[i, :depth], 0)
+            value = terms[:w] + terms[w : 2 * w] + terms[2 * w :]
+            for k in range(2):
+                at = (c * zs + z) * xs + x + k
+                staged[block, pl.ds(at, w, stride=rows), :] = value[:, k * ny : (k + 1) * ny]
+        copy = pltpu.make_async_copy(staged.at[block], out.at[block], sems.at[block])
+        copy.start()
+        return copy
+
+    steps = factor(gram, 3 * w, (w // 4, 3 * w // 8))
+    upper, inverse = next(steps)
+    mix = [jnp.concatenate([p, p], axis=1) for p in parts(inverse[w:, : 2 * w], 3)]
+    copies = [combine(0, jnp.concatenate(mix, axis=0), 4 * w)]
+    upper, inverse = next(steps)
+    mix = [
+        jnp.concatenate([p[:, : 2 * w], p[:, : 2 * w], p[:, 2 * w :], p[:, 2 * w :]], axis=1)
+        for p in parts(inverse[2 * w :], 3)
+    ]
+    copies.append(combine(1, jnp.concatenate(mix, axis=0), 6 * w))
     identity = jnp.where(
         lax.broadcasted_iota(jnp.int32, (w, w), 0) == lax.broadcasted_iota(jnp.int32, (w, w), 1),
         shift,
@@ -406,6 +430,8 @@
     couplings[0, 1] = factor_one
     couplings[1, 0] = precise(u12 - precise(factor_one, u01, 0), x1, 1) + identity
     couplings[1, 1] = precise(u22, x1, 1)
+    for copy in copies:
+        copy.wait()
 
 
 def moved(name, value, slabs, trans):
@@ -471,11 +497,18 @@
         scratch=[pltpu.VMEM((outside, 8, ny), jnp.float32)],
     )
     moments = total_sum(moments, deep, trans, slabs * trans)
+    (basis,) = call(
+        functools.partial(basis_body, zs, xs, width),
+        [jax.ShapeDtypeStruct((len(cell_pairs(zs, xs)), 6 * width, 2 * ny), jnp.bfloat16)],
+        [s0, s1, s2],
+    )
     blocks, couplings = call(
         functools.partial(last_body, zs, xs, width, ny, classes, entries),
-        [shape(2 * rows, ny), shape(2, 2, width, width)],
-        [eps_table, moments, s0, s1, s2],
+        [shape(2, rows, ny), shape(2, 2, width, width)],
+        [eps_table, moments, basis],
         smem=(0,),
+        hbm_out=(0,),
+        scratch=[pltpu.VMEM((2, rows, ny), jnp.float32), pltpu.SemaphoreType.DMA((2,))],
     )
     return blocks.reshape(2, width, 3, zs, xs, ny), couplings
 

time: 65.9 us -> 64.8 us (0.983)
  blocking collectives: 16.8 us -> 0 us
  starting transfers between devices: 22.2 us -> 31.6 us
  waiting for transfers between devices: 12.6 us -> 17.6 us
  local copies, waits for them, and re-layouts: 0.03 us -> 4.79 us
  Pallas kernels: 13.4 us -> 9.72 us
    all_to_all x1 -> x0, blocking collectives: 16.8 us -> none  [total_sum(): return lax.all_to_all(copies, ('y', 'x'), 0, 0, tiled=True)]
    all_to_all x0 -> x1, starting transfers between devices: none -> 9.36 us  [total_sum(): return lax.all_to_all(copies, ('y', 'x'), 0, 0, tiled=True)]
    all_to_all x0 -> x1, waiting for transfers between devices: none -> 5.14 us  [total_sum(): return lax.all_to_all(copies, ('y', 'x'), 0, 0, tiled=True)]
    unnamed x2 -> x10, local copies, waits for them, and re-layouts: 0.01 us -> 4.03 us
    pallas_call x5 -> x6, Pallas kernels: 13.4 us -> 9.72 us  [call(): pl.pallas_call(body, out_shape=out_shape, in_specs=specs, out_specs=outs,...]
    broadcast_in_dim x1, local copies, waits for them, and re-layouts: 0.02 us -> 0.76 us  [total_sum(): copies = jnp.broadcast_to(value[None], (count, *value.shape))]
  transfers between devices with their start and end apart: 12 -> 13, of which waited for: 6 -> 7; matrix products, arithmetic and copies ran while one was open for 0% -> 0% of each run, Pallas kernels for 1% -> 1%
where the time goes in v4:
time: 64.8 us; the launch traced here: 64.6 us
  starting transfers between devices  31.6 us (49%)
  waiting for transfers between devices  17.6 us (27%)
  Pallas kernels  9.72 us (15%)
  local copies, waits for them, and re-layouts  4.79 us (7%)
  between operations  0.86 us (1%)
    ppermute x6, starting transfers between devices, moved(): return lax.ppermute(value, AXES, pairs)  15.1 us
    pallas_call x6, Pallas kernels, call(): pl.pallas_call(body, out_shape=out_shape, in_specs=specs, out_specs=outs,...  9.72 us
    all_to_all x1, starting transfers between devices, total_sum(): return lax.all_to_all(copies, ('y', 'x'), 0, 0, tiled=True)  9.36 us
    ppermute x6, starting transfers between devices, total_sum(): lax.ppermute(value, AXES, [(i, i ^ m) for i in range(devices)])  7.17 us
    ppermute x6, waiting for transfers between devices, moved(): return lax.ppermute(value, AXES, pairs)  7.01 us
    ppermute x6, waiting for transfers between devices, total_sum(): lax.ppermute(value, AXES, [(i, i ^ m) for i in range(devices)])  5.43 us
    all_to_all x1, waiting for transfers between devices, total_sum(): return lax.all_to_all(copies, ('y', 'x'), 0, 0, tiled=True)  5.14 us
    unnamed x10, local copies, waits for them, and re-layouts  4.03 us
  transfers between devices with their start and end apart: 13, of which 7 were waited for; matrix products, arithmetic and copies ran while one was open for 0% of the time, Pallas kernels for 1%

profile of v4, /device:TPU:2, one launch (start us, length us, event | category | flops | bytes accessed | tf_op | source)
XLA Modules:
  0.0 64.6 jit_solution(16624558874916555179)
XLA Ops:
  0.6 1.5 %shard_map.59 = (f32[2,3,8,32,128]{4,3,2,1,0:T(8,128)S(1)}, f32[2,8,128]{2,1,0:T(8,128)S(1)}, f32[392,128]{1,0:T(8,128)S(1)}, f32[328,128]{1,0:T(8,128)S(1)}, f3...) custom-call(f32[4]{0:T(128)} %eps.3, s32[2,8,128]{2,1,0:T(8,128)} %material.1, s32[2,8,128]{2,1,0:T(8,128)} %mask.1, ...), custom_call_target="tpu_custom_call" | custom-call | tf_op jit(solution)/shard_map/pallas_call | solution.py:25
  2.1 0.1 collective-permute-start.2
  2.2 7.8 %collective-permute-start.3 = (f32[1288,128]{1,0:T(8,128)S(1)}, f32[1288,128]{1,0:T(8,128)S(1)}, u32[]{:S(2)}, u32[]{:S(2)}) collective-permute-start(f32[1288,128]{1,0:T(8,128)S(1)} %get-tuple-element.20), channel_id=1, source_target_pairs={{0,252},{1,253},{2,254},{3,255},{4,0},{5,1},{6,2},{7,3},{8,4},{9,5... | collective-permute-start | bytes 1978376 | tf_op jit(solution)/shard_map/ppermute | solution.py:444
  10.1 1.5 %collective-permute-start = (f32[392,128]{1,0:T(8,128)S(1)}, f32[392,128]{1,0:T(8,128)S(1)}, u32[]{:S(2)}, u32[]{:S(2)}) collective-permute-start(f32[392,128]{1,0:T(8,128)S(1)} %get-tuple-element.17), channel_id=1, source_target_pairs={{0,1},{1,2},{2,3},{3,0},{4,5},{5,6},{6,7},{7,4},{8,9},{9,10},{10,1... | collective-permute-start | bytes 602120 | tf_op jit(solution)/shard_map/ppermute | solution.py:444
  11.5 0.5 collective-permute-start.1
  12.1 4.8 %collective-permute-done.1.after.refs_1_ = f32[328,128]{1,0:T(8,128)S(1)} collective-permute-done((f32[328,128]{1,0:T(8,128)S(1)}, f32[328,128]{1,0:T(8,128)S(1)}, u32[]{:S(2)}, u32[]{:S(2)}) %collective-permute-start.1) | collective-permute-done | bytes 167968 | tf_op jit(solution)/shard_map/ppermute | solution.py:444
  16.9 0.0 collective-permute-done.before.refs_0_
  16.9 0.1 collective-permute-start.4
  17.0 5.1 %collective-permute-start.5 = (f32[264,128]{1,0:T(8,128)S(1)}, f32[264,128]{1,0:T(8,128)S(1)}, u32[]{:S(2)}, u32[]{:S(2)}) collective-permute-start(f32[264,128]{1,0:T(8,128)S(1)} %get-tuple-element.22), channel_id=1, source_target_pairs={{0,252},{1,253},{2,254},{3,255},{4,0},{5,1},{6,2},{7,3},{8,4},{9,5... | collective-permute-start | bytes 405512 | tf_op jit(solution)/shard_map/ppermute | solution.py:444
  22.1 0.5 shard_map.60.gram
  22.6 2.2 %collective-permute-done.4.refs_4_ = f32[264,128]{1,0:T(8,128)S(1)} collective-permute-done((f32[264,128]{1,0:T(8,128)S(1)}, f32[264,128]{1,0:T(8,128)S(1)}, u32[]{:S(2)}, u32[]{:S(2)}) %collective-permute-start.4) | collective-permute-done | bytes 135200 | tf_op jit(solution)/shard_map/ppermute | solution.py:444
  24.8 0.0 collective-permute-done.5.refs_5_
  24.8 0.0 collective-permute-done.3.refs_3_
  24.8 0.0 collective-permute-done.2.refs_2_
  24.8 2.4 %shard_map.62 = (f32[2,3,8,32,128]{4,3,2,1,0:T(8,128)S(1)}, f32[2,3,8,32,128]{4,3,2,1,0:T(8,128)S(1)}, f32[40,128]{1,0:T(8,128)S(1)}) custom-call(f32[2,3,8,32,128]{4,3,2,1,0:T(8,128)S(1)} %get-tuple-element.15.s0, f32[2,8,128]{2,1,0:T(8,128)S(1)} %get-tuple-element.16.diag, f32[32,32]{1,0:T(8,128)S(1)} %shard_map.60.gram, ...), custom_call_target="tpu_custom_call" | custom-call | tf_op jit(solution)/shard_map/pallas_call | solution.py:25
  27.2 0.0 copy-start
  27.2 0.9 %copy-done = f32[2,3,8,32,128]{4,3,2,1,0:T(8,128)} copy-done((f32[2,3,8,32,128]{4,3,2,1,0:T(8,128)}, f32[2,3,8,32,128]{4,3,2,1,0:T(8,128)S(1)}, u32[]{:S(2)}) %copy-start) | copy-done | bytes 786456
  28.1 0.0 copy-start.2
  28.1 0.9 %copy-done.2 = f32[2,3,8,32,128]{4,3,2,1,0:T(8,128)} copy-done((f32[2,3,8,32,128]{4,3,2,1,0:T(8,128)}, f32[2,3,8,32,128]{4,3,2,1,0:T(8,128)S(1)}, u32[]{:S(2)}) %copy-start.2) | copy-done | bytes 786456
  29.0 0.0 collective-permute-start.8
  29.0 0.0 collective-permute-start.7
  29.0 1.9 %collective-permute-start.6 = (f32[40,128]{1,0:T(8,128)S(1)}, f32[40,128]{1,0:T(8,128)S(1)}, u32[]{:S(2)}, u32[]{:S(2)}) collective-permute-start(f32[40,128]{1,0:T(8,128)S(1)} %get-tuple-element.23), channel_id=1, source_target_pairs={{0,4},{1,5},{2,6},{3,7},{4,0},{5,1},{6,2},{7,3},{8,12},{9,13},{10,... | collective-permute-start | bytes 61448 | tf_op jit(solution)/shard_map/ppermute | solution.py:455
  30.8 1.3 %collective-permute-done.8 = f32[40,128]{1,0:T(8,128)S(1)} collective-permute-done((f32[40,128]{1,0:T(8,128)S(1)}, f32[40,128]{1,0:T(8,128)S(1)}, u32[]{:S(2)}, u32[]{:S(2)}) %collective-permute-start.8) | collective-permute-done | bytes 20512 | tf_op jit(solution)/shard_map/ppermute | solution.py:455
  32.2 0.6 collective-permute-done.7
  32.8 0.0 collective-permute-done.6
  32.8 1.7 %collective-permute-start.11 = (f32[40,128]{1,0:T(8,128)S(1)}, f32[40,128]{1,0:T(8,128)S(1)}, u32[]{:S(2)}, u32[]{:S(2)}) collective-permute-start(f32[40,128]{1,0:T(8,128)S(1)} %add_add_fusion.1), channel_id=1, source_target_pairs={{0,48},{1,49},{2,50},{3,51},{4,52},{5,53},{6,54},{7,55},{8,56},{9,... | collective-permute-start | bytes 61448 | tf_op jit(solution)/shard_map/ppermute | solution.py:455
  34.5 1.7 %collective-permute-start.10 = (f32[40,128]{1,0:T(8,128)S(1)}, f32[40,128]{1,0:T(8,128)S(1)}, u32[]{:S(2)}, u32[]{:S(2)}) collective-permute-start(f32[40,128]{1,0:T(8,128)S(1)} %add_add_fusion.1), channel_id=1, source_target_pairs={{0,40},{1,41},{2,42},{3,43},{4,44},{5,45},{6,46},{7,47},{8,32},{9,... | collective-permute-start | bytes 61448 | tf_op jit(solution)/shard_map/ppermute | solution.py:455
  36.2 1.9 %collective-permute-start.9 = (f32[40,128]{1,0:T(8,128)S(1)}, f32[40,128]{1,0:T(8,128)S(1)}, u32[]{:S(2)}, u32[]{:S(2)}) collective-permute-start(f32[40,128]{1,0:T(8,128)S(1)} %add_add_fusion.1), channel_id=1, source_target_pairs={{0,16},{1,17},{2,18},{3,19},{4,20},{5,21},{6,22},{7,23},{8,24},{9,... | collective-permute-start | bytes 61448 | tf_op jit(solution)/shard_map/ppermute | solution.py:455
  38.1 0.7 %collective-permute-done.11 = f32[40,128]{1,0:T(8,128)S(1)} collective-permute-done((f32[40,128]{1,0:T(8,128)S(1)}, f32[40,128]{1,0:T(8,128)S(1)}, u32[]{:S(2)}, u32[]{:S(2)}) %collective-permute-start.11) | collective-permute-done | bytes 20512 | tf_op jit(solution)/shard_map/ppermute | solution.py:455
  38.8 2.8 %collective-permute-done.10 = f32[40,128]{1,0:T(8,128)S(1)} collective-permute-done((f32[40,128]{1,0:T(8,128)S(1)}, f32[40,128]{1,0:T(8,128)S(1)}, u32[]{:S(2)}, u32[]{:S(2)}) %collective-permute-start.10) | collective-permute-done | bytes 20512 | tf_op jit(solution)/shard_map/ppermute | solution.py:455
  41.6 0.0 collective-permute-done.9
  41.6 0.8 %broadcast_in_dim.2 = f32[16,40,128]{2,1,0:T(8,128)} broadcast(f32[40,128]{1,0:T(8,128)S(1)} %add_add_fusion), dimensions={1,2} | broadcast | bytes 348160 | tf_op jit(solution)/shard_map/broadcast_in_dim | solution.py:459
  42.3 9.4 %all-to-all-start = ((f32[16,40,128]{2,1,0:T(8,128)}), f32[16,40,128]{2,1,0:T(8,128)S(1)}, u32[]{:S(2)}, u32[]{:S(2)}) async-start(f32[16,40,128]{2,1,0:T(8,128)} %broadcast_in_dim.2), calls=%async_computation | async-start | bytes 655360 | tf_op jit(solution)/shard_map/all_to_all | solution.py:460
  51.7 0.0 copy-start.1
  51.7 1.1 %copy-done.1 = f32[2,3,8,32,128]{4,3,2,1,0:T(8,128)S(1)} copy-done((f32[2,3,8,32,128]{4,3,2,1,0:T(8,128)S(1)}, f32[2,3,8,32,128]{4,3,2,1,0:T(8,128)}, u32[]{:S(2)}) %copy-start.1) | copy-done | bytes 786456
  52.8 0.0 copy-start.3
  52.8 1.1 %copy-done.3 = f32[2,3,8,32,128]{4,3,2,1,0:T(8,128)S(1)} copy-done((f32[2,3,8,32,128]{4,3,2,1,0:T(8,128)S(1)}, f32[2,3,8,32,128]{4,3,2,1,0:T(8,128)}, u32[]{:S(2)}) %copy-start.3) | copy-done | bytes 786456
  54.0 0.0 copy-start.4
  54.0 0.3 shard_map.63.basis
  54.2 5.1 %all-to-all-done.moments = f32[16,40,128]{2,1,0:T(8,128)S(1)} async-done(((f32[16,40,128]{2,1,0:T(8,128)}), f32[16,40,128]{2,1,0:T(8,128)S(1)}, u32[]{:S(2)}, u32[]{:S(2)}) %all-to-all-start) | async-done | bytes 327712 | tf_op jit(solution)/shard_map/all_to_all | solution.py:460
  59.4 0.0 copy-done.4
  59.4 5.0 %shard_map.64 = (f32[2,1536,128]{2,1,0:T(8,128)}, f32[2,2,32,32]{3,2,1,0:T(8,128)}) custom-call(f32[4]{0:T(128)S(1)} %copy-done.4, f32[16,40,128]{2,1,0:T(8,128)S(1)} %all-to-all-done.moments, bf16[24,192,256]{2,1,0:T(8,128)(2,1)S(1)} %shard_map.63.basis), custom_call_target="tpu_custom_call" | custom-call | tf_op jit(solution)/shard_map/pallas_call | solution.py:25
  (3 shorter events, 0.0 us)
Async XLA Ops:
  2.1 22.6 %collective-permute-start.2 = (f32[1544,128]{1,0:T(8,128)S(1)}, f32[1544,128]{1,0:T(8,128)S(1)}, u32[]{:S(2)}, u32[]{:S(2)}) collective-permute-start(f32[1544,128]{1,0:T(8,128)S(1)} %get-tuple-element.19), channel_id=1, source_target_pairs={{0,4},{1,5},{2,6},{3,7},{4,8},{5,9},{6,10},{7,11},{8,12},{9,13},{1... | collective-permute-start | bytes 2371592 | tf_op jit(solution)/shard_map/ppermute | solution.py:444
  2.2 22.5 %collective-permute-start.3 = (f32[1288,128]{1,0:T(8,128)S(1)}, f32[1288,128]{1,0:T(8,128)S(1)}, u32[]{:S(2)}, u32[]{:S(2)}) collective-permute-start(f32[1288,128]{1,0:T(8,128)S(1)} %get-tuple-element.20), channel_id=1, source_target_pairs={{0,252},{1,253},{2,254},{3,255},{4,0},{5,1},{6,2},{7,3},{8,4},{9,5... | collective-permute-start | bytes 1978376 | tf_op jit(solution)/shard_map/ppermute | solution.py:444
  10.1 6.9 %collective-permute-start = (f32[392,128]{1,0:T(8,128)S(1)}, f32[392,128]{1,0:T(8,128)S(1)}, u32[]{:S(2)}, u32[]{:S(2)}) collective-permute-start(f32[392,128]{1,0:T(8,128)S(1)} %get-tuple-element.17), channel_id=1, source_target_pairs={{0,1},{1,2},{2,3},{3,0},{4,5},{5,6},{6,7},{7,4},{8,9},{9,10},{10,1... | collective-permute-start | bytes 602120 | tf_op jit(solution)/shard_map/ppermute | solution.py:444
  11.5 5.4 %collective-permute-start.1 = (f32[328,128]{1,0:T(8,128)S(1)}, f32[328,128]{1,0:T(8,128)S(1)}, u32[]{:S(2)}, u32[]{:S(2)}) collective-permute-start(f32[328,128]{1,0:T(8,128)S(1)} %get-tuple-element.18), channel_id=1, source_target_pairs={{0,3},{1,0},{2,1},{3,2},{4,7},{5,4},{6,5},{7,6},{8,11},{9,8},{10,9... | collective-permute-start | bytes 503816 | tf_op jit(solution)/shard_map/ppermute | solution.py:444
  16.9 7.8 %collective-permute-start.4 = (f32[264,128]{1,0:T(8,128)S(1)}, f32[264,128]{1,0:T(8,128)S(1)}, u32[]{:S(2)}, u32[]{:S(2)}) collective-permute-start(f32[264,128]{1,0:T(8,128)S(1)} %get-tuple-element.21), channel_id=1, source_target_pairs={{0,4},{1,5},{2,6},{3,7},{4,8},{5,9},{6,10},{7,11},{8,12},{9,13},{1... | collective-permute-start | bytes 405512 | tf_op jit(solution)/shard_map/ppermute | solution.py:444
  17.0 7.7 %collective-permute-start.5 = (f32[264,128]{1,0:T(8,128)S(1)}, f32[264,128]{1,0:T(8,128)S(1)}, u32[]{:S(2)}, u32[]{:S(2)}) collective-permute-start(f32[264,128]{1,0:T(8,128)S(1)} %get-tuple-element.22), channel_id=1, source_target_pairs={{0,252},{1,253},{2,254},{3,255},{4,0},{5,1},{6,2},{7,3},{8,4},{9,5... | collective-permute-start | bytes 405512 | tf_op jit(solution)/shard_map/ppermute | solution.py:444
  27.2 0.9 %copy-start = (f32[2,3,8,32,128]{4,3,2,1,0:T(8,128)}, f32[2,3,8,32,128]{4,3,2,1,0:T(8,128)S(1)}, u32[]{:S(2)}) copy-start(f32[2,3,8,32,128]{4,3,2,1,0:T(8,128)S(1)} %get-tuple-element.24.s1) | copy-start | bytes 2359300
  28.1 0.9 %copy-start.2 = (f32[2,3,8,32,128]{4,3,2,1,0:T(8,128)}, f32[2,3,8,32,128]{4,3,2,1,0:T(8,128)S(1)}, u32[]{:S(2)}) copy-start(f32[2,3,8,32,128]{4,3,2,1,0:T(8,128)S(1)} %get-tuple-element.25.s2) | copy-start | bytes 2359300
  29.0 3.2 %collective-permute-start.8 = (f32[40,128]{1,0:T(8,128)S(1)}, f32[40,128]{1,0:T(8,128)S(1)}, u32[]{:S(2)}, u32[]{:S(2)}) collective-permute-start(f32[40,128]{1,0:T(8,128)S(1)} %get-tuple-element.23), channel_id=1, source_target_pairs={{0,12},{1,13},{2,14},{3,15},{4,8},{5,9},{6,10},{7,11},{8,4},{9,5},... | collective-permute-start | bytes 61448 | tf_op jit(solution)/shard_map/ppermute | solution.py:455
  29.0 3.8 %collective-permute-start.7 = (f32[40,128]{1,0:T(8,128)S(1)}, f32[40,128]{1,0:T(8,128)S(1)}, u32[]{:S(2)}, u32[]{:S(2)}) collective-permute-start(f32[40,128]{1,0:T(8,128)S(1)} %get-tuple-element.23), channel_id=1, source_target_pairs={{0,8},{1,9},{2,10},{3,11},{4,12},{5,13},{6,14},{7,15},{8,0},{9,1},... | collective-permute-start | bytes 61448 | tf_op jit(solution)/shard_map/ppermute | solution.py:455
  29.0 3.8 %collective-permute-start.6 = (f32[40,128]{1,0:T(8,128)S(1)}, f32[40,128]{1,0:T(8,128)S(1)}, u32[]{:S(2)}, u32[]{:S(2)}) collective-permute-start(f32[40,128]{1,0:T(8,128)S(1)} %get-tuple-element.23), channel_id=1, source_target_pairs={{0,4},{1,5},{2,6},{3,7},{4,0},{5,1},{6,2},{7,3},{8,12},{9,13},{10,... | collective-permute-start | bytes 61448 | tf_op jit(solution)/shard_map/ppermute | solution.py:455
  32.8 6.0 %collective-permute-start.11 = (f32[40,128]{1,0:T(8,128)S(1)}, f32[40,128]{1,0:T(8,128)S(1)}, u32[]{:S(2)}, u32[]{:S(2)}) collective-permute-start(f32[40,128]{1,0:T(8,128)S(1)} %add_add_fusion.1), channel_id=1, source_target_pairs={{0,48},{1,49},{2,50},{3,51},{4,52},{5,53},{6,54},{7,55},{8,56},{9,... | collective-permute-start | bytes 61448 | tf_op jit(solution)/shard_map/ppermute | solution.py:455
  34.5 7.1 %collective-permute-start.10 = (f32[40,128]{1,0:T(8,128)S(1)}, f32[40,128]{1,0:T(8,128)S(1)}, u32[]{:S(2)}, u32[]{:S(2)}) collective-permute-start(f32[40,128]{1,0:T(8,128)S(1)} %add_add_fusion.1), channel_id=1, source_target_pairs={{0,40},{1,41},{2,42},{3,43},{4,44},{5,45},{6,46},{7,47},{8,32},{9,... | collective-permute-start | bytes 61448 | tf_op jit(solution)/shard_map/ppermute | solution.py:455
  36.2 5.4 %collective-permute-start.9 = (f32[40,128]{1,0:T(8,128)S(1)}, f32[40,128]{1,0:T(8,128)S(1)}, u32[]{:S(2)}, u32[]{:S(2)}) collective-permute-start(f32[40,128]{1,0:T(8,128)S(1)} %add_add_fusion.1), channel_id=1, source_target_pairs={{0,16},{1,17},{2,18},{3,19},{4,20},{5,21},{6,22},{7,23},{8,24},{9,... | collective-permute-start | bytes 61448 | tf_op jit(solution)/shard_map/ppermute | solution.py:455
  42.3 17.0 %all-to-all-start = ((f32[16,40,128]{2,1,0:T(8,128)}), f32[16,40,128]{2,1,0:T(8,128)S(1)}, u32[]{:S(2)}, u32[]{:S(2)}) async-start(f32[16,40,128]{2,1,0:T(8,128)} %broadcast_in_dim.2), calls=%async_computation | async-start | bytes 655360 | tf_op jit(solution)/shard_map/all_to_all | solution.py:460
  51.7 1.1 %copy-start.1 = (f32[2,3,8,32,128]{4,3,2,1,0:T(8,128)S(1)}, f32[2,3,8,32,128]{4,3,2,1,0:T(8,128)}, u32[]{:S(2)}) copy-start(f32[2,3,8,32,128]{4,3,2,1,0:T(8,128)} %copy-done) | copy-start | bytes 2359300
  52.8 1.1 %copy-start.3 = (f32[2,3,8,32,128]{4,3,2,1,0:T(8,128)S(1)}, f32[2,3,8,32,128]{4,3,2,1,0:T(8,128)}, u32[]{:S(2)}) copy-start(f32[2,3,8,32,128]{4,3,2,1,0:T(8,128)} %copy-done.2) | copy-start | bytes 2359300
  54.0 5.4 %copy-start.4 = (f32[4]{0:T(128)S(1)}, f32[4]{0:T(128)}, u32[]{:S(2)}) copy-start(f32[4]{0:T(128)} %eps.3) | copy-start | bytes 52

commit v5 on v4

--- a/solution.py
+++ b/solution.py
@@ -219,21 +219,23 @@
     return rows[:, :right] + rows[:, right : 2 * right] + rows[:, 2 * right :]
 
 
+def cell_pairs(zs, xs):
+    return [(z, c, x) for z in range(zs) for c in range(3) for x in range(0, xs, 2)]
+
+
 def start_gram_body(zs, xs, s0, out):
     total = None
-    for z in range(zs):
-        for c in range(3):
-            for x in range(0, xs, 2):
-                stack = jnp.concatenate(parts(pair(s0, z, c, x), 3), axis=0)
-                term = product(stack, stack, 1)
-                total = term if total is None else total + term
+    for z, c, x in cell_pairs(zs, xs):
+        stack = jnp.concatenate(parts(pair(s0, z, c, x), 3), axis=0)
+        term = product(stack, stack, 1)
+        total = term if total is None else total + term
     out[...] = fold(total, *out.shape)
 
 
 def apply_body(halo, width, ny, slabs, trans, s0, diag, gram, *refs):
     zs, xs = halo.zs, halo.xs
     messages = dict(zip(halo.names, refs[:6]))
-    s1, s2, moments, outer = refs[6:]
+    basis, moments, s1, s2, outer = refs[6:]
     slab, across = lax.axis_index(AXES[:3]), lax.axis_index("x")
     held_z = {-1: slab > 0, 0: slab >= 0, 1: slab < slabs - 1}
     held_x = {-1: across > 0, 0: across >= 0, 1: across < trans - 1}
@@ -289,16 +291,13 @@
         group(at)
 
     total = None
-    for z in range(zs):
-        for c in range(3):
-            for x in range(0, xs, 2):
-                split = [parts(pair(s, z, c, x), 3) for s in (s0, s1, s2)]
-                left = jnp.concatenate([p for i in range(3) for p in (s[i] for s in split)], axis=0)
-                right = jnp.concatenate(
-                    [p for i in range(3) for p in (s[i] for s in split[1:])], axis=0
-                )
-                term = product(left, right, 1)
-                total = term if total is None else total + term
+    for i, (z, c, x) in enumerate(cell_pairs(zs, xs)):
+        k0, k1, k2 = (parts(pair(s, z, c, x), 3) for s in (s0, s1, s2))
+        basis[i] = jnp.concatenate([k0[0], k1[0], k0[1], k1[1], k2[0], k2[1]], axis=0)
+        left = jnp.concatenate([p for three in zip(k0, k1, k2) for p in three], axis=0)
+        right = jnp.concatenate([p for two in zip(k1, k2) for p in two], axis=0)
+        term = product(left, right, 1)
+        total = term if total is None else total + term
     found = fold(total, 3 * width, 2 * width)
     w = width
     found = [
@@ -365,18 +364,6 @@
             yield jnp.concatenate(found_u, axis=0), jnp.concatenate(found_i, axis=0)
 
 
-def basis_body(zs, xs, width, s0, s1, s2, out):
-    w = width
-    for i, (z, c, x) in enumerate(cell_pairs(zs, xs)):
-        first = jnp.concatenate([pair(s0, z, c, x), pair(s1, z, c, x)], axis=0)
-        out[i, : 4 * w] = jnp.concatenate(parts(first, 2), axis=0)
-        out[i, 4 * w :] = jnp.concatenate(parts(pair(s2, z, c, x), 2), axis=0)
-
-
-def cell_pairs(zs, xs):
-    return [(z, c, x) for z in range(zs) for c in range(3) for x in range(0, xs, 2)]
-
-
 def last_body(zs, xs, width, ny, classes, entries, eps, moments, basis, out, couplings, *scratch):
     w = width
     staged, sems = scratch
@@ -490,18 +477,20 @@
     messages += [moved(n, m, slabs, trans) for n, m in zip(halo.names[4:], passed)]
     (gram,) = call(functools.partial(start_gram_body, zs, xs), [shape(width, width)], [s0])
     outside = len(halo.first) - 3 * zs * xs
-    s1, s2, moments = call(
+    basis, moments = call(
         functools.partial(apply_body, halo, width, ny, slabs, trans),
-        [field, field, shape(40, 4 * width)],
+        [
+            jax.ShapeDtypeStruct((len(cell_pairs(zs, xs)), 6 * width, 2 * ny), jnp.bfloat16),
+            shape(40, 4 * width),
+        ],
         [s0, diag, gram] + messages,
-        scratch=[pltpu.VMEM((outside, 8, ny), jnp.float32)],
+        scratch=[
+            pltpu.VMEM(field.shape, jnp.float32),
+            pltpu.VMEM(field.shape, jnp.float32),
+            pltpu.VMEM((outside, 8, ny), jnp.float32),
+        ],
     )
     moments = total_sum(moments, deep, trans, slabs * trans)
-    (basis,) = call(
-        functools.partial(basis_body, zs, xs, width),
-        [jax.ShapeDtypeStruct((len(cell_pairs(zs, xs)), 6 * width, 2 * ny), jnp.bfloat16)],
-        [s0, s1, s2],
-    )
     blocks, couplings = call(
         functools.partial(last_body, zs, xs, width, ny, classes, entries),
         [shape(2, rows, ny), shape(2, 2, width, width)],

time: 64.8 us -> 62.2 us (0.960)
  blocking collectives: 0 us -> 16.8 us
  starting transfers between devices: 31.6 us -> 22.2 us
  waiting for transfers between devices: 17.6 us -> 12.6 us
  local copies, waits for them, and re-layouts: 4.79 us -> 0.03 us
    all_to_all x0 -> x1, blocking collectives: none -> 16.8 us  [total_sum(): return lax.all_to_all(copies, ('y', 'x'), 0, 0, tiled=True)]
    all_to_all x1 -> x0, starting transfers between devices: 9.36 us -> none  [total_sum(): return lax.all_to_all(copies, ('y', 'x'), 0, 0, tiled=True)]
    all_to_all x1 -> x0, waiting for transfers between devices: 5.14 us -> none  [total_sum(): return lax.all_to_all(copies, ('y', 'x'), 0, 0, tiled=True)]
    unnamed x10 -> x2, local copies, waits for them, and re-layouts: 4.03 us -> 0.01 us
    broadcast_in_dim x1, local copies, waits for them, and re-layouts: 0.76 us -> 0.02 us  [total_sum(): copies = jnp.broadcast_to(value[None], (count, *value.shape))]
    pallas_call x6 -> x5, Pallas kernels: 9.72 us -> 9.6 us  [call(): pl.pallas_call(body, out_shape=out_shape, in_specs=specs, out_specs=outs,...]
  transfers between devices with their start and end apart: 13 -> 12, of which waited for: 7 -> 6; matrix products, arithmetic and copies ran while one was open for 0% -> 0% of each run, Pallas kernels for 1% -> 1%
where the time goes in v5:
time: 62.2 us; the launch traced here: 62.1 us
  starting transfers between devices  22.2 us (36%)
  blocking collectives  16.8 us (27%)
  waiting for transfers between devices  12.6 us (20%)
  Pallas kernels  9.6 us (15%)
  between operations  0.86 us (1%)
    all_to_all x1, blocking collectives, total_sum(): return lax.all_to_all(copies, ('y', 'x'), 0, 0, tiled=True)  16.8 us
    ppermute x6, starting transfers between devices, moved(): return lax.ppermute(value, AXES, pairs)  15.1 us
    pallas_call x5, Pallas kernels, call(): pl.pallas_call(body, out_shape=out_shape, in_specs=specs, out_specs=outs,...  9.6 us
    ppermute x6, starting transfers between devices, total_sum(): lax.ppermute(value, AXES, [(i, i ^ m) for i in range(devices)])  7.18 us
    ppermute x6, waiting for transfers between devices, moved(): return lax.ppermute(value, AXES, pairs)  7.01 us
    ppermute x6, waiting for transfers between devices, total_sum(): lax.ppermute(value, AXES, [(i, i ^ m) for i in range(devices)])  5.56 us
  transfers between devices with their start and end apart: 12, of which 6 were waited for; matrix products, arithmetic and copies ran while one was open for 0% of the time, Pallas kernels for 1%

profile of v5, /device:TPU:2, one launch (start us, length us, event | category | flops | bytes accessed | tf_op | source)
XLA Modules:
  0.0 62.1 jit_solution(3715192001909667067)
XLA Ops:
  0.6 1.5 %shard_map.59 = (f32[2,3,8,32,128]{4,3,2,1,0:T(8,128)S(1)}, f32[2,8,128]{2,1,0:T(8,128)S(1)}, f32[392,128]{1,0:T(8,128)S(1)}, f32[328,128]{1,0:T(8,128)S(1)}, f3...) custom-call(f32[4]{0:T(128)} %eps.3, s32[2,8,128]{2,1,0:T(8,128)} %material.1, s32[2,8,128]{2,1,0:T(8,128)} %mask.1, ...), custom_call_target="tpu_custom_call" | custom-call | tf_op jit(solution)/shard_map/pallas_call | solution.py:25
  2.1 0.1 collective-permute-start.2
  2.2 7.8 %collective-permute-start.3 = (f32[1288,128]{1,0:T(8,128)S(1)}, f32[1288,128]{1,0:T(8,128)S(1)}, u32[]{:S(2)}, u32[]{:S(2)}) collective-permute-start(f32[1288,128]{1,0:T(8,128)S(1)} %get-tuple-element.19), channel_id=1, source_target_pairs={{0,252},{1,253},{2,254},{3,255},{4,0},{5,1},{6,2},{7,3},{8,4},{9,5... | collective-permute-start | bytes 1978376 | tf_op jit(solution)/shard_map/ppermute | solution.py:431
  10.1 1.5 %collective-permute-start = (f32[392,128]{1,0:T(8,128)S(1)}, f32[392,128]{1,0:T(8,128)S(1)}, u32[]{:S(2)}, u32[]{:S(2)}) collective-permute-start(f32[392,128]{1,0:T(8,128)S(1)} %get-tuple-element.16), channel_id=1, source_target_pairs={{0,1},{1,2},{2,3},{3,0},{4,5},{5,6},{6,7},{7,4},{8,9},{9,10},{10,1... | collective-permute-start | bytes 602120 | tf_op jit(solution)/shard_map/ppermute | solution.py:431
  11.5 0.5 collective-permute-start.1
  12.1 4.8 %collective-permute-done.1.after.refs_1_ = f32[328,128]{1,0:T(8,128)S(1)} collective-permute-done((f32[328,128]{1,0:T(8,128)S(1)}, f32[328,128]{1,0:T(8,128)S(1)}, u32[]{:S(2)}, u32[]{:S(2)}) %collective-permute-start.1) | collective-permute-done | bytes 167968 | tf_op jit(solution)/shard_map/ppermute | solution.py:431
  16.9 0.0 collective-permute-done.before.refs_0_
  16.9 0.1 collective-permute-start.4
  17.0 5.1 %collective-permute-start.5 = (f32[264,128]{1,0:T(8,128)S(1)}, f32[264,128]{1,0:T(8,128)S(1)}, u32[]{:S(2)}, u32[]{:S(2)}) collective-permute-start(f32[264,128]{1,0:T(8,128)S(1)} %get-tuple-element.21), channel_id=1, source_target_pairs={{0,252},{1,253},{2,254},{3,255},{4,0},{5,1},{6,2},{7,3},{8,4},{9,5... | collective-permute-start | bytes 405512 | tf_op jit(solution)/shard_map/ppermute | solution.py:431
  22.1 0.0 copy-start
  22.1 0.5 shard_map.60.gram
  22.6 2.2 %collective-permute-done.4.refs_4_ = f32[264,128]{1,0:T(8,128)S(1)} collective-permute-done((f32[264,128]{1,0:T(8,128)S(1)}, f32[264,128]{1,0:T(8,128)S(1)}, u32[]{:S(2)}, u32[]{:S(2)}) %collective-permute-start.4) | collective-permute-done | bytes 135200 | tf_op jit(solution)/shard_map/ppermute | solution.py:431
  24.8 0.0 collective-permute-done.5.refs_5_
  24.8 0.0 collective-permute-done.3.refs_3_
  24.8 0.0 collective-permute-done.2.refs_2_
  24.8 2.6 %shard_map.62 = (bf16[24,192,256]{2,1,0:T(8,128)(2,1)S(1)}, f32[40,128]{1,0:T(8,128)S(1)}) custom-call(f32[2,3,8,32,128]{4,3,2,1,0:T(8,128)S(1)} %get-tuple-element.14.s0, f32[2,8,128]{2,1,0:T(8,128)S(1)} %get-tuple-element.15.diag, f32[32,32]{1,0:T(8,128)S(1)} %shard_map.60.gram, f32[392,128]{1,0:T(8,128)S(1)} %collective-permute-done.before.refs_0_, ...), custom_call_target="tpu_custom_call" | custom-call | tf_op jit(solution)/shard_map/pallas_call | solution.py:25
  27.3 0.1 collective-permute-start.8
  27.4 0.1 collective-permute-start.7
  27.5 1.7 %collective-permute-start.6 = (f32[40,128]{1,0:T(8,128)S(1)}, f32[40,128]{1,0:T(8,128)S(1)}, u32[]{:S(2)}, u32[]{:S(2)}) collective-permute-start(f32[40,128]{1,0:T(8,128)S(1)} %get-tuple-element.22), channel_id=1, source_target_pairs={{0,4},{1,5},{2,6},{3,7},{4,0},{5,1},{6,2},{7,3},{8,12},{9,13},{10,... | collective-permute-start | bytes 61448 | tf_op jit(solution)/shard_map/ppermute | solution.py:442
  29.3 1.3 %collective-permute-done.8 = f32[40,128]{1,0:T(8,128)S(1)} collective-permute-done((f32[40,128]{1,0:T(8,128)S(1)}, f32[40,128]{1,0:T(8,128)S(1)}, u32[]{:S(2)}, u32[]{:S(2)}) %collective-permute-start.8) | collective-permute-done | bytes 20512 | tf_op jit(solution)/shard_map/ppermute | solution.py:442
  30.6 0.7 %collective-permute-done.7 = f32[40,128]{1,0:T(8,128)S(1)} collective-permute-done((f32[40,128]{1,0:T(8,128)S(1)}, f32[40,128]{1,0:T(8,128)S(1)}, u32[]{:S(2)}, u32[]{:S(2)}) %collective-permute-start.7) | collective-permute-done | bytes 20512 | tf_op jit(solution)/shard_map/ppermute | solution.py:442
  31.3 0.0 collective-permute-done.6
  31.3 1.6 %collective-permute-start.11 = (f32[40,128]{1,0:T(8,128)S(1)}, f32[40,128]{1,0:T(8,128)S(1)}, u32[]{:S(2)}, u32[]{:S(2)}) collective-permute-start(f32[40,128]{1,0:T(8,128)S(1)} %add_add_fusion.1), channel_id=1, source_target_pairs={{0,48},{1,49},{2,50},{3,51},{4,52},{5,53},{6,54},{7,55},{8,56},{9,... | collective-permute-start | bytes 61448 | tf_op jit(solution)/shard_map/ppermute | solution.py:442
  33.0 1.7 %collective-permute-start.10 = (f32[40,128]{1,0:T(8,128)S(1)}, f32[40,128]{1,0:T(8,128)S(1)}, u32[]{:S(2)}, u32[]{:S(2)}) collective-permute-start(f32[40,128]{1,0:T(8,128)S(1)} %add_add_fusion.1), channel_id=1, source_target_pairs={{0,40},{1,41},{2,42},{3,43},{4,44},{5,45},{6,46},{7,47},{8,32},{9,... | collective-permute-start | bytes 61448 | tf_op jit(solution)/shard_map/ppermute | solution.py:442
  34.7 1.9 %collective-permute-start.9 = (f32[40,128]{1,0:T(8,128)S(1)}, f32[40,128]{1,0:T(8,128)S(1)}, u32[]{:S(2)}, u32[]{:S(2)}) collective-permute-start(f32[40,128]{1,0:T(8,128)S(1)} %add_add_fusion.1), channel_id=1, source_target_pairs={{0,16},{1,17},{2,18},{3,19},{4,20},{5,21},{6,22},{7,23},{8,24},{9,... | collective-permute-start | bytes 61448 | tf_op jit(solution)/shard_map/ppermute | solution.py:442
  36.6 0.7 %collective-permute-done.11 = f32[40,128]{1,0:T(8,128)S(1)} collective-permute-done((f32[40,128]{1,0:T(8,128)S(1)}, f32[40,128]{1,0:T(8,128)S(1)}, u32[]{:S(2)}, u32[]{:S(2)}) %collective-permute-start.11) | collective-permute-done | bytes 20512 | tf_op jit(solution)/shard_map/ppermute | solution.py:442
  37.3 2.8 %collective-permute-done.10 = f32[40,128]{1,0:T(8,128)S(1)} collective-permute-done((f32[40,128]{1,0:T(8,128)S(1)}, f32[40,128]{1,0:T(8,128)S(1)}, u32[]{:S(2)}, u32[]{:S(2)}) %collective-permute-start.10) | collective-permute-done | bytes 20512 | tf_op jit(solution)/shard_map/ppermute | solution.py:442
  40.1 0.0 collective-permute-done.9
  40.1 16.8 %all_to_all.5.moments = f32[16,40,128]{2,1,0:T(8,128)S(1)} all-to-all(f32[16,40,128]{2,1,0:T(8,128)S(1)} %broadcast_in_dim.2), channel_id=1, replica_groups=mesh['y'=4,'z'=8,'core'=2,'x'=4] {'y','x'}, dimensions={0} | all-to-all | bytes 655360 | tf_op jit(solution)/shard_map/all_to_all | solution.py:447
  56.9 0.0 copy-done
  56.9 5.0 %shard_map.63 = (f32[2,1536,128]{2,1,0:T(8,128)}, f32[2,2,32,32]{3,2,1,0:T(8,128)}) custom-call(f32[4]{0:T(128)S(1)} %copy-done, f32[16,40,128]{2,1,0:T(8,128)S(1)} %all_to_all.5.moments, bf16[24,192,256]{2,1,0:T(8,128)(2,1)S(1)} %get-tuple-element.23.basis), custom_call_target="tpu_custom_call" | custom-call | tf_op jit(solution)/shard_map/pallas_call | solution.py:25
  (4 shorter events, 0.1 us)
Async XLA Ops:
  2.1 22.6 %collective-permute-start.2 = (f32[1544,128]{1,0:T(8,128)S(1)}, f32[1544,128]{1,0:T(8,128)S(1)}, u32[]{:S(2)}, u32[]{:S(2)}) collective-permute-start(f32[1544,128]{1,0:T(8,128)S(1)} %get-tuple-element.18), channel_id=1, source_target_pairs={{0,4},{1,5},{2,6},{3,7},{4,8},{5,9},{6,10},{7,11},{8,12},{9,13},{1... | collective-permute-start | bytes 2371592 | tf_op jit(solution)/shard_map/ppermute | solution.py:431
  2.2 22.5 %collective-permute-start.3 = (f32[1288,128]{1,0:T(8,128)S(1)}, f32[1288,128]{1,0:T(8,128)S(1)}, u32[]{:S(2)}, u32[]{:S(2)}) collective-permute-start(f32[1288,128]{1,0:T(8,128)S(1)} %get-tuple-element.19), channel_id=1, source_target_pairs={{0,252},{1,253},{2,254},{3,255},{4,0},{5,1},{6,2},{7,3},{8,4},{9,5... | collective-permute-start | bytes 1978376 | tf_op jit(solution)/shard_map/ppermute | solution.py:431
  10.1 6.9 %collective-permute-start = (f32[392,128]{1,0:T(8,128)S(1)}, f32[392,128]{1,0:T(8,128)S(1)}, u32[]{:S(2)}, u32[]{:S(2)}) collective-permute-start(f32[392,128]{1,0:T(8,128)S(1)} %get-tuple-element.16), channel_id=1, source_target_pairs={{0,1},{1,2},{2,3},{3,0},{4,5},{5,6},{6,7},{7,4},{8,9},{9,10},{10,1... | collective-permute-start | bytes 602120 | tf_op jit(solution)/shard_map/ppermute | solution.py:431
  11.5 5.4 %collective-permute-start.1 = (f32[328,128]{1,0:T(8,128)S(1)}, f32[328,128]{1,0:T(8,128)S(1)}, u32[]{:S(2)}, u32[]{:S(2)}) collective-permute-start(f32[328,128]{1,0:T(8,128)S(1)} %get-tuple-element.17), channel_id=1, source_target_pairs={{0,3},{1,0},{2,1},{3,2},{4,7},{5,4},{6,5},{7,6},{8,11},{9,8},{10,9... | collective-permute-start | bytes 503816 | tf_op jit(solution)/shard_map/ppermute | solution.py:431
  16.9 7.8 %collective-permute-start.4 = (f32[264,128]{1,0:T(8,128)S(1)}, f32[264,128]{1,0:T(8,128)S(1)}, u32[]{:S(2)}, u32[]{:S(2)}) collective-permute-start(f32[264,128]{1,0:T(8,128)S(1)} %get-tuple-element.20), channel_id=1, source_target_pairs={{0,4},{1,5},{2,6},{3,7},{4,8},{5,9},{6,10},{7,11},{8,12},{9,13},{1... | collective-permute-start | bytes 405512 | tf_op jit(solution)/shard_map/ppermute | solution.py:431
  17.0 7.7 %collective-permute-start.5 = (f32[264,128]{1,0:T(8,128)S(1)}, f32[264,128]{1,0:T(8,128)S(1)}, u32[]{:S(2)}, u32[]{:S(2)}) collective-permute-start(f32[264,128]{1,0:T(8,128)S(1)} %get-tuple-element.21), channel_id=1, source_target_pairs={{0,252},{1,253},{2,254},{3,255},{4,0},{5,1},{6,2},{7,3},{8,4},{9,5... | collective-permute-start | bytes 405512 | tf_op jit(solution)/shard_map/ppermute | solution.py:431
  22.1 34.8 %copy-start = (f32[4]{0:T(128)S(1)}, f32[4]{0:T(128)}, u32[]{:S(2)}) copy-start(f32[4]{0:T(128)} %eps.3) | copy-start | bytes 52
  27.3 3.3 %collective-permute-start.8 = (f32[40,128]{1,0:T(8,128)S(1)}, f32[40,128]{1,0:T(8,128)S(1)}, u32[]{:S(2)}, u32[]{:S(2)}) collective-permute-start(f32[40,128]{1,0:T(8,128)S(1)} %get-tuple-element.22), channel_id=1, source_target_pairs={{0,12},{1,13},{2,14},{3,15},{4,8},{5,9},{6,10},{7,11},{8,4},{9,5},... | collective-permute-start | bytes 61448 | tf_op jit(solution)/shard_map/ppermute | solution.py:442
  27.4 3.9 %collective-permute-start.7 = (f32[40,128]{1,0:T(8,128)S(1)}, f32[40,128]{1,0:T(8,128)S(1)}, u32[]{:S(2)}, u32[]{:S(2)}) collective-permute-start(f32[40,128]{1,0:T(8,128)S(1)} %get-tuple-element.22), channel_id=1, source_target_pairs={{0,8},{1,9},{2,10},{3,11},{4,12},{5,13},{6,14},{7,15},{8,0},{9,1},... | collective-permute-start | bytes 61448 | tf_op jit(solution)/shard_map/ppermute | solution.py:442
  27.5 3.8 %collective-permute-start.6 = (f32[40,128]{1,0:T(8,128)S(1)}, f32[40,128]{1,0:T(8,128)S(1)}, u32[]{:S(2)}, u32[]{:S(2)}) collective-permute-start(f32[40,128]{1,0:T(8,128)S(1)} %get-tuple-element.22), channel_id=1, source_target_pairs={{0,4},{1,5},{2,6},{3,7},{4,0},{5,1},{6,2},{7,3},{8,12},{9,13},{10,... | collective-permute-start | bytes 61448 | tf_op jit(solution)/shard_map/ppermute | solution.py:442
  31.3 6.0 %collective-permute-start.11 = (f32[40,128]{1,0:T(8,128)S(1)}, f32[40,128]{1,0:T(8,128)S(1)}, u32[]{:S(2)}, u32[]{:S(2)}) collective-permute-start(f32[40,128]{1,0:T(8,128)S(1)} %add_add_fusion.1), channel_id=1, source_target_pairs={{0,48},{1,49},{2,50},{3,51},{4,52},{5,53},{6,54},{7,55},{8,56},{9,... | collective-permute-start | bytes 61448 | tf_op jit(solution)/shard_map/ppermute | solution.py:442
  33.0 7.2 %collective-permute-start.10 = (f32[40,128]{1,0:T(8,128)S(1)}, f32[40,128]{1,0:T(8,128)S(1)}, u32[]{:S(2)}, u32[]{:S(2)}) collective-permute-start(f32[40,128]{1,0:T(8,128)S(1)} %add_add_fusion.1), channel_id=1, source_target_pairs={{0,40},{1,41},{2,42},{3,43},{4,44},{5,45},{6,46},{7,47},{8,32},{9,... | collective-permute-start | bytes 61448 | tf_op jit(solution)/shard_map/ppermute | solution.py:442
  34.7 5.4 %collective-permute-start.9 = (f32[40,128]{1,0:T(8,128)S(1)}, f32[40,128]{1,0:T(8,128)S(1)}, u32[]{:S(2)}, u32[]{:S(2)}) collective-permute-start(f32[40,128]{1,0:T(8,128)S(1)} %add_add_fusion.1), channel_id=1, source_target_pairs={{0,16},{1,17},{2,18},{3,19},{4,20},{5,21},{6,22},{7,23},{8,24},{9,... | collective-permute-start | bytes 61448 | tf_op jit(solution)/shard_map/ppermute | solution.py:442

commit v6 on v5

--- a/solution.py
+++ b/solution.py
@@ -53,16 +53,23 @@
         cells = set(self.first)
         for cell in self.first:
             cells |= reach(*cell)
-        self.names = [(0, -1), (0, 1), (-1, 0), (1, 0), (-1, 2), (1, 2)]
-        self.blocks, self.diagonal = {}, {}
-        for name in self.names:
-            self.blocks[name] = sorted(q for q in cells if self.name(q[1], q[2]) == name)
-            near = {q[1:] for q in self.first if self.name(q[1], q[2]) == name}
-            self.diagonal[name] = sorted(near)
-
-    def name(self, z, x):
-        side = self.side(z, x)
-        return (side[0], 2) if side[0] and side[1] else side
+        self.edge = set()
+        for c, z, x in cells:
+            side = self.side(z, x)
+            if side[0] and side[1]:
+                self.edge.add((c, z, x - side[1] * xs))
+        cells |= self.edge
+        self.names = [
+            ("edge", -1, 0),
+            ("edge", 1, 0),
+            ("main", -1, 0),
+            ("main", 1, 0),
+            ("x", 0, -1),
+            ("x", 0, 1),
+        ]
+        near = {q[1:] for q in self.first}
+        self.blocks = {n: sorted(q for q in cells if self.name(*q) == n) for n in self.names}
+        self.diagonal = {n: sorted(q for q in near if self.row_name(*q) == n) for n in self.names}
 
     def side(self, z, x):
         return (
@@ -70,16 +77,31 @@
             -1 if x < 0 else int(x >= self.xs),
         )
 
+    def name(self, c, z, x):
+        dz, dx = self.side(z, x)
+        if dx:
+            return ("x", 0, dx)
+        if dz:
+            return ("edge" if (c, z, x) in self.edge else "main", dz, 0)
+        return None
+
+    def row_name(self, z, x):
+        dz, dx = self.side(z, x)
+        if dx:
+            return ("x", 0, dx)
+        return ("edge", dz, 0) if dz else None
+
     def own(self, name, z, x):
-        return z - name[0] * self.zs, x - name[1] % 2 * name[1] * self.xs
+        return z - name[1] * self.zs, x - name[2] * self.xs
 
     def rows(self, name, width):
-        return len(self.blocks[name]) * width + 8
-
-    def block_row(self, name, c, z, x, width):
-        return self.blocks[name].index((c, z, x)) * width
-
-    def diagonal_row(self, name, z, x, width):
+        return len(self.blocks[name]) * width + (8 if self.diagonal[name] else 0)
+
+    def block_row(self, c, z, x, width):
+        return self.blocks[self.name(c, z, x)].index((c, z, x)) * width
+
+    def diagonal_row(self, z, x, width):
+        name = self.row_name(z, x)
         return len(self.blocks[name]) * width + self.diagonal[name].index((z, x))
 
 
@@ -136,7 +158,7 @@
 def split_body(halo, width, classes, eps, material, mask, start, field, diag, *refs):
     zs, xs = halo.zs, halo.xs
     rows = 3 * zs * xs
-    messages, (start_in, material_in, mask_in, eps_in, sems) = refs[:4], refs[4:]
+    messages, (start_in, material_in, mask_in, eps_in, sems) = refs[:2], refs[2:]
     copies = [
         pltpu.make_async_copy(source, target, sems.at[i])
         for i, (source, target) in enumerate(
@@ -160,14 +182,9 @@
     places = {}
     for name, message in zip(halo.names, messages):
         for c, z, x in halo.blocks[name]:
-            row = halo.block_row(name, c, z, x, width)
+            row = halo.block_row(c, z, x, width)
             places.setdefault((c, *halo.own(name, z, x)), []).append((message, row))
-        base = len(halo.blocks[name]) * width
-        message[base : base + 8, :] = jnp.zeros((8, message.shape[1]), jnp.float32)
-        for z, x in halo.diagonal[name]:
-            row = halo.diagonal_row(name, z, x, width)
-            oz, ox = halo.own(name, z, x)
-            message[row : row + 1, :] = diag[oz, ox : ox + 1, :]
+        fill_rows(halo, name, message, width, lambda z, x: diag[z, x : x + 1, :])
     copies[3].wait()
     for z in range(zs):
         for c in range(3):
@@ -178,21 +195,36 @@
                     message[row : row + width, :] = cell
 
 
-def relay_body(halo, width, before, after, *passed):
-    received = {-1: ((0, -1), before), 1: ((0, 1), after)}
-    for name, message in zip(halo.names[4:], passed):
+def fill_rows(halo, name, message, width, row_of):
+    if halo.diagonal[name]:
         base = len(halo.blocks[name]) * width
         message[base : base + 8, :] = jnp.zeros((8, message.shape[1]), jnp.float32)
+    for z, x in halo.diagonal[name]:
+        row = halo.diagonal_row(z, x, width)
+        message[row : row + 1, :] = row_of(*halo.own(name, z, x))
+
+
+def across_body(halo, width, field, diag, before, after, *messages):
+    edges = {-1: before, 1: after}
+
+    def row_of(z, x):
+        dz = halo.side(z, x)[0]
+        if dz == 0:
+            return diag[z, x : x + 1, :]
+        row = halo.diagonal_row(z, x, width)
+        return edges[dz][row : row + 1, :]
+
+    for name, message in zip(halo.names[2:], messages):
         for c, z, x in halo.blocks[name]:
-            side, source = received[halo.side(z, x)[1]]
-            at = halo.block_row(side, c, z - name[0] * halo.zs, x, width)
-            row = halo.block_row(name, c, z, x, width)
-            message[row : row + width, :] = source[at : at + width, :]
-        for z, x in halo.diagonal[name]:
-            side, source = received[halo.side(z, x)[1]]
-            at = halo.diagonal_row(side, z - name[0] * halo.zs, x, width)
-            row = halo.diagonal_row(name, z, x, width)
-            message[row : row + 1, :] = source[at : at + 1, :]
+            row = halo.block_row(c, z, x, width)
+            z, x = halo.own(name, z, x)
+            dz = halo.side(z, x)[0]
+            if dz == 0:
+                message[row : row + width, :] = field[z, c, x]
+            else:
+                at = halo.block_row(c, z, x, width)
+                message[row : row + width, :] = edges[dz][at : at + width, :]
+        fill_rows(halo, name, message, width, row_of)
 
 
 def parts(value, count):
@@ -249,18 +281,18 @@
     lane = lax.broadcasted_iota(jnp.int32, (8, ny), 1)
 
     def diagonal(z, x):
-        name = halo.name(z, x)
-        if name == (0, 0):
+        name = halo.row_name(z, x)
+        if name is None:
             return diag[z, x : x + 1, :]
-        row = halo.diagonal_row(name, z, x, width)
+        row = halo.diagonal_row(z, x, width)
         return messages[name][row : row + 1, :]
 
     def group(at):
         def start(c, z, x):
-            name = halo.name(z, x)
-            if name == (0, 0):
+            name = halo.name(c, z, x)
+            if name is None:
                 return s0[z, c, x, pl.ds(at, 8), :]
-            row = halo.block_row(name, c, z, x, width)
+            row = halo.block_row(c, z, x, width)
             return messages[name][pl.ds(row + at, 8), :] * inside[halo.side(z, x)]
 
         def once(c, z, x):
@@ -422,7 +454,7 @@
 
 
 def moved(name, value, slabs, trans):
-    dz, dx = name[0], name[1] % 2 * name[1]
+    _, dz, dx = name
     pairs = [
         (i * trans + j, (i - dz) % slabs * trans + (j - dx) % trans)
         for i in range(slabs)
@@ -457,7 +489,7 @@
 
     s0, diag, *messages = call(
         functools.partial(split_body, halo, width, classes),
-        [field, shape(zs, xs, ny)] + [shape(halo.rows(n, width), ny) for n in halo.names[:4]],
+        [field, shape(zs, xs, ny)] + [shape(halo.rows(n, width), ny) for n in halo.names[:2]],
         [eps_table, material, pml_mask, start_block.reshape(rows, ny)],
         hbm=(0, 1, 2, 3),
         scratch=[
@@ -469,12 +501,12 @@
         ],
     )
     messages = [moved(n, m, slabs, trans) for n, m in zip(halo.names, messages)]
-    passed = call(
-        functools.partial(relay_body, halo, width),
-        [shape(halo.rows(n, width), ny) for n in halo.names[4:]],
-        messages[:2],
-    )
-    messages += [moved(n, m, slabs, trans) for n, m in zip(halo.names[4:], passed)]
+    others = call(
+        functools.partial(across_body, halo, width),
+        [shape(halo.rows(n, width), ny) for n in halo.names[2:]],
+        [s0, diag] + messages,
+    )
+    messages += [moved(n, m, slabs, trans) for n, m in zip(halo.names[2:], others)]
     (gram,) = call(functools.partial(start_gram_body, zs, xs), [shape(width, width)], [s0])
     outside = len(halo.first) - 3 * zs * xs
     basis, moments = call(

time: 62.2 us -> 62.5 us (level)
    ppermute x6, waiting for transfers between devices: 7.01 us -> 8.34 us  [moved(): return lax.ppermute(value, AXES, pairs)]
    ppermute x6, waiting for transfers between devices: 5.56 us -> 4.56 us  [total_sum(): lax.ppermute(value, AXES, [(i, i ^ m) for i in range(devices)])]
  transfers between devices with their start and end apart: 12 -> 12, of which waited for: 6 -> 7; matrix products, arithmetic and copies ran while one was open for 0% -> 0% of each run, Pallas kernels for 1% -> 1%
where the time goes in v6:
time: 62.5 us; the launch traced here: 62.3 us
  starting transfers between devices  22.4 us (36%)
  blocking collectives  16.4 us (26%)
  waiting for transfers between devices  12.9 us (21%)
  Pallas kernels  9.69 us (16%)
  between operations  0.86 us (1%)
    all_to_all x1, blocking collectives, total_sum(): return lax.all_to_all(copies, ('y', 'x'), 0, 0, tiled=True)  16.4 us
    ppermute x6, starting transfers between devices, moved(): return lax.ppermute(value, AXES, pairs)  15.2 us
    pallas_call x5, Pallas kernels, call(): pl.pallas_call(body, out_shape=out_shape, in_specs=specs, out_specs=outs,...  9.69 us
    ppermute x6, waiting for transfers between devices, moved(): return lax.ppermute(value, AXES, pairs)  8.34 us
    ppermute x6, starting transfers between devices, total_sum(): lax.ppermute(value, AXES, [(i, i ^ m) for i in range(devices)])  7.18 us
    ppermute x6, waiting for transfers between devices, total_sum(): lax.ppermute(value, AXES, [(i, i ^ m) for i in range(devices)])  4.56 us
  transfers between devices with their start and end apart: 12, of which 7 were waited for; matrix products, arithmetic and copies ran while one was open for 0% of the time, Pallas kernels for 1%

profile of v6, /device:TPU:2, one launch (start us, length us, event | category | flops | bytes accessed | tf_op | source)
XLA Modules:
  0.0 62.3 jit_solution(15537448743546297008)
XLA Ops:
  0.6 1.5 %shard_map.59 = (f32[2,3,8,32,128]{4,3,2,1,0:T(8,128)S(1)}, f32[2,8,128]{2,1,0:T(8,128)S(1)}, f32[264,128]{1,0:T(8,128)S(1)}, f32[264,128]{1,0:T(8,128)S(1)}) custom-call(f32[4]{0:T(128)} %eps.3, s32[2,8,128]{2,1,0:T(8,128)} %material.1, s32[2,8,128]{2,1,0:T(8,128)} %mask.1, f32[1536,128]{1,0:T(8,128)} %bitcast.2), custom_call_target="tpu_custom_call" | custom-call | tf_op jit(solution)/shard_map/pallas_call | solution.py:25
  2.1 0.1 collective-permute-start
  2.2 7.8 %collective-permute-start.1 = (f32[264,128]{1,0:T(8,128)S(1)}, f32[264,128]{1,0:T(8,128)S(1)}, u32[]{:S(2)}, u32[]{:S(2)}) collective-permute-start(f32[264,128]{1,0:T(8,128)S(1)} %get-tuple-element.17), channel_id=1, source_target_pairs={{0,252},{1,253},{2,254},{3,255},{4,0},{5,1},{6,2},{7,3},{8,4},{9,5... | collective-permute-start | bytes 405512 | tf_op jit(solution)/shard_map/ppermute | solution.py:463
  10.0 2.6 %collective-permute-done.before.refs_0_ = f32[264,128]{1,0:T(8,128)S(1)} collective-permute-done((f32[264,128]{1,0:T(8,128)S(1)}, f32[264,128]{1,0:T(8,128)S(1)}, u32[]{:S(2)}, u32[]{:S(2)}) %collective-permute-start) | collective-permute-done | bytes 135200 | tf_op jit(solution)/shard_map/ppermute | solution.py:463
  12.6 0.0 collective-permute-done.1.after.refs_1_
  12.6 0.1 shard_map.61
  12.7 0.1 collective-permute-start.2
  12.8 5.2 %collective-permute-start.3 = (f32[1024,128]{1,0:T(8,128)S(1)}, f32[1024,128]{1,0:T(8,128)S(1)}, u32[]{:S(2)}, u32[]{:S(2)}) collective-permute-start(f32[1024,128]{1,0:T(8,128)S(1)} %get-tuple-element.19), channel_id=1, source_target_pairs={{0,252},{1,253},{2,254},{3,255},{4,0},{5,1},{6,2},{7,3},{8,4},{9,5... | collective-permute-start | bytes 1572872 | tf_op jit(solution)/shard_map/ppermute | solution.py:463
  18.1 1.5 %collective-permute-start.4 = (f32[648,128]{1,0:T(8,128)S(1)}, f32[648,128]{1,0:T(8,128)S(1)}, u32[]{:S(2)}, u32[]{:S(2)}) collective-permute-start(f32[648,128]{1,0:T(8,128)S(1)} %get-tuple-element.20), channel_id=1, source_target_pairs={{0,1},{1,2},{2,3},{3,0},{4,5},{5,6},{6,7},{7,4},{8,9},{9,10},{10,1... | collective-permute-start | bytes 995336 | tf_op jit(solution)/shard_map/ppermute | solution.py:463
  19.5 0.0 copy-start
  19.5 0.5 collective-permute-start.5
  20.1 0.5 shard_map.60.gram
  20.6 5.7 %collective-permute-done.5.refs_5_ = f32[584,128]{1,0:T(8,128)S(1)} collective-permute-done((f32[584,128]{1,0:T(8,128)S(1)}, f32[584,128]{1,0:T(8,128)S(1)}, u32[]{:S(2)}, u32[]{:S(2)}) %collective-permute-start.5) | collective-permute-done | bytes 299040 | tf_op jit(solution)/shard_map/ppermute | solution.py:463
  26.3 0.0 collective-permute-done.4.refs_4_
  26.3 0.0 collective-permute-done.3.refs_3_
  26.3 0.0 collective-permute-done.2.refs_2_
  26.3 2.6 %shard_map.62 = (bf16[24,192,256]{2,1,0:T(8,128)(2,1)S(1)}, f32[40,128]{1,0:T(8,128)S(1)}) custom-call(f32[2,3,8,32,128]{4,3,2,1,0:T(8,128)S(1)} %get-tuple-element.14.s0.field, f32[2,8,128]{2,1,0:T(8,128)S(1)} %get-tuple-element.15.diag, f32[32,32]{1,0:T(8,128)S(1)} %shard_map.60.gram, f32[264,128]{1,0:T(8,128)S(1)} %collective-permute-done.before.refs_0_, ...), custom_call_target="tpu_custom_call" | custom-call | tf_op jit(solution)/shard_map/pallas_call | solution.py:25
  28.9 0.1 collective-permute-start.8
  29.0 0.1 collective-permute-start.7
  29.1 1.7 %collective-permute-start.6 = (f32[40,128]{1,0:T(8,128)S(1)}, f32[40,128]{1,0:T(8,128)S(1)}, u32[]{:S(2)}, u32[]{:S(2)}) collective-permute-start(f32[40,128]{1,0:T(8,128)S(1)} %get-tuple-element.22), channel_id=1, source_target_pairs={{0,4},{1,5},{2,6},{3,7},{4,0},{5,1},{6,2},{7,3},{8,12},{9,13},{10,... | collective-permute-start | bytes 61448 | tf_op jit(solution)/shard_map/ppermute | solution.py:474
  30.8 1.3 %collective-permute-done.8 = f32[40,128]{1,0:T(8,128)S(1)} collective-permute-done((f32[40,128]{1,0:T(8,128)S(1)}, f32[40,128]{1,0:T(8,128)S(1)}, u32[]{:S(2)}, u32[]{:S(2)}) %collective-permute-start.8) | collective-permute-done | bytes 20512 | tf_op jit(solution)/shard_map/ppermute | solution.py:474
  32.2 0.7 %collective-permute-done.7 = f32[40,128]{1,0:T(8,128)S(1)} collective-permute-done((f32[40,128]{1,0:T(8,128)S(1)}, f32[40,128]{1,0:T(8,128)S(1)}, u32[]{:S(2)}, u32[]{:S(2)}) %collective-permute-start.7) | collective-permute-done | bytes 20512 | tf_op jit(solution)/shard_map/ppermute | solution.py:474
  32.9 0.0 collective-permute-done.6
  32.9 0.2 collective-permute-start.11
  33.1 2.8 %collective-permute-start.10 = (f32[40,128]{1,0:T(8,128)S(1)}, f32[40,128]{1,0:T(8,128)S(1)}, u32[]{:S(2)}, u32[]{:S(2)}) collective-permute-start(f32[40,128]{1,0:T(8,128)S(1)} %add_add_fusion.1), channel_id=1, source_target_pairs={{0,40},{1,41},{2,42},{3,43},{4,44},{5,45},{6,46},{7,47},{8,32},{9,... | collective-permute-start | bytes 61448 | tf_op jit(solution)/shard_map/ppermute | solution.py:474
  35.9 2.2 %collective-permute-start.9 = (f32[40,128]{1,0:T(8,128)S(1)}, f32[40,128]{1,0:T(8,128)S(1)}, u32[]{:S(2)}, u32[]{:S(2)}) collective-permute-start(f32[40,128]{1,0:T(8,128)S(1)} %add_add_fusion.1), channel_id=1, source_target_pairs={{0,16},{1,17},{2,18},{3,19},{4,20},{5,21},{6,22},{7,23},{8,24},{9,... | collective-permute-start | bytes 61448 | tf_op jit(solution)/shard_map/ppermute | solution.py:474
  38.1 0.7 %collective-permute-done.11 = f32[40,128]{1,0:T(8,128)S(1)} collective-permute-done((f32[40,128]{1,0:T(8,128)S(1)}, f32[40,128]{1,0:T(8,128)S(1)}, u32[]{:S(2)}, u32[]{:S(2)}) %collective-permute-start.11) | collective-permute-done | bytes 20512 | tf_op jit(solution)/shard_map/ppermute | solution.py:474
  38.8 1.0 %collective-permute-done.10 = f32[40,128]{1,0:T(8,128)S(1)} collective-permute-done((f32[40,128]{1,0:T(8,128)S(1)}, f32[40,128]{1,0:T(8,128)S(1)}, u32[]{:S(2)}, u32[]{:S(2)}) %collective-permute-start.10) | collective-permute-done | bytes 20512 | tf_op jit(solution)/shard_map/ppermute | solution.py:474
  39.9 0.8 %collective-permute-done.9 = f32[40,128]{1,0:T(8,128)S(1)} collective-permute-done((f32[40,128]{1,0:T(8,128)S(1)}, f32[40,128]{1,0:T(8,128)S(1)}, u32[]{:S(2)}, u32[]{:S(2)}) %collective-permute-start.9) | collective-permute-done | bytes 20512 | tf_op jit(solution)/shard_map/ppermute | solution.py:474
  40.7 16.4 %all_to_all.5.moments = f32[16,40,128]{2,1,0:T(8,128)S(1)} all-to-all(f32[16,40,128]{2,1,0:T(8,128)S(1)} %broadcast_in_dim.2), channel_id=1, replica_groups=mesh['y'=4,'z'=8,'core'=2,'x'=4] {'y','x'}, dimensions={0} | all-to-all | bytes 655360 | tf_op jit(solution)/shard_map/all_to_all | solution.py:479
  57.1 0.0 copy-done
  57.1 5.0 %shard_map.63 = (f32[2,1536,128]{2,1,0:T(8,128)}, f32[2,2,32,32]{3,2,1,0:T(8,128)}) custom-call(f32[4]{0:T(128)S(1)} %copy-done, f32[16,40,128]{2,1,0:T(8,128)S(1)} %all_to_all.5.moments, bf16[24,192,256]{2,1,0:T(8,128)(2,1)S(1)} %get-tuple-element.23.basis), custom_call_target="tpu_custom_call" | custom-call | tf_op jit(solution)/shard_map/pallas_call | solution.py:25
  (3 shorter events, 0.0 us)
Async XLA Ops:
  2.1 10.5 %collective-permute-start = (f32[264,128]{1,0:T(8,128)S(1)}, f32[264,128]{1,0:T(8,128)S(1)}, u32[]{:S(2)}, u32[]{:S(2)}) collective-permute-start(f32[264,128]{1,0:T(8,128)S(1)} %get-tuple-element.16), channel_id=1, source_target_pairs={{0,4},{1,5},{2,6},{3,7},{4,8},{5,9},{6,10},{7,11},{8,12},{9,13},{1... | collective-permute-start | bytes 405512 | tf_op jit(solution)/shard_map/ppermute | solution.py:463
  2.2 10.4 %collective-permute-start.1 = (f32[264,128]{1,0:T(8,128)S(1)}, f32[264,128]{1,0:T(8,128)S(1)}, u32[]{:S(2)}, u32[]{:S(2)}) collective-permute-start(f32[264,128]{1,0:T(8,128)S(1)} %get-tuple-element.17), channel_id=1, source_target_pairs={{0,252},{1,253},{2,254},{3,255},{4,0},{5,1},{6,2},{7,3},{8,4},{9,5... | collective-permute-start | bytes 405512 | tf_op jit(solution)/shard_map/ppermute | solution.py:463
  12.7 13.6 %collective-permute-start.2 = (f32[1280,128]{1,0:T(8,128)S(1)}, f32[1280,128]{1,0:T(8,128)S(1)}, u32[]{:S(2)}, u32[]{:S(2)}) collective-permute-start(f32[1280,128]{1,0:T(8,128)S(1)} %get-tuple-element.18), channel_id=1, source_target_pairs={{0,4},{1,5},{2,6},{3,7},{4,8},{5,9},{6,10},{7,11},{8,12},{9,13},{1... | collective-permute-start | bytes 1966088 | tf_op jit(solution)/shard_map/ppermute | solution.py:463
  12.8 13.5 %collective-permute-start.3 = (f32[1024,128]{1,0:T(8,128)S(1)}, f32[1024,128]{1,0:T(8,128)S(1)}, u32[]{:S(2)}, u32[]{:S(2)}) collective-permute-start(f32[1024,128]{1,0:T(8,128)S(1)} %get-tuple-element.19), channel_id=1, source_target_pairs={{0,252},{1,253},{2,254},{3,255},{4,0},{5,1},{6,2},{7,3},{8,4},{9,5... | collective-permute-start | bytes 1572872 | tf_op jit(solution)/shard_map/ppermute | solution.py:463
  18.1 8.3 %collective-permute-start.4 = (f32[648,128]{1,0:T(8,128)S(1)}, f32[648,128]{1,0:T(8,128)S(1)}, u32[]{:S(2)}, u32[]{:S(2)}) collective-permute-start(f32[648,128]{1,0:T(8,128)S(1)} %get-tuple-element.20), channel_id=1, source_target_pairs={{0,1},{1,2},{2,3},{3,0},{4,5},{5,6},{6,7},{7,4},{8,9},{9,10},{10,1... | collective-permute-start | bytes 995336 | tf_op jit(solution)/shard_map/ppermute | solution.py:463
  19.5 37.6 %copy-start = (f32[4]{0:T(128)S(1)}, f32[4]{0:T(128)}, u32[]{:S(2)}) copy-start(f32[4]{0:T(128)} %eps.3) | copy-start | bytes 52
  19.5 6.8 %collective-permute-start.5 = (f32[584,128]{1,0:T(8,128)S(1)}, f32[584,128]{1,0:T(8,128)S(1)}, u32[]{:S(2)}, u32[]{:S(2)}) collective-permute-start(f32[584,128]{1,0:T(8,128)S(1)} %get-tuple-element.21), channel_id=1, source_target_pairs={{0,3},{1,0},{2,1},{3,2},{4,7},{5,4},{6,5},{7,6},{8,11},{9,8},{10,9... | collective-permute-start | bytes 897032 | tf_op jit(solution)/shard_map/ppermute | solution.py:463
  28.9 3.3 %collective-permute-start.8 = (f32[40,128]{1,0:T(8,128)S(1)}, f32[40,128]{1,0:T(8,128)S(1)}, u32[]{:S(2)}, u32[]{:S(2)}) collective-permute-start(f32[40,128]{1,0:T(8,128)S(1)} %get-tuple-element.22), channel_id=1, source_target_pairs={{0,12},{1,13},{2,14},{3,15},{4,8},{5,9},{6,10},{7,11},{8,4},{9,5},... | collective-permute-start | bytes 61448 | tf_op jit(solution)/shard_map/ppermute | solution.py:474
  29.0 3.9 %collective-permute-start.7 = (f32[40,128]{1,0:T(8,128)S(1)}, f32[40,128]{1,0:T(8,128)S(1)}, u32[]{:S(2)}, u32[]{:S(2)}) collective-permute-start(f32[40,128]{1,0:T(8,128)S(1)} %get-tuple-element.22), channel_id=1, source_target_pairs={{0,8},{1,9},{2,10},{3,11},{4,12},{5,13},{6,14},{7,15},{8,0},{9,1},... | collective-permute-start | bytes 61448 | tf_op jit(solution)/shard_map/ppermute | solution.py:474
  29.1 3.8 %collective-permute-start.6 = (f32[40,128]{1,0:T(8,128)S(1)}, f32[40,128]{1,0:T(8,128)S(1)}, u32[]{:S(2)}, u32[]{:S(2)}) collective-permute-start(f32[40,128]{1,0:T(8,128)S(1)} %get-tuple-element.22), channel_id=1, source_target_pairs={{0,4},{1,5},{2,6},{3,7},{4,0},{5,1},{6,2},{7,3},{8,12},{9,13},{10,... | collective-permute-start | bytes 61448 | tf_op jit(solution)/shard_map/ppermute | solution.py:474
  32.9 6.0 %collective-permute-start.11 = (f32[40,128]{1,0:T(8,128)S(1)}, f32[40,128]{1,0:T(8,128)S(1)}, u32[]{:S(2)}, u32[]{:S(2)}) collective-permute-start(f32[40,128]{1,0:T(8,128)S(1)} %add_add_fusion.1), channel_id=1, source_target_pairs={{0,48},{1,49},{2,50},{3,51},{4,52},{5,53},{6,54},{7,55},{8,56},{9,... | collective-permute-start | bytes 61448 | tf_op jit(solution)/shard_map/ppermute | solution.py:474
  33.1 6.8 %collective-permute-start.10 = (f32[40,128]{1,0:T(8,128)S(1)}, f32[40,128]{1,0:T(8,128)S(1)}, u32[]{:S(2)}, u32[]{:S(2)}) collective-permute-start(f32[40,128]{1,0:T(8,128)S(1)} %add_add_fusion.1), channel_id=1, source_target_pairs={{0,40},{1,41},{2,42},{3,43},{4,44},{5,45},{6,46},{7,47},{8,32},{9,... | collective-permute-start | bytes 61448 | tf_op jit(solution)/shard_map/ppermute | solution.py:474
  35.9 4.7 %collective-permute-start.9 = (f32[40,128]{1,0:T(8,128)S(1)}, f32[40,128]{1,0:T(8,128)S(1)}, u32[]{:S(2)}, u32[]{:S(2)}) collective-permute-start(f32[40,128]{1,0:T(8,128)S(1)} %add_add_fusion.1), channel_id=1, source_target_pairs={{0,16},{1,17},{2,18},{3,19},{4,20},{5,21},{6,22},{7,23},{8,24},{9,... | collective-permute-start | bytes 61448 | tf_op jit(solution)/shard_map/ppermute | solution.py:474

commit v7 on v5

--- a/solution.py
+++ b/solution.py
@@ -137,11 +137,13 @@
     zs, xs = halo.zs, halo.xs
     rows = 3 * zs * xs
     messages, (start_in, material_in, mask_in, eps_in, sems) = refs[:4], refs[4:]
+    pairs = [(eps, eps_in), (material, material_in), (mask, mask_in)]
+    for g in range(0, width, 8):
+        part = pl.ds(g * rows, 8 * rows)
+        pairs.append((start.at[part], start_in.at[part]))
     copies = [
         pltpu.make_async_copy(source, target, sems.at[i])
-        for i, (source, target) in enumerate(
-            [(eps, eps_in), (material, material_in), (mask, mask_in), (start, start_in)]
-        )
+        for i, (source, target) in enumerate(pairs)
     ]
     for copy in copies:
         copy.start()
@@ -168,14 +170,16 @@
             row = halo.diagonal_row(name, z, x, width)
             oz, ox = halo.own(name, z, x)
             message[row : row + 1, :] = diag[oz, ox : ox + 1, :]
-    copies[3].wait()
-    for z in range(zs):
-        for c in range(3):
-            for x in range(xs):
-                cell = start_in[pl.ds((c * zs + z) * xs + x, width, stride=rows), :]
-                field[z, c, x] = cell
-                for message, row in places.get((c, z, x), ()):
-                    message[row : row + width, :] = cell
+    for g in range(0, width, 8):
+        copies[3 + g // 8].wait()
+        for z in range(zs):
+            for c in range(3):
+                for x in range(xs):
+                    at = g * rows + (c * zs + z) * xs + x
+                    cell = start_in[pl.ds(at, 8, stride=rows), :]
+                    field[z, c, x, g : g + 8] = cell
+                    for message, row in places.get((c, z, x), ()):
+                        message[row + g : row + g + 8, :] = cell
 
 
 def relay_body(halo, width, before, after, *passed):
@@ -372,38 +376,41 @@
         total = total + eps[level]
     shift = total / classes + CURL_CENTRE
     m = []
-    summed = moments[0]
-    for i in range(1, moments.shape[0]):
-        summed = summed + moments[i]
     for k in range(5):
-        rows = summed[8 * k : 8 * k + 8, :] * (1.0 / entries)
+        rows = moments[8 * k : 8 * k + 8, :] * (1.0 / entries)
         m.append(jnp.concatenate([rows[:, w * j : w * j + w] for j in range(w // 8)], axis=0))
     gram = jnp.concatenate(
         [jnp.concatenate([m[i + j] for j in range(3)], axis=1) for i in range(3)], axis=0
     )
     rows = 3 * zs * xs
 
+    flat = staged.reshape(2, w * rows, ny)
+
     def combine(block, mix, depth):
+        found = []
         for i, (z, c, x) in enumerate(cell_pairs(zs, xs)):
             terms = product(mix, basis[i, :depth], 0)
             value = terms[:w] + terms[w : 2 * w] + terms[2 * w :]
             for k in range(2):
                 at = (c * zs + z) * xs + x + k
-                staged[block, pl.ds(at, w, stride=rows), :] = value[:, k * ny : (k + 1) * ny]
-        copy = pltpu.make_async_copy(staged.at[block], out.at[block], sems.at[block])
-        copy.start()
-        return copy
+                flat[block, pl.ds(at, w, stride=rows), :] = value[:, k * ny : (k + 1) * ny]
+            if x == xs - 2:
+                plane = c * zs + z
+                source, target = staged.at[block, :, plane], out.at[block, :, plane]
+                found.append(pltpu.make_async_copy(source, target, sems.at[block, plane]))
+                found[-1].start()
+        return found
 
     steps = factor(gram, 3 * w, (w // 4, 3 * w // 8))
     upper, inverse = next(steps)
     mix = [jnp.concatenate([p, p], axis=1) for p in parts(inverse[w:, : 2 * w], 3)]
-    copies = [combine(0, jnp.concatenate(mix, axis=0), 4 * w)]
+    copies = combine(0, jnp.concatenate(mix, axis=0), 4 * w)
     upper, inverse = next(steps)
     mix = [
         jnp.concatenate([p[:, : 2 * w], p[:, : 2 * w], p[:, 2 * w :], p[:, 2 * w :]], axis=1)
         for p in parts(inverse[2 * w :], 3)
     ]
-    copies.append(combine(1, jnp.concatenate(mix, axis=0), 6 * w))
+    copies += combine(1, jnp.concatenate(mix, axis=0), 6 * w)
     identity = jnp.where(
         lax.broadcasted_iota(jnp.int32, (w, w), 0) == lax.broadcasted_iota(jnp.int32, (w, w), 1),
         shift,
@@ -432,19 +439,18 @@
 
 
 def total_sum(value, deep, trans, devices):
-    core, near = trans, 2 * trans
-    rounds = [(core, near, core ^ near)]
-    if deep == 8:
-        middle, far = 4 * trans, 8 * trans
-        rounds.append((middle, far ^ near, far ^ middle))
+    count = devices // (2 * deep)
+    copies = jnp.broadcast_to(value[None], (count, *value.shape))
+    value = lax.all_to_all(copies, ("y", "x"), 0, 0, tiled=True).sum(0)
+    core, near, middle, far = trans, 2 * trans, 4 * trans, 8 * trans
+    rounds = [(middle, far ^ near, far ^ middle)] if deep == 8 else []
+    rounds.append((core, near, core ^ near))
     for masks in rounds:
         one, two, three = (
             lax.ppermute(value, AXES, [(i, i ^ m) for i in range(devices)]) for m in masks
         )
         value = (value + one) + (two + three)
-    count = devices // (2 * deep)
-    copies = jnp.broadcast_to(value[None], (count, *value.shape))
-    return lax.all_to_all(copies, ("y", "x"), 0, 0, tiled=True)
+    return value
 
 
 def per_device(slabs, deep, trans, start_block, material, pml_mask, eps_table):
@@ -465,7 +471,7 @@
             pltpu.VMEM((zs, xs, ny), jnp.int32),
             pltpu.VMEM((zs, xs, ny), jnp.int32),
             pltpu.SMEM((classes,), jnp.float32),
-            pltpu.SemaphoreType.DMA((4,)),
+            pltpu.SemaphoreType.DMA((3 + width // 8,)),
         ],
     )
     messages = [moved(n, m, slabs, trans) for n, m in zip(halo.names, messages)]
@@ -493,11 +499,14 @@
     moments = total_sum(moments, deep, trans, slabs * trans)
     blocks, couplings = call(
         functools.partial(last_body, zs, xs, width, ny, classes, entries),
-        [shape(2, rows, ny), shape(2, 2, width, width)],
+        [shape(2, width, 3 * zs, xs, ny), shape(2, 2, width, width)],
         [eps_table, moments, basis],
         smem=(0,),
         hbm_out=(0,),
-        scratch=[pltpu.VMEM((2, rows, ny), jnp.float32), pltpu.SemaphoreType.DMA((2,))],
+        scratch=[
+            pltpu.VMEM((2, width, 3 * zs, xs, ny), jnp.float32),
+            pltpu.SemaphoreType.DMA((2, 3 * zs)),
+        ],
     )
     return blocks.reshape(2, width, 3, zs, xs, ny), couplings
 

time: 62.2 us -> 59.3 us (0.953)
  blocking collectives: 16.8 us -> 12.3 us
  waiting for transfers between devices: 12.6 us -> 15.2 us
  starting transfers between devices: 22.2 us -> 21.3 us
    all_to_all x1, blocking collectives: 16.8 us -> 12.3 us  [total_sum(): value = lax.all_to_all(copies, ('y', 'x'), 0, 0, tiled=True).sum(0)]
    ppermute x6, waiting for transfers between devices: 5.56 us -> 8.22 us  [total_sum(): lax.ppermute(value, AXES, [(i, i ^ m) for i in range(devices)])]
    ppermute x6, starting transfers between devices: 7.18 us -> 6.2 us  [total_sum(): lax.ppermute(value, AXES, [(i, i ^ m) for i in range(devices)])]
where the time goes in v7:
time: 59.3 us; the launch traced here: 59.1 us
  starting transfers between devices  21.3 us (36%)
  waiting for transfers between devices  15.2 us (26%)
  blocking collectives  12.3 us (21%)
  Pallas kernels  9.46 us (16%)
  between operations  0.87 us (1%)
    ppermute x6, starting transfers between devices, moved(): return lax.ppermute(value, AXES, pairs)  15.1 us
    all_to_all x1, blocking collectives, total_sum(): value = lax.all_to_all(copies, ('y', 'x'), 0, 0, tiled=True).sum(0)  12.3 us
    pallas_call x5, Pallas kernels, call(): pl.pallas_call(body, out_shape=out_shape, in_specs=specs, out_specs=outs,...  9.46 us
    ppermute x6, waiting for transfers between devices, total_sum(): lax.ppermute(value, AXES, [(i, i ^ m) for i in range(devices)])  8.22 us
    ppermute x6, waiting for transfers between devices, moved(): return lax.ppermute(value, AXES, pairs)  6.98 us
    ppermute x6, starting transfers between devices, total_sum(): lax.ppermute(value, AXES, [(i, i ^ m) for i in range(devices)])  6.2 us
  transfers between devices with their start and end apart: 12, of which 6 were waited for; matrix products, arithmetic and copies ran while one was open for 0% of the time, Pallas kernels for 1%

profile of v7, /device:TPU:2, one launch (start us, length us, event | category | flops | bytes accessed | tf_op | source)
XLA Modules:
  0.0 59.1 jit_solution(4846279224933203257)
XLA Ops:
  0.6 1.4 %shard_map.59 = (f32[2,3,8,32,128]{4,3,2,1,0:T(8,128)S(1)}, f32[2,8,128]{2,1,0:T(8,128)S(1)}, f32[392,128]{1,0:T(8,128)S(1)}, f32[328,128]{1,0:T(8,128)S(1)}, f3...) custom-call(f32[4]{0:T(128)} %eps.3, s32[2,8,128]{2,1,0:T(8,128)} %material.1, s32[2,8,128]{2,1,0:T(8,128)} %mask.1, ...), custom_call_target="tpu_custom_call" | custom-call | tf_op jit(solution)/shard_map/pallas_call | solution.py:25
  2.0 0.1 collective-permute-start.2
  2.1 7.8 %collective-permute-start.3 = (f32[1288,128]{1,0:T(8,128)S(1)}, f32[1288,128]{1,0:T(8,128)S(1)}, u32[]{:S(2)}, u32[]{:S(2)}) collective-permute-start(f32[1288,128]{1,0:T(8,128)S(1)} %get-tuple-element.19), channel_id=1, source_target_pairs={{0,252},{1,253},{2,254},{3,255},{4,0},{5,1},{6,2},{7,3},{8,4},{9,5... | collective-permute-start | bytes 1978376 | tf_op jit(solution)/shard_map/ppermute | solution.py:438
  9.9 1.5 %collective-permute-start = (f32[392,128]{1,0:T(8,128)S(1)}, f32[392,128]{1,0:T(8,128)S(1)}, u32[]{:S(2)}, u32[]{:S(2)}) collective-permute-start(f32[392,128]{1,0:T(8,128)S(1)} %get-tuple-element.16), channel_id=1, source_target_pairs={{0,1},{1,2},{2,3},{3,0},{4,5},{5,6},{6,7},{7,4},{8,9},{9,10},{10,1... | collective-permute-start | bytes 602120 | tf_op jit(solution)/shard_map/ppermute | solution.py:438
  11.4 0.5 collective-permute-start.1
  12.0 4.8 %collective-permute-done.1.after.refs_1_ = f32[328,128]{1,0:T(8,128)S(1)} collective-permute-done((f32[328,128]{1,0:T(8,128)S(1)}, f32[328,128]{1,0:T(8,128)S(1)}, u32[]{:S(2)}, u32[]{:S(2)}) %collective-permute-start.1) | collective-permute-done | bytes 167968 | tf_op jit(solution)/shard_map/ppermute | solution.py:438
  16.8 0.0 collective-permute-done.before.refs_0_
  16.8 0.1 collective-permute-start.4
  16.9 5.1 %collective-permute-start.5 = (f32[264,128]{1,0:T(8,128)S(1)}, f32[264,128]{1,0:T(8,128)S(1)}, u32[]{:S(2)}, u32[]{:S(2)}) collective-permute-start(f32[264,128]{1,0:T(8,128)S(1)} %get-tuple-element.21), channel_id=1, source_target_pairs={{0,252},{1,253},{2,254},{3,255},{4,0},{5,1},{6,2},{7,3},{8,4},{9,5... | collective-permute-start | bytes 405512 | tf_op jit(solution)/shard_map/ppermute | solution.py:438
  22.0 0.5 shard_map.60.gram
  22.5 0.0 copy-start
  22.5 2.1 %collective-permute-done.4.refs_4_ = f32[264,128]{1,0:T(8,128)S(1)} collective-permute-done((f32[264,128]{1,0:T(8,128)S(1)}, f32[264,128]{1,0:T(8,128)S(1)}, u32[]{:S(2)}, u32[]{:S(2)}) %collective-permute-start.4) | collective-permute-done | bytes 135200 | tf_op jit(solution)/shard_map/ppermute | solution.py:438
  24.7 0.0 collective-permute-done.5.refs_5_
  24.7 0.0 collective-permute-done.3.refs_3_
  24.7 0.0 collective-permute-done.2.refs_2_
  24.7 2.6 %shard_map.62 = (bf16[24,192,256]{2,1,0:T(8,128)(2,1)S(1)}, f32[40,128]{1,0:T(8,128)S(1)}) custom-call(f32[2,3,8,32,128]{4,3,2,1,0:T(8,128)S(1)} %get-tuple-element.14.s0, f32[2,8,128]{2,1,0:T(8,128)S(1)} %get-tuple-element.15.diag, f32[32,32]{1,0:T(8,128)S(1)} %shard_map.60.gram, f32[392,128]{1,0:T(8,128)S(1)} %collective-permute-done.before.refs_0_, ...), custom_call_target="tpu_custom_call" | custom-call | tf_op jit(solution)/shard_map/pallas_call | solution.py:25
  27.3 12.3 %all_to_all.5 = f32[16,40,128]{2,1,0:T(8,128)S(1)} all-to-all(f32[16,40,128]{2,1,0:T(8,128)S(1)} %broadcast_in_dim.2), channel_id=1, replica_groups=mesh['y'=4,'z'=8,'core'=2,'x'=4] {'y','x'}, dimensions={0} | all-to-all | bytes 655360 | tf_op jit(solution)/shard_map/all_to_all | solution.py:444
  39.5 1.3 %collective-permute-start.8 = (f32[40,128]{1,0:T(8,128)S(1)}, f32[40,128]{1,0:T(8,128)S(1)}, u32[]{:S(2)}, u32[]{:S(2)}) collective-permute-start(f32[40,128]{1,0:T(8,128)S(1)} %reduce_sum.9), channel_id=1, source_target_pairs={{0,48},{1,49},{2,50},{3,51},{4,52},{5,53},{6,54},{7,55},{8,56},{9,... | collective-permute-start | bytes 61448 | tf_op jit(solution)/shard_map/ppermute | solution.py:450
  40.8 0.9 %collective-permute-start.7 = (f32[40,128]{1,0:T(8,128)S(1)}, f32[40,128]{1,0:T(8,128)S(1)}, u32[]{:S(2)}, u32[]{:S(2)}) collective-permute-start(f32[40,128]{1,0:T(8,128)S(1)} %reduce_sum.9), channel_id=1, source_target_pairs={{0,40},{1,41},{2,42},{3,43},{4,44},{5,45},{6,46},{7,47},{8,32},{9,... | collective-permute-start | bytes 61448 | tf_op jit(solution)/shard_map/ppermute | solution.py:450
  41.7 1.3 %collective-permute-start.6 = (f32[40,128]{1,0:T(8,128)S(1)}, f32[40,128]{1,0:T(8,128)S(1)}, u32[]{:S(2)}, u32[]{:S(2)}) collective-permute-start(f32[40,128]{1,0:T(8,128)S(1)} %reduce_sum.9), channel_id=1, source_target_pairs={{0,16},{1,17},{2,18},{3,19},{4,20},{5,21},{6,22},{7,23},{8,24},{9,... | collective-permute-start | bytes 61448 | tf_op jit(solution)/shard_map/ppermute | solution.py:450
  43.0 2.5 %collective-permute-done.8 = f32[40,128]{1,0:T(8,128)S(1)} collective-permute-done((f32[40,128]{1,0:T(8,128)S(1)}, f32[40,128]{1,0:T(8,128)S(1)}, u32[]{:S(2)}, u32[]{:S(2)}) %collective-permute-start.8) | collective-permute-done | bytes 20512 | tf_op jit(solution)/shard_map/ppermute | solution.py:450
  45.5 2.2 %collective-permute-done.7 = f32[40,128]{1,0:T(8,128)S(1)} collective-permute-done((f32[40,128]{1,0:T(8,128)S(1)}, f32[40,128]{1,0:T(8,128)S(1)}, u32[]{:S(2)}, u32[]{:S(2)}) %collective-permute-start.7) | collective-permute-done | bytes 20512 | tf_op jit(solution)/shard_map/ppermute | solution.py:450
  47.7 0.0 collective-permute-done.6
  47.7 2.5 %collective-permute-start.11 = (f32[40,128]{1,0:T(8,128)S(1)}, f32[40,128]{1,0:T(8,128)S(1)}, u32[]{:S(2)}, u32[]{:S(2)}) collective-permute-start(f32[40,128]{1,0:T(8,128)S(1)} %add_add_fusion.1), channel_id=1, source_target_pairs={{0,12},{1,13},{2,14},{3,15},{4,8},{5,9},{6,10},{7,11},{8,4},{9,5},... | collective-permute-start | bytes 61448 | tf_op jit(solution)/shard_map/ppermute | solution.py:450
  50.2 0.0 collective-permute-start.10
  50.2 0.2 collective-permute-start.9
  50.4 1.3 %collective-permute-done.11 = f32[40,128]{1,0:T(8,128)S(1)} collective-permute-done((f32[40,128]{1,0:T(8,128)S(1)}, f32[40,128]{1,0:T(8,128)S(1)}, u32[]{:S(2)}, u32[]{:S(2)}) %collective-permute-start.11) | collective-permute-done | bytes 20512 | tf_op jit(solution)/shard_map/ppermute | solution.py:450
  51.7 2.3 %collective-permute-done.10 = f32[40,128]{1,0:T(8,128)S(1)} collective-permute-done((f32[40,128]{1,0:T(8,128)S(1)}, f32[40,128]{1,0:T(8,128)S(1)}, u32[]{:S(2)}, u32[]{:S(2)}) %collective-permute-start.10) | collective-permute-done | bytes 20512 | tf_op jit(solution)/shard_map/ppermute | solution.py:450
  54.0 0.0 collective-permute-done.9
  54.0 0.0 copy-done
  54.0 5.0 %shard_map.63 = (f32[2,32,6,8,128]{4,3,2,1,0:T(8,128)}, f32[2,2,32,32]{3,2,1,0:T(8,128)}) custom-call(f32[4]{0:T(128)S(1)} %copy-done, f32[40,128]{1,0:T(8,128)S(1)} %add_add_fusion.moments, bf16[24,192,256]{2,1,0:T(8,128)(2,1)S(1)} %get-tuple-element.23.basis), custom_call_target="tpu_custom_call" | custom-call | tf_op jit(solution)/shard_map/pallas_call | solution.py:25
  (5 shorter events, 0.1 us)
Async XLA Ops:
  2.0 22.6 %collective-permute-start.2 = (f32[1544,128]{1,0:T(8,128)S(1)}, f32[1544,128]{1,0:T(8,128)S(1)}, u32[]{:S(2)}, u32[]{:S(2)}) collective-permute-start(f32[1544,128]{1,0:T(8,128)S(1)} %get-tuple-element.18), channel_id=1, source_target_pairs={{0,4},{1,5},{2,6},{3,7},{4,8},{5,9},{6,10},{7,11},{8,12},{9,13},{1... | collective-permute-start | bytes 2371592 | tf_op jit(solution)/shard_map/ppermute | solution.py:438
  2.1 22.5 %collective-permute-start.3 = (f32[1288,128]{1,0:T(8,128)S(1)}, f32[1288,128]{1,0:T(8,128)S(1)}, u32[]{:S(2)}, u32[]{:S(2)}) collective-permute-start(f32[1288,128]{1,0:T(8,128)S(1)} %get-tuple-element.19), channel_id=1, source_target_pairs={{0,252},{1,253},{2,254},{3,255},{4,0},{5,1},{6,2},{7,3},{8,4},{9,5... | collective-permute-start | bytes 1978376 | tf_op jit(solution)/shard_map/ppermute | solution.py:438
  9.9 6.9 %collective-permute-start = (f32[392,128]{1,0:T(8,128)S(1)}, f32[392,128]{1,0:T(8,128)S(1)}, u32[]{:S(2)}, u32[]{:S(2)}) collective-permute-start(f32[392,128]{1,0:T(8,128)S(1)} %get-tuple-element.16), channel_id=1, source_target_pairs={{0,1},{1,2},{2,3},{3,0},{4,5},{5,6},{6,7},{7,4},{8,9},{9,10},{10,1... | collective-permute-start | bytes 602120 | tf_op jit(solution)/shard_map/ppermute | solution.py:438
  11.4 5.4 %collective-permute-start.1 = (f32[328,128]{1,0:T(8,128)S(1)}, f32[328,128]{1,0:T(8,128)S(1)}, u32[]{:S(2)}, u32[]{:S(2)}) collective-permute-start(f32[328,128]{1,0:T(8,128)S(1)} %get-tuple-element.17), channel_id=1, source_target_pairs={{0,3},{1,0},{2,1},{3,2},{4,7},{5,4},{6,5},{7,6},{8,11},{9,8},{10,9... | collective-permute-start | bytes 503816 | tf_op jit(solution)/shard_map/ppermute | solution.py:438
  16.8 7.8 %collective-permute-start.4 = (f32[264,128]{1,0:T(8,128)S(1)}, f32[264,128]{1,0:T(8,128)S(1)}, u32[]{:S(2)}, u32[]{:S(2)}) collective-permute-start(f32[264,128]{1,0:T(8,128)S(1)} %get-tuple-element.20), channel_id=1, source_target_pairs={{0,4},{1,5},{2,6},{3,7},{4,8},{5,9},{6,10},{7,11},{8,12},{9,13},{1... | collective-permute-start | bytes 405512 | tf_op jit(solution)/shard_map/ppermute | solution.py:438
  16.9 7.7 %collective-permute-start.5 = (f32[264,128]{1,0:T(8,128)S(1)}, f32[264,128]{1,0:T(8,128)S(1)}, u32[]{:S(2)}, u32[]{:S(2)}) collective-permute-start(f32[264,128]{1,0:T(8,128)S(1)} %get-tuple-element.21), channel_id=1, source_target_pairs={{0,252},{1,253},{2,254},{3,255},{4,0},{5,1},{6,2},{7,3},{8,4},{9,5... | collective-permute-start | bytes 405512 | tf_op jit(solution)/shard_map/ppermute | solution.py:438
  22.5 31.5 %copy-start = (f32[4]{0:T(128)S(1)}, f32[4]{0:T(128)}, u32[]{:S(2)}) copy-start(f32[4]{0:T(128)} %eps.3) | copy-start | bytes 52
  39.5 6.0 %collective-permute-start.8 = (f32[40,128]{1,0:T(8,128)S(1)}, f32[40,128]{1,0:T(8,128)S(1)}, u32[]{:S(2)}, u32[]{:S(2)}) collective-permute-start(f32[40,128]{1,0:T(8,128)S(1)} %reduce_sum.9), channel_id=1, source_target_pairs={{0,48},{1,49},{2,50},{3,51},{4,52},{5,53},{6,54},{7,55},{8,56},{9,... | collective-permute-start | bytes 61448 | tf_op jit(solution)/shard_map/ppermute | solution.py:450
  40.8 6.8 %collective-permute-start.7 = (f32[40,128]{1,0:T(8,128)S(1)}, f32[40,128]{1,0:T(8,128)S(1)}, u32[]{:S(2)}, u32[]{:S(2)}) collective-permute-start(f32[40,128]{1,0:T(8,128)S(1)} %reduce_sum.9), channel_id=1, source_target_pairs={{0,40},{1,41},{2,42},{3,43},{4,44},{5,45},{6,46},{7,47},{8,32},{9,... | collective-permute-start | bytes 61448 | tf_op jit(solution)/shard_map/ppermute | solution.py:450
  41.7 5.9 %collective-permute-start.6 = (f32[40,128]{1,0:T(8,128)S(1)}, f32[40,128]{1,0:T(8,128)S(1)}, u32[]{:S(2)}, u32[]{:S(2)}) collective-permute-start(f32[40,128]{1,0:T(8,128)S(1)} %reduce_sum.9), channel_id=1, source_target_pairs={{0,16},{1,17},{2,18},{3,19},{4,20},{5,21},{6,22},{7,23},{8,24},{9,... | collective-permute-start | bytes 61448 | tf_op jit(solution)/shard_map/ppermute | solution.py:450
  47.7 4.0 %collective-permute-start.11 = (f32[40,128]{1,0:T(8,128)S(1)}, f32[40,128]{1,0:T(8,128)S(1)}, u32[]{:S(2)}, u32[]{:S(2)}) collective-permute-start(f32[40,128]{1,0:T(8,128)S(1)} %add_add_fusion.1), channel_id=1, source_target_pairs={{0,12},{1,13},{2,14},{3,15},{4,8},{5,9},{6,10},{7,11},{8,4},{9,5},... | collective-permute-start | bytes 61448 | tf_op jit(solution)/shard_map/ppermute | solution.py:450
  50.2 3.8 %collective-permute-start.10 = (f32[40,128]{1,0:T(8,128)S(1)}, f32[40,128]{1,0:T(8,128)S(1)}, u32[]{:S(2)}, u32[]{:S(2)}) collective-permute-start(f32[40,128]{1,0:T(8,128)S(1)} %add_add_fusion.1), channel_id=1, source_target_pairs={{0,8},{1,9},{2,10},{3,11},{4,12},{5,13},{6,14},{7,15},{8,0},{9,1},... | collective-permute-start | bytes 61448 | tf_op jit(solution)/shard_map/ppermute | solution.py:450
  50.2 3.8 %collective-permute-start.9 = (f32[40,128]{1,0:T(8,128)S(1)}, f32[40,128]{1,0:T(8,128)S(1)}, u32[]{:S(2)}, u32[]{:S(2)}) collective-permute-start(f32[40,128]{1,0:T(8,128)S(1)} %add_add_fusion.1), channel_id=1, source_target_pairs={{0,4},{1,5},{2,6},{3,7},{4,0},{5,1},{6,2},{7,3},{8,12},{9,13},{10,... | collective-permute-start | bytes 61448 | tf_op jit(solution)/shard_map/ppermute | solution.py:450

commit v8 on v7

--- a/solution.py
+++ b/solution.py
@@ -441,7 +441,7 @@
 def total_sum(value, deep, trans, devices):
     count = devices // (2 * deep)
     copies = jnp.broadcast_to(value[None], (count, *value.shape))
-    value = lax.all_to_all(copies, ("y", "x"), 0, 0, tiled=True).sum(0)
+    value = lax.all_to_all(copies, ("x", "y"), 0, 0, tiled=True).sum(0)
     core, near, middle, far = trans, 2 * trans, 4 * trans, 8 * trans
     rounds = [(middle, far ^ near, far ^ middle)] if deep == 8 else []
     rounds.append((core, near, core ^ near))

time: 59.3 us -> 58.8 us (level)
  blocking collectives: 12.3 us -> 11.6 us
    all_to_all x1, blocking collectives: 12.3 us -> 11.6 us  [total_sum(): value = lax.all_to_all(copies, ('x', 'y'), 0, 0, tiled=True).sum(0)]
where the time goes in v8:
time: 58.8 us; the launch traced here: 58.5 us
  starting transfers between devices  21.6 us (37%)
  waiting for transfers between devices  14.8 us (25%)
  blocking collectives  11.6 us (20%)
  Pallas kernels  9.46 us (16%)
  between operations  0.87 us (1%)
    ppermute x6, starting transfers between devices, moved(): return lax.ppermute(value, AXES, pairs)  15.1 us
    all_to_all x1, blocking collectives, total_sum(): value = lax.all_to_all(copies, ('x', 'y'), 0, 0, tiled=True).sum(0)  11.6 us
    pallas_call x5, Pallas kernels, call(): pl.pallas_call(body, out_shape=out_shape, in_specs=specs, out_specs=outs,...  9.46 us
    ppermute x6, waiting for transfers between devices, total_sum(): lax.ppermute(value, AXES, [(i, i ^ m) for i in range(devices)])  7.87 us
    ppermute x6, waiting for transfers between devices, moved(): return lax.ppermute(value, AXES, pairs)  6.98 us
    ppermute x6, starting transfers between devices, total_sum(): lax.ppermute(value, AXES, [(i, i ^ m) for i in range(devices)])  6.55 us
  transfers between devices with their start and end apart: 12, of which 6 were waited for; matrix products, arithmetic and copies ran while one was open for 0% of the time, Pallas kernels for 1%

profile of v8, /device:TPU:2, one launch (start us, length us, event | category | flops | bytes accessed | tf_op | source)
XLA Modules:
  0.0 58.5 jit_solution(7162499355604520521)
XLA Ops:
  0.6 1.4 %shard_map.59 = (f32[2,3,8,32,128]{4,3,2,1,0:T(8,128)S(1)}, f32[2,8,128]{2,1,0:T(8,128)S(1)}, f32[392,128]{1,0:T(8,128)S(1)}, f32[328,128]{1,0:T(8,128)S(1)}, f3...) custom-call(f32[4]{0:T(128)} %eps.3, s32[2,8,128]{2,1,0:T(8,128)} %material.1, s32[2,8,128]{2,1,0:T(8,128)} %mask.1, ...), custom_call_target="tpu_custom_call" | custom-call | tf_op jit(solution)/shard_map/pallas_call | solution.py:25
  2.0 0.1 collective-permute-start.2
  2.1 7.8 %collective-permute-start.3 = (f32[1288,128]{1,0:T(8,128)S(1)}, f32[1288,128]{1,0:T(8,128)S(1)}, u32[]{:S(2)}, u32[]{:S(2)}) collective-permute-start(f32[1288,128]{1,0:T(8,128)S(1)} %get-tuple-element.19), channel_id=1, source_target_pairs={{0,252},{1,253},{2,254},{3,255},{4,0},{5,1},{6,2},{7,3},{8,4},{9,5... | collective-permute-start | bytes 1978376 | tf_op jit(solution)/shard_map/ppermute | solution.py:438
  9.9 1.5 %collective-permute-start = (f32[392,128]{1,0:T(8,128)S(1)}, f32[392,128]{1,0:T(8,128)S(1)}, u32[]{:S(2)}, u32[]{:S(2)}) collective-permute-start(f32[392,128]{1,0:T(8,128)S(1)} %get-tuple-element.16), channel_id=1, source_target_pairs={{0,1},{1,2},{2,3},{3,0},{4,5},{5,6},{6,7},{7,4},{8,9},{9,10},{10,1... | collective-permute-start | bytes 602120 | tf_op jit(solution)/shard_map/ppermute | solution.py:438
  11.4 0.5 collective-permute-start.1
  12.0 4.8 %collective-permute-done.1.after.refs_1_ = f32[328,128]{1,0:T(8,128)S(1)} collective-permute-done((f32[328,128]{1,0:T(8,128)S(1)}, f32[328,128]{1,0:T(8,128)S(1)}, u32[]{:S(2)}, u32[]{:S(2)}) %collective-permute-start.1) | collective-permute-done | bytes 167968 | tf_op jit(solution)/shard_map/ppermute | solution.py:438
  16.8 0.0 collective-permute-done.before.refs_0_
  16.8 0.1 collective-permute-start.4
  16.9 5.1 %collective-permute-start.5 = (f32[264,128]{1,0:T(8,128)S(1)}, f32[264,128]{1,0:T(8,128)S(1)}, u32[]{:S(2)}, u32[]{:S(2)}) collective-permute-start(f32[264,128]{1,0:T(8,128)S(1)} %get-tuple-element.21), channel_id=1, source_target_pairs={{0,252},{1,253},{2,254},{3,255},{4,0},{5,1},{6,2},{7,3},{8,4},{9,5... | collective-permute-start | bytes 405512 | tf_op jit(solution)/shard_map/ppermute | solution.py:438
  22.0 0.5 shard_map.60.gram
  22.5 0.0 copy-start
  22.5 2.1 %collective-permute-done.4.refs_4_ = f32[264,128]{1,0:T(8,128)S(1)} collective-permute-done((f32[264,128]{1,0:T(8,128)S(1)}, f32[264,128]{1,0:T(8,128)S(1)}, u32[]{:S(2)}, u32[]{:S(2)}) %collective-permute-start.4) | collective-permute-done | bytes 135200 | tf_op jit(solution)/shard_map/ppermute | solution.py:438
  24.7 0.0 collective-permute-done.5.refs_5_
  24.7 0.0 collective-permute-done.3.refs_3_
  24.7 0.0 collective-permute-done.2.refs_2_
  24.7 2.6 %shard_map.62 = (bf16[24,192,256]{2,1,0:T(8,128)(2,1)S(1)}, f32[40,128]{1,0:T(8,128)S(1)}) custom-call(f32[2,3,8,32,128]{4,3,2,1,0:T(8,128)S(1)} %get-tuple-element.14.s0, f32[2,8,128]{2,1,0:T(8,128)S(1)} %get-tuple-element.15.diag, f32[32,32]{1,0:T(8,128)S(1)} %shard_map.60.gram, f32[392,128]{1,0:T(8,128)S(1)} %collective-permute-done.before.refs_0_, ...), custom_call_target="tpu_custom_call" | custom-call | tf_op jit(solution)/shard_map/pallas_call | solution.py:25
  27.3 11.6 %all_to_all.5 = f32[16,40,128]{2,1,0:T(8,128)S(1)} all-to-all(f32[16,40,128]{2,1,0:T(8,128)S(1)} %broadcast_in_dim.2), channel_id=1, replica_groups=mesh['y'=4,'z'=8,'core'=2,'x'=4] {'x','y'}, dimensions={0} | all-to-all | bytes 655360 | tf_op jit(solution)/shard_map/all_to_all | solution.py:444
  38.9 1.0 %collective-permute-start.8 = (f32[40,128]{1,0:T(8,128)S(1)}, f32[40,128]{1,0:T(8,128)S(1)}, u32[]{:S(2)}, u32[]{:S(2)}) collective-permute-start(f32[40,128]{1,0:T(8,128)S(1)} %reduce_sum.9), channel_id=1, source_target_pairs={{0,48},{1,49},{2,50},{3,51},{4,52},{5,53},{6,54},{7,55},{8,56},{9,... | collective-permute-start | bytes 61448 | tf_op jit(solution)/shard_map/ppermute | solution.py:450
  39.9 1.2 %collective-permute-start.7 = (f32[40,128]{1,0:T(8,128)S(1)}, f32[40,128]{1,0:T(8,128)S(1)}, u32[]{:S(2)}, u32[]{:S(2)}) collective-permute-start(f32[40,128]{1,0:T(8,128)S(1)} %reduce_sum.9), channel_id=1, source_target_pairs={{0,40},{1,41},{2,42},{3,43},{4,44},{5,45},{6,46},{7,47},{8,32},{9,... | collective-permute-start | bytes 61448 | tf_op jit(solution)/shard_map/ppermute | solution.py:450
  41.0 1.3 %collective-permute-start.6 = (f32[40,128]{1,0:T(8,128)S(1)}, f32[40,128]{1,0:T(8,128)S(1)}, u32[]{:S(2)}, u32[]{:S(2)}) collective-permute-start(f32[40,128]{1,0:T(8,128)S(1)} %reduce_sum.9), channel_id=1, source_target_pairs={{0,16},{1,17},{2,18},{3,19},{4,20},{5,21},{6,22},{7,23},{8,24},{9,... | collective-permute-start | bytes 61448 | tf_op jit(solution)/shard_map/ppermute | solution.py:450
  42.4 2.5 %collective-permute-done.8 = f32[40,128]{1,0:T(8,128)S(1)} collective-permute-done((f32[40,128]{1,0:T(8,128)S(1)}, f32[40,128]{1,0:T(8,128)S(1)}, u32[]{:S(2)}, u32[]{:S(2)}) %collective-permute-start.8) | collective-permute-done | bytes 20512 | tf_op jit(solution)/shard_map/ppermute | solution.py:450
  44.9 1.8 %collective-permute-done.7 = f32[40,128]{1,0:T(8,128)S(1)} collective-permute-done((f32[40,128]{1,0:T(8,128)S(1)}, f32[40,128]{1,0:T(8,128)S(1)}, u32[]{:S(2)}, u32[]{:S(2)}) %collective-permute-start.7) | collective-permute-done | bytes 20512 | tf_op jit(solution)/shard_map/ppermute | solution.py:450
  46.7 0.0 collective-permute-done.6
  46.7 2.8 %collective-permute-start.11 = (f32[40,128]{1,0:T(8,128)S(1)}, f32[40,128]{1,0:T(8,128)S(1)}, u32[]{:S(2)}, u32[]{:S(2)}) collective-permute-start(f32[40,128]{1,0:T(8,128)S(1)} %add_add_fusion.1), channel_id=1, source_target_pairs={{0,12},{1,13},{2,14},{3,15},{4,8},{5,9},{6,10},{7,11},{8,4},{9,5},... | collective-permute-start | bytes 61448 | tf_op jit(solution)/shard_map/ppermute | solution.py:450
  49.5 0.0 collective-permute-start.10
  49.5 0.2 collective-permute-start.9
  49.7 1.3 %collective-permute-done.11 = f32[40,128]{1,0:T(8,128)S(1)} collective-permute-done((f32[40,128]{1,0:T(8,128)S(1)}, f32[40,128]{1,0:T(8,128)S(1)}, u32[]{:S(2)}, u32[]{:S(2)}) %collective-permute-start.11) | collective-permute-done | bytes 20512 | tf_op jit(solution)/shard_map/ppermute | solution.py:450
  51.0 2.3 %collective-permute-done.10 = f32[40,128]{1,0:T(8,128)S(1)} collective-permute-done((f32[40,128]{1,0:T(8,128)S(1)}, f32[40,128]{1,0:T(8,128)S(1)}, u32[]{:S(2)}, u32[]{:S(2)}) %collective-permute-start.10) | collective-permute-done | bytes 20512 | tf_op jit(solution)/shard_map/ppermute | solution.py:450
  53.3 0.0 collective-permute-done.9
  53.3 0.0 copy-done
  53.3 5.0 %shard_map.63 = (f32[2,32,6,8,128]{4,3,2,1,0:T(8,128)}, f32[2,2,32,32]{3,2,1,0:T(8,128)}) custom-call(f32[4]{0:T(128)S(1)} %copy-done, f32[40,128]{1,0:T(8,128)S(1)} %add_add_fusion.moments, bf16[24,192,256]{2,1,0:T(8,128)(2,1)S(1)} %get-tuple-element.23.basis), custom_call_target="tpu_custom_call" | custom-call | tf_op jit(solution)/shard_map/pallas_call | solution.py:25
  (5 shorter events, 0.1 us)
Async XLA Ops:
  2.0 22.6 %collective-permute-start.2 = (f32[1544,128]{1,0:T(8,128)S(1)}, f32[1544,128]{1,0:T(8,128)S(1)}, u32[]{:S(2)}, u32[]{:S(2)}) collective-permute-start(f32[1544,128]{1,0:T(8,128)S(1)} %get-tuple-element.18), channel_id=1, source_target_pairs={{0,4},{1,5},{2,6},{3,7},{4,8},{5,9},{6,10},{7,11},{8,12},{9,13},{1... | collective-permute-start | bytes 2371592 | tf_op jit(solution)/shard_map/ppermute | solution.py:438
  2.1 22.5 %collective-permute-start.3 = (f32[1288,128]{1,0:T(8,128)S(1)}, f32[1288,128]{1,0:T(8,128)S(1)}, u32[]{:S(2)}, u32[]{:S(2)}) collective-permute-start(f32[1288,128]{1,0:T(8,128)S(1)} %get-tuple-element.19), channel_id=1, source_target_pairs={{0,252},{1,253},{2,254},{3,255},{4,0},{5,1},{6,2},{7,3},{8,4},{9,5... | collective-permute-start | bytes 1978376 | tf_op jit(solution)/shard_map/ppermute | solution.py:438
  9.9 6.9 %collective-permute-start = (f32[392,128]{1,0:T(8,128)S(1)}, f32[392,128]{1,0:T(8,128)S(1)}, u32[]{:S(2)}, u32[]{:S(2)}) collective-permute-start(f32[392,128]{1,0:T(8,128)S(1)} %get-tuple-element.16), channel_id=1, source_target_pairs={{0,1},{1,2},{2,3},{3,0},{4,5},{5,6},{6,7},{7,4},{8,9},{9,10},{10,1... | collective-permute-start | bytes 602120 | tf_op jit(solution)/shard_map/ppermute | solution.py:438
  11.4 5.4 %collective-permute-start.1 = (f32[328,128]{1,0:T(8,128)S(1)}, f32[328,128]{1,0:T(8,128)S(1)}, u32[]{:S(2)}, u32[]{:S(2)}) collective-permute-start(f32[328,128]{1,0:T(8,128)S(1)} %get-tuple-element.17), channel_id=1, source_target_pairs={{0,3},{1,0},{2,1},{3,2},{4,7},{5,4},{6,5},{7,6},{8,11},{9,8},{10,9... | collective-permute-start | bytes 503816 | tf_op jit(solution)/shard_map/ppermute | solution.py:438
  16.8 7.8 %collective-permute-start.4 = (f32[264,128]{1,0:T(8,128)S(1)}, f32[264,128]{1,0:T(8,128)S(1)}, u32[]{:S(2)}, u32[]{:S(2)}) collective-permute-start(f32[264,128]{1,0:T(8,128)S(1)} %get-tuple-element.20), channel_id=1, source_target_pairs={{0,4},{1,5},{2,6},{3,7},{4,8},{5,9},{6,10},{7,11},{8,12},{9,13},{1... | collective-permute-start | bytes 405512 | tf_op jit(solution)/shard_map/ppermute | solution.py:438
  16.9 7.7 %collective-permute-start.5 = (f32[264,128]{1,0:T(8,128)S(1)}, f32[264,128]{1,0:T(8,128)S(1)}, u32[]{:S(2)}, u32[]{:S(2)}) collective-permute-start(f32[264,128]{1,0:T(8,128)S(1)} %get-tuple-element.21), channel_id=1, source_target_pairs={{0,252},{1,253},{2,254},{3,255},{4,0},{5,1},{6,2},{7,3},{8,4},{9,5... | collective-permute-start | bytes 405512 | tf_op jit(solution)/shard_map/ppermute | solution.py:438
  22.5 30.8 %copy-start = (f32[4]{0:T(128)S(1)}, f32[4]{0:T(128)}, u32[]{:S(2)}) copy-start(f32[4]{0:T(128)} %eps.3) | copy-start | bytes 52
  38.9 6.0 %collective-permute-start.8 = (f32[40,128]{1,0:T(8,128)S(1)}, f32[40,128]{1,0:T(8,128)S(1)}, u32[]{:S(2)}, u32[]{:S(2)}) collective-permute-start(f32[40,128]{1,0:T(8,128)S(1)} %reduce_sum.9), channel_id=1, source_target_pairs={{0,48},{1,49},{2,50},{3,51},{4,52},{5,53},{6,54},{7,55},{8,56},{9,... | collective-permute-start | bytes 61448 | tf_op jit(solution)/shard_map/ppermute | solution.py:450
  39.9 6.8 %collective-permute-start.7 = (f32[40,128]{1,0:T(8,128)S(1)}, f32[40,128]{1,0:T(8,128)S(1)}, u32[]{:S(2)}, u32[]{:S(2)}) collective-permute-start(f32[40,128]{1,0:T(8,128)S(1)} %reduce_sum.9), channel_id=1, source_target_pairs={{0,40},{1,41},{2,42},{3,43},{4,44},{5,45},{6,46},{7,47},{8,32},{9,... | collective-permute-start | bytes 61448 | tf_op jit(solution)/shard_map/ppermute | solution.py:450
  41.0 5.6 %collective-permute-start.6 = (f32[40,128]{1,0:T(8,128)S(1)}, f32[40,128]{1,0:T(8,128)S(1)}, u32[]{:S(2)}, u32[]{:S(2)}) collective-permute-start(f32[40,128]{1,0:T(8,128)S(1)} %reduce_sum.9), channel_id=1, source_target_pairs={{0,16},{1,17},{2,18},{3,19},{4,20},{5,21},{6,22},{7,23},{8,24},{9,... | collective-permute-start | bytes 61448 | tf_op jit(solution)/shard_map/ppermute | solution.py:450
  46.7 4.3 %collective-permute-start.11 = (f32[40,128]{1,0:T(8,128)S(1)}, f32[40,128]{1,0:T(8,128)S(1)}, u32[]{:S(2)}, u32[]{:S(2)}) collective-permute-start(f32[40,128]{1,0:T(8,128)S(1)} %add_add_fusion.1), channel_id=1, source_target_pairs={{0,12},{1,13},{2,14},{3,15},{4,8},{5,9},{6,10},{7,11},{8,4},{9,5},... | collective-permute-start | bytes 61448 | tf_op jit(solution)/shard_map/ppermute | solution.py:450
  49.5 3.8 %collective-permute-start.10 = (f32[40,128]{1,0:T(8,128)S(1)}, f32[40,128]{1,0:T(8,128)S(1)}, u32[]{:S(2)}, u32[]{:S(2)}) collective-permute-start(f32[40,128]{1,0:T(8,128)S(1)} %add_add_fusion.1), channel_id=1, source_target_pairs={{0,8},{1,9},{2,10},{3,11},{4,12},{5,13},{6,14},{7,15},{8,0},{9,1},... | collective-permute-start | bytes 61448 | tf_op jit(solution)/shard_map/ppermute | solution.py:450
  49.5 3.8 %collective-permute-start.9 = (f32[40,128]{1,0:T(8,128)S(1)}, f32[40,128]{1,0:T(8,128)S(1)}, u32[]{:S(2)}, u32[]{:S(2)}) collective-permute-start(f32[40,128]{1,0:T(8,128)S(1)} %add_add_fusion.1), channel_id=1, source_target_pairs={{0,4},{1,5},{2,6},{3,7},{4,0},{5,1},{6,2},{7,3},{8,12},{9,13},{10,... | collective-permute-start | bytes 61448 | tf_op jit(solution)/shard_map/ppermute | solution.py:450

commit v9 on v8

--- a/solution.py
+++ b/solution.py
@@ -384,7 +384,7 @@
     )
     rows = 3 * zs * xs
 
-    flat = staged.reshape(2, w * rows, ny)
+    flat = staged.reshape(2, (w + 1) * rows, ny)
 
     def combine(block, mix, depth):
         found = []
@@ -396,7 +396,8 @@
                 flat[block, pl.ds(at, w, stride=rows), :] = value[:, k * ny : (k + 1) * ny]
             if x == xs - 2:
                 plane = c * zs + z
-                source, target = staged.at[block, :, plane], out.at[block, :, plane]
+                source = staged.at[block, pl.ds(0, w), plane]
+                target = out.at[block, :, plane]
                 found.append(pltpu.make_async_copy(source, target, sems.at[block, plane]))
                 found[-1].start()
         return found
@@ -467,7 +468,7 @@
         [eps_table, material, pml_mask, start_block.reshape(rows, ny)],
         hbm=(0, 1, 2, 3),
         scratch=[
-            pltpu.VMEM((rows, ny), jnp.float32),
+            pltpu.VMEM((rows + 3 * zs * xs, ny), jnp.float32),
             pltpu.VMEM((zs, xs, ny), jnp.int32),
             pltpu.VMEM((zs, xs, ny), jnp.int32),
             pltpu.SMEM((classes,), jnp.float32),
@@ -504,7 +505,7 @@
         smem=(0,),
         hbm_out=(0,),
         scratch=[
-            pltpu.VMEM((2, width, 3 * zs, xs, ny), jnp.float32),
+            pltpu.VMEM((2, width + 1, 3 * zs, xs, ny), jnp.float32),
             pltpu.SemaphoreType.DMA((2, 3 * zs)),
         ],
     )

time: 58.8 us -> 58.8 us (level)
  no operation moved by 1% of the time
where the time goes in v9:
time: 58.8 us; the launch traced here: 58.5 us
  starting transfers between devices  21.6 us (37%)
  waiting for transfers between devices  14.8 us (25%)
  blocking collectives  11.6 us (20%)
  Pallas kernels  9.46 us (16%)
  between operations  0.87 us (1%)
    ppermute x6, starting transfers between devices, moved(): return lax.ppermute(value, AXES, pairs)  15.1 us
    all_to_all x1, blocking collectives, total_sum(): value = lax.all_to_all(copies, ('x', 'y'), 0, 0, tiled=True).sum(0)  11.6 us
    pallas_call x5, Pallas kernels, call(): pl.pallas_call(body, out_shape=out_shape, in_specs=specs, out_specs=outs,...  9.46 us
    ppermute x6, waiting for transfers between devices, total_sum(): lax.ppermute(value, AXES, [(i, i ^ m) for i in range(devices)])  7.87 us
    ppermute x6, waiting for transfers between devices, moved(): return lax.ppermute(value, AXES, pairs)  6.98 us
    ppermute x6, starting transfers between devices, total_sum(): lax.ppermute(value, AXES, [(i, i ^ m) for i in range(devices)])  6.55 us
  transfers between devices with their start and end apart: 12, of which 6 were waited for; matrix products, arithmetic and copies ran while one was open for 0% of the time, Pallas kernels for 1%

profile of v9, /device:TPU:2, one launch (start us, length us, event | category | flops | bytes accessed | tf_op | source)
XLA Modules:
  0.0 58.5 jit_solution(5796164000726776929)
XLA Ops:
  0.6 1.4 %shard_map.59 = (f32[2,3,8,32,128]{4,3,2,1,0:T(8,128)S(1)}, f32[2,8,128]{2,1,0:T(8,128)S(1)}, f32[392,128]{1,0:T(8,128)S(1)}, f32[328,128]{1,0:T(8,128)S(1)}, f3...) custom-call(f32[4]{0:T(128)} %eps.3, s32[2,8,128]{2,1,0:T(8,128)} %material.1, s32[2,8,128]{2,1,0:T(8,128)} %mask.1, ...), custom_call_target="tpu_custom_call" | custom-call | tf_op jit(solution)/shard_map/pallas_call | solution.py:25
  2.0 0.1 collective-permute-start.2
  2.1 7.8 %collective-permute-start.3 = (f32[1288,128]{1,0:T(8,128)S(1)}, f32[1288,128]{1,0:T(8,128)S(1)}, u32[]{:S(2)}, u32[]{:S(2)}) collective-permute-start(f32[1288,128]{1,0:T(8,128)S(1)} %get-tuple-element.19), channel_id=1, source_target_pairs={{0,252},{1,253},{2,254},{3,255},{4,0},{5,1},{6,2},{7,3},{8,4},{9,5... | collective-permute-start | bytes 1978376 | tf_op jit(solution)/shard_map/ppermute | solution.py:439
  9.9 1.5 %collective-permute-start = (f32[392,128]{1,0:T(8,128)S(1)}, f32[392,128]{1,0:T(8,128)S(1)}, u32[]{:S(2)}, u32[]{:S(2)}) collective-permute-start(f32[392,128]{1,0:T(8,128)S(1)} %get-tuple-element.16), channel_id=1, source_target_pairs={{0,1},{1,2},{2,3},{3,0},{4,5},{5,6},{6,7},{7,4},{8,9},{9,10},{10,1... | collective-permute-start | bytes 602120 | tf_op jit(solution)/shard_map/ppermute | solution.py:439
  11.4 0.5 collective-permute-start.1
  12.0 4.8 %collective-permute-done.1.after.refs_1_ = f32[328,128]{1,0:T(8,128)S(1)} collective-permute-done((f32[328,128]{1,0:T(8,128)S(1)}, f32[328,128]{1,0:T(8,128)S(1)}, u32[]{:S(2)}, u32[]{:S(2)}) %collective-permute-start.1) | collective-permute-done | bytes 167968 | tf_op jit(solution)/shard_map/ppermute | solution.py:439
  16.8 0.0 collective-permute-done.before.refs_0_
  16.8 0.1 collective-permute-start.4
  16.9 5.1 %collective-permute-start.5 = (f32[264,128]{1,0:T(8,128)S(1)}, f32[264,128]{1,0:T(8,128)S(1)}, u32[]{:S(2)}, u32[]{:S(2)}) collective-permute-start(f32[264,128]{1,0:T(8,128)S(1)} %get-tuple-element.21), channel_id=1, source_target_pairs={{0,252},{1,253},{2,254},{3,255},{4,0},{5,1},{6,2},{7,3},{8,4},{9,5... | collective-permute-start | bytes 405512 | tf_op jit(solution)/shard_map/ppermute | solution.py:439
  22.0 0.5 shard_map.60.gram
  22.5 0.0 copy-start
  22.5 2.1 %collective-permute-done.4.refs_4_ = f32[264,128]{1,0:T(8,128)S(1)} collective-permute-done((f32[264,128]{1,0:T(8,128)S(1)}, f32[264,128]{1,0:T(8,128)S(1)}, u32[]{:S(2)}, u32[]{:S(2)}) %collective-permute-start.4) | collective-permute-done | bytes 135200 | tf_op jit(solution)/shard_map/ppermute | solution.py:439
  24.7 0.0 collective-permute-done.5.refs_5_
  24.7 0.0 collective-permute-done.3.refs_3_
  24.7 0.0 collective-permute-done.2.refs_2_
  24.7 2.6 %shard_map.62 = (bf16[24,192,256]{2,1,0:T(8,128)(2,1)S(1)}, f32[40,128]{1,0:T(8,128)S(1)}) custom-call(f32[2,3,8,32,128]{4,3,2,1,0:T(8,128)S(1)} %get-tuple-element.14.s0, f32[2,8,128]{2,1,0:T(8,128)S(1)} %get-tuple-element.15.diag, f32[32,32]{1,0:T(8,128)S(1)} %shard_map.60.gram, f32[392,128]{1,0:T(8,128)S(1)} %collective-permute-done.before.refs_0_, ...), custom_call_target="tpu_custom_call" | custom-call | tf_op jit(solution)/shard_map/pallas_call | solution.py:25
  27.3 11.6 %all_to_all.5 = f32[16,40,128]{2,1,0:T(8,128)S(1)} all-to-all(f32[16,40,128]{2,1,0:T(8,128)S(1)} %broadcast_in_dim.2), channel_id=1, replica_groups=mesh['y'=4,'z'=8,'core'=2,'x'=4] {'x','y'}, dimensions={0} | all-to-all | bytes 655360 | tf_op jit(solution)/shard_map/all_to_all | solution.py:445
  38.9 1.0 %collective-permute-start.8 = (f32[40,128]{1,0:T(8,128)S(1)}, f32[40,128]{1,0:T(8,128)S(1)}, u32[]{:S(2)}, u32[]{:S(2)}) collective-permute-start(f32[40,128]{1,0:T(8,128)S(1)} %reduce_sum.9), channel_id=1, source_target_pairs={{0,48},{1,49},{2,50},{3,51},{4,52},{5,53},{6,54},{7,55},{8,56},{9,... | collective-permute-start | bytes 61448 | tf_op jit(solution)/shard_map/ppermute | solution.py:451
  39.9 1.2 %collective-permute-start.7 = (f32[40,128]{1,0:T(8,128)S(1)}, f32[40,128]{1,0:T(8,128)S(1)}, u32[]{:S(2)}, u32[]{:S(2)}) collective-permute-start(f32[40,128]{1,0:T(8,128)S(1)} %reduce_sum.9), channel_id=1, source_target_pairs={{0,40},{1,41},{2,42},{3,43},{4,44},{5,45},{6,46},{7,47},{8,32},{9,... | collective-permute-start | bytes 61448 | tf_op jit(solution)/shard_map/ppermute | solution.py:451
  41.0 1.3 %collective-permute-start.6 = (f32[40,128]{1,0:T(8,128)S(1)}, f32[40,128]{1,0:T(8,128)S(1)}, u32[]{:S(2)}, u32[]{:S(2)}) collective-permute-start(f32[40,128]{1,0:T(8,128)S(1)} %reduce_sum.9), channel_id=1, source_target_pairs={{0,16},{1,17},{2,18},{3,19},{4,20},{5,21},{6,22},{7,23},{8,24},{9,... | collective-permute-start | bytes 61448 | tf_op jit(solution)/shard_map/ppermute | solution.py:451
  42.4 2.5 %collective-permute-done.8 = f32[40,128]{1,0:T(8,128)S(1)} collective-permute-done((f32[40,128]{1,0:T(8,128)S(1)}, f32[40,128]{1,0:T(8,128)S(1)}, u32[]{:S(2)}, u32[]{:S(2)}) %collective-permute-start.8) | collective-permute-done | bytes 20512 | tf_op jit(solution)/shard_map/ppermute | solution.py:451
  44.9 1.8 %collective-permute-done.7 = f32[40,128]{1,0:T(8,128)S(1)} collective-permute-done((f32[40,128]{1,0:T(8,128)S(1)}, f32[40,128]{1,0:T(8,128)S(1)}, u32[]{:S(2)}, u32[]{:S(2)}) %collective-permute-start.7) | collective-permute-done | bytes 20512 | tf_op jit(solution)/shard_map/ppermute | solution.py:451
  46.7 0.0 collective-permute-done.6
  46.7 2.8 %collective-permute-start.11 = (f32[40,128]{1,0:T(8,128)S(1)}, f32[40,128]{1,0:T(8,128)S(1)}, u32[]{:S(2)}, u32[]{:S(2)}) collective-permute-start(f32[40,128]{1,0:T(8,128)S(1)} %add_add_fusion.1), channel_id=1, source_target_pairs={{0,12},{1,13},{2,14},{3,15},{4,8},{5,9},{6,10},{7,11},{8,4},{9,5},... | collective-permute-start | bytes 61448 | tf_op jit(solution)/shard_map/ppermute | solution.py:451
  49.5 0.0 collective-permute-start.10
  49.5 0.2 collective-permute-start.9
  49.7 1.3 %collective-permute-done.11 = f32[40,128]{1,0:T(8,128)S(1)} collective-permute-done((f32[40,128]{1,0:T(8,128)S(1)}, f32[40,128]{1,0:T(8,128)S(1)}, u32[]{:S(2)}, u32[]{:S(2)}) %collective-permute-start.11) | collective-permute-done | bytes 20512 | tf_op jit(solution)/shard_map/ppermute | solution.py:451
  51.0 2.3 %collective-permute-done.10 = f32[40,128]{1,0:T(8,128)S(1)} collective-permute-done((f32[40,128]{1,0:T(8,128)S(1)}, f32[40,128]{1,0:T(8,128)S(1)}, u32[]{:S(2)}, u32[]{:S(2)}) %collective-permute-start.10) | collective-permute-done | bytes 20512 | tf_op jit(solution)/shard_map/ppermute | solution.py:451
  53.3 0.0 collective-permute-done.9
  53.3 0.0 copy-done
  53.3 5.0 %shard_map.63 = (f32[2,32,6,8,128]{4,3,2,1,0:T(8,128)}, f32[2,2,32,32]{3,2,1,0:T(8,128)}) custom-call(f32[4]{0:T(128)S(1)} %copy-done, f32[40,128]{1,0:T(8,128)S(1)} %add_add_fusion.moments, bf16[24,192,256]{2,1,0:T(8,128)(2,1)S(1)} %get-tuple-element.23.basis), custom_call_target="tpu_custom_call" | custom-call | tf_op jit(solution)/shard_map/pallas_call | solution.py:25
  (5 shorter events, 0.1 us)
Async XLA Ops:
  2.0 22.6 %collective-permute-start.2 = (f32[1544,128]{1,0:T(8,128)S(1)}, f32[1544,128]{1,0:T(8,128)S(1)}, u32[]{:S(2)}, u32[]{:S(2)}) collective-permute-start(f32[1544,128]{1,0:T(8,128)S(1)} %get-tuple-element.18), channel_id=1, source_target_pairs={{0,4},{1,5},{2,6},{3,7},{4,8},{5,9},{6,10},{7,11},{8,12},{9,13},{1... | collective-permute-start | bytes 2371592 | tf_op jit(solution)/shard_map/ppermute | solution.py:439
  2.1 22.5 %collective-permute-start.3 = (f32[1288,128]{1,0:T(8,128)S(1)}, f32[1288,128]{1,0:T(8,128)S(1)}, u32[]{:S(2)}, u32[]{:S(2)}) collective-permute-start(f32[1288,128]{1,0:T(8,128)S(1)} %get-tuple-element.19), channel_id=1, source_target_pairs={{0,252},{1,253},{2,254},{3,255},{4,0},{5,1},{6,2},{7,3},{8,4},{9,5... | collective-permute-start | bytes 1978376 | tf_op jit(solution)/shard_map/ppermute | solution.py:439
  9.9 6.9 %collective-permute-start = (f32[392,128]{1,0:T(8,128)S(1)}, f32[392,128]{1,0:T(8,128)S(1)}, u32[]{:S(2)}, u32[]{:S(2)}) collective-permute-start(f32[392,128]{1,0:T(8,128)S(1)} %get-tuple-element.16), channel_id=1, source_target_pairs={{0,1},{1,2},{2,3},{3,0},{4,5},{5,6},{6,7},{7,4},{8,9},{9,10},{10,1... | collective-permute-start | bytes 602120 | tf_op jit(solution)/shard_map/ppermute | solution.py:439
  11.4 5.4 %collective-permute-start.1 = (f32[328,128]{1,0:T(8,128)S(1)}, f32[328,128]{1,0:T(8,128)S(1)}, u32[]{:S(2)}, u32[]{:S(2)}) collective-permute-start(f32[328,128]{1,0:T(8,128)S(1)} %get-tuple-element.17), channel_id=1, source_target_pairs={{0,3},{1,0},{2,1},{3,2},{4,7},{5,4},{6,5},{7,6},{8,11},{9,8},{10,9... | collective-permute-start | bytes 503816 | tf_op jit(solution)/shard_map/ppermute | solution.py:439
  16.8 7.8 %collective-permute-start.4 = (f32[264,128]{1,0:T(8,128)S(1)}, f32[264,128]{1,0:T(8,128)S(1)}, u32[]{:S(2)}, u32[]{:S(2)}) collective-permute-start(f32[264,128]{1,0:T(8,128)S(1)} %get-tuple-element.20), channel_id=1, source_target_pairs={{0,4},{1,5},{2,6},{3,7},{4,8},{5,9},{6,10},{7,11},{8,12},{9,13},{1... | collective-permute-start | bytes 405512 | tf_op jit(solution)/shard_map/ppermute | solution.py:439
  16.9 7.7 %collective-permute-start.5 = (f32[264,128]{1,0:T(8,128)S(1)}, f32[264,128]{1,0:T(8,128)S(1)}, u32[]{:S(2)}, u32[]{:S(2)}) collective-permute-start(f32[264,128]{1,0:T(8,128)S(1)} %get-tuple-element.21), channel_id=1, source_target_pairs={{0,252},{1,253},{2,254},{3,255},{4,0},{5,1},{6,2},{7,3},{8,4},{9,5... | collective-permute-start | bytes 405512 | tf_op jit(solution)/shard_map/ppermute | solution.py:439
  22.5 30.8 %copy-start = (f32[4]{0:T(128)S(1)}, f32[4]{0:T(128)}, u32[]{:S(2)}) copy-start(f32[4]{0:T(128)} %eps.3) | copy-start | bytes 52
  38.9 6.0 %collective-permute-start.8 = (f32[40,128]{1,0:T(8,128)S(1)}, f32[40,128]{1,0:T(8,128)S(1)}, u32[]{:S(2)}, u32[]{:S(2)}) collective-permute-start(f32[40,128]{1,0:T(8,128)S(1)} %reduce_sum.9), channel_id=1, source_target_pairs={{0,48},{1,49},{2,50},{3,51},{4,52},{5,53},{6,54},{7,55},{8,56},{9,... | collective-permute-start | bytes 61448 | tf_op jit(solution)/shard_map/ppermute | solution.py:451
  39.9 6.8 %collective-permute-start.7 = (f32[40,128]{1,0:T(8,128)S(1)}, f32[40,128]{1,0:T(8,128)S(1)}, u32[]{:S(2)}, u32[]{:S(2)}) collective-permute-start(f32[40,128]{1,0:T(8,128)S(1)} %reduce_sum.9), channel_id=1, source_target_pairs={{0,40},{1,41},{2,42},{3,43},{4,44},{5,45},{6,46},{7,47},{8,32},{9,... | collective-permute-start | bytes 61448 | tf_op jit(solution)/shard_map/ppermute | solution.py:451
  41.0 5.6 %collective-permute-start.6 = (f32[40,128]{1,0:T(8,128)S(1)}, f32[40,128]{1,0:T(8,128)S(1)}, u32[]{:S(2)}, u32[]{:S(2)}) collective-permute-start(f32[40,128]{1,0:T(8,128)S(1)} %reduce_sum.9), channel_id=1, source_target_pairs={{0,16},{1,17},{2,18},{3,19},{4,20},{5,21},{6,22},{7,23},{8,24},{9,... | collective-permute-start | bytes 61448 | tf_op jit(solution)/shard_map/ppermute | solution.py:451
  46.7 4.3 %collective-permute-start.11 = (f32[40,128]{1,0:T(8,128)S(1)}, f32[40,128]{1,0:T(8,128)S(1)}, u32[]{:S(2)}, u32[]{:S(2)}) collective-permute-start(f32[40,128]{1,0:T(8,128)S(1)} %add_add_fusion.1), channel_id=1, source_target_pairs={{0,12},{1,13},{2,14},{3,15},{4,8},{5,9},{6,10},{7,11},{8,4},{9,5},... | collective-permute-start | bytes 61448 | tf_op jit(solution)/shard_map/ppermute | solution.py:451
  49.5 3.8 %collective-permute-start.10 = (f32[40,128]{1,0:T(8,128)S(1)}, f32[40,128]{1,0:T(8,128)S(1)}, u32[]{:S(2)}, u32[]{:S(2)}) collective-permute-start(f32[40,128]{1,0:T(8,128)S(1)} %add_add_fusion.1), channel_id=1, source_target_pairs={{0,8},{1,9},{2,10},{3,11},{4,12},{5,13},{6,14},{7,15},{8,0},{9,1},... | collective-permute-start | bytes 61448 | tf_op jit(solution)/shard_map/ppermute | solution.py:451
  49.5 3.8 %collective-permute-start.9 = (f32[40,128]{1,0:T(8,128)S(1)}, f32[40,128]{1,0:T(8,128)S(1)}, u32[]{:S(2)}, u32[]{:S(2)}) collective-permute-start(f32[40,128]{1,0:T(8,128)S(1)} %add_add_fusion.1), channel_id=1, source_target_pairs={{0,4},{1,5},{2,6},{3,7},{4,0},{5,1},{6,2},{7,3},{8,12},{9,13},{10,... | collective-permute-start | bytes 61448 | tf_op jit(solution)/shard_map/ppermute | solution.py:451

commit v10 on v9

--- a/solution.py
+++ b/solution.py
@@ -227,16 +227,17 @@
     return [(z, c, x) for z in range(zs) for c in range(3) for x in range(0, xs, 2)]
 
 
-def start_gram_body(zs, xs, s0, out):
+def start_gram_body(zs, xs, s0, out, split):
     total = None
-    for z, c, x in cell_pairs(zs, xs):
+    for i, (z, c, x) in enumerate(cell_pairs(zs, xs)):
         stack = jnp.concatenate(parts(pair(s0, z, c, x), 3), axis=0)
+        split[i] = stack
         term = product(stack, stack, 1)
         total = term if total is None else total + term
     out[...] = fold(total, *out.shape)
 
 
-def apply_body(halo, width, ny, slabs, trans, s0, diag, gram, *refs):
+def apply_body(halo, width, ny, slabs, trans, s0, diag, gram, split, *refs):
     zs, xs = halo.zs, halo.xs
     messages = dict(zip(halo.names, refs[:6]))
     basis, moments, s1, s2, outer = refs[6:]
@@ -296,7 +297,8 @@
 
     total = None
     for i, (z, c, x) in enumerate(cell_pairs(zs, xs)):
-        k0, k1, k2 = (parts(pair(s, z, c, x), 3) for s in (s0, s1, s2))
+        k0 = [split[i, k * width : (k + 1) * width] for k in range(3)]
+        k1, k2 = (parts(pair(s, z, c, x), 3) for s in (s1, s2))
         basis[i] = jnp.concatenate([k0[0], k1[0], k0[1], k1[1], k2[0], k2[1]], axis=0)
         left = jnp.concatenate([p for three in zip(k0, k1, k2) for p in three], axis=0)
         right = jnp.concatenate([p for two in zip(k1, k2) for p in two], axis=0)
@@ -482,7 +484,12 @@
         messages[:2],
     )
     messages += [moved(n, m, slabs, trans) for n, m in zip(halo.names[4:], passed)]
-    (gram,) = call(functools.partial(start_gram_body, zs, xs), [shape(width, width)], [s0])
+    pairs = len(cell_pairs(zs, xs))
+    gram, split = call(
+        functools.partial(start_gram_body, zs, xs),
+        [shape(width, width), jax.ShapeDtypeStruct((pairs, 3 * width, 2 * ny), jnp.bfloat16)],
+        [s0],
+    )
     outside = len(halo.first) - 3 * zs * xs
     basis, moments = call(
         functools.partial(apply_body, halo, width, ny, slabs, trans),
@@ -490,7 +497,7 @@
             jax.ShapeDtypeStruct((len(cell_pairs(zs, xs)), 6 * width, 2 * ny), jnp.bfloat16),
             shape(40, 4 * width),
         ],
-        [s0, diag, gram] + messages,
+        [s0, diag, gram, split] + messages,
         scratch=[
             pltpu.VMEM(field.shape, jnp.float32),
             pltpu.VMEM(field.shape, jnp.float32),

time: 58.8 us -> 58.8 us (level)
  no operation moved by 1% of the time
where the time goes in v10:
time: 58.8 us; the launch traced here: 58.4 us
  starting transfers between devices  21.6 us (37%)
  waiting for transfers between devices  14.9 us (25%)
  blocking collectives  11.6 us (20%)
  Pallas kernels  9.41 us (16%)
  between operations  0.87 us (1%)
    ppermute x6, starting transfers between devices, moved(): return lax.ppermute(value, AXES, pairs)  15.1 us
    all_to_all x1, blocking collectives, total_sum(): value = lax.all_to_all(copies, ('x', 'y'), 0, 0, tiled=True).sum(0)  11.6 us
    pallas_call x5, Pallas kernels, call(): pl.pallas_call(body, out_shape=out_shape, in_specs=specs, out_specs=outs,...  9.41 us
    ppermute x6, waiting for transfers between devices, total_sum(): lax.ppermute(value, AXES, [(i, i ^ m) for i in range(devices)])  7.86 us
    ppermute x6, waiting for transfers between devices, moved(): return lax.ppermute(value, AXES, pairs)  7 us
    ppermute x6, starting transfers between devices, total_sum(): lax.ppermute(value, AXES, [(i, i ^ m) for i in range(devices)])  6.55 us
  transfers between devices with their start and end apart: 12, of which 6 were waited for; matrix products, arithmetic and copies ran while one was open for 0% of the time, Pallas kernels for 1%

profile of v10, /device:TPU:2, one launch (start us, length us, event | category | flops | bytes accessed | tf_op | source)
XLA Modules:
  0.0 58.4 jit_solution(13741628747390104609)
XLA Ops:
  0.6 1.4 %shard_map.59 = (f32[2,3,8,32,128]{4,3,2,1,0:T(8,128)S(1)}, f32[2,8,128]{2,1,0:T(8,128)S(1)}, f32[392,128]{1,0:T(8,128)S(1)}, f32[328,128]{1,0:T(8,128)S(1)}, f3...) custom-call(f32[4]{0:T(128)} %eps.3, s32[2,8,128]{2,1,0:T(8,128)} %material.1, s32[2,8,128]{2,1,0:T(8,128)} %mask.1, ...), custom_call_target="tpu_custom_call" | custom-call | tf_op jit(solution)/shard_map/pallas_call | solution.py:25
  2.0 0.1 collective-permute-start.2
  2.1 7.8 %collective-permute-start.3 = (f32[1288,128]{1,0:T(8,128)S(1)}, f32[1288,128]{1,0:T(8,128)S(1)}, u32[]{:S(2)}, u32[]{:S(2)}) collective-permute-start(f32[1288,128]{1,0:T(8,128)S(1)} %get-tuple-element.23), channel_id=1, source_target_pairs={{0,252},{1,253},{2,254},{3,255},{4,0},{5,1},{6,2},{7,3},{8,4},{9,5... | collective-permute-start | bytes 1978376 | tf_op jit(solution)/shard_map/ppermute | solution.py:441
  9.9 1.5 %collective-permute-start = (f32[392,128]{1,0:T(8,128)S(1)}, f32[392,128]{1,0:T(8,128)S(1)}, u32[]{:S(2)}, u32[]{:S(2)}) collective-permute-start(f32[392,128]{1,0:T(8,128)S(1)} %get-tuple-element.20), channel_id=1, source_target_pairs={{0,1},{1,2},{2,3},{3,0},{4,5},{5,6},{6,7},{7,4},{8,9},{9,10},{10,1... | collective-permute-start | bytes 602120 | tf_op jit(solution)/shard_map/ppermute | solution.py:441
  11.4 0.5 collective-permute-start.1
  12.0 4.8 %collective-permute-done.1.after.refs_1_ = f32[328,128]{1,0:T(8,128)S(1)} collective-permute-done((f32[328,128]{1,0:T(8,128)S(1)}, f32[328,128]{1,0:T(8,128)S(1)}, u32[]{:S(2)}, u32[]{:S(2)}) %collective-permute-start.1) | collective-permute-done | bytes 167968 | tf_op jit(solution)/shard_map/ppermute | solution.py:441
  16.8 0.0 collective-permute-done.before.refs_0_
  16.8 0.1 collective-permute-start.4
  16.9 5.1 %collective-permute-start.5 = (f32[264,128]{1,0:T(8,128)S(1)}, f32[264,128]{1,0:T(8,128)S(1)}, u32[]{:S(2)}, u32[]{:S(2)}) collective-permute-start(f32[264,128]{1,0:T(8,128)S(1)} %get-tuple-element.25), channel_id=1, source_target_pairs={{0,252},{1,253},{2,254},{3,255},{4,0},{5,1},{6,2},{7,3},{8,4},{9,5... | collective-permute-start | bytes 405512 | tf_op jit(solution)/shard_map/ppermute | solution.py:441
  22.0 0.5 shard_map.60
  22.5 2.2 %collective-permute-done.4.refs_4_ = f32[264,128]{1,0:T(8,128)S(1)} collective-permute-done((f32[264,128]{1,0:T(8,128)S(1)}, f32[264,128]{1,0:T(8,128)S(1)}, u32[]{:S(2)}, u32[]{:S(2)}) %collective-permute-start.4) | collective-permute-done | bytes 135200 | tf_op jit(solution)/shard_map/ppermute | solution.py:441
  24.7 0.0 collective-permute-done.5.refs_5_
  24.7 0.0 collective-permute-done.3.refs_3_
  24.7 0.0 collective-permute-done.2.refs_2_
  24.7 0.0 copy-start
  24.7 2.5 %shard_map.62 = (bf16[24,192,256]{2,1,0:T(8,128)(2,1)S(1)}, f32[40,128]{1,0:T(8,128)S(1)}) custom-call(f32[2,3,8,32,128]{4,3,2,1,0:T(8,128)S(1)} %get-tuple-element.16.s0, f32[2,8,128]{2,1,0:T(8,128)S(1)} %get-tuple-element.17.diag, f32[32,32]{1,0:T(8,128)S(1)} %get-tuple-element.18.gram, bf16[24,96,256]{2,1,0:T(8,128)(2,1)S(1)} %get-tuple-element.19.split, ...), custom_call_target="tpu_custom_call" | custom-call | tf_op jit(solution)/shard_map/pallas_call | solution.py:25
  27.2 11.6 %all_to_all.5 = f32[16,40,128]{2,1,0:T(8,128)S(1)} all-to-all(f32[16,40,128]{2,1,0:T(8,128)S(1)} %broadcast_in_dim.2), channel_id=1, replica_groups=mesh['y'=4,'z'=8,'core'=2,'x'=4] {'x','y'}, dimensions={0} | all-to-all | bytes 655360 | tf_op jit(solution)/shard_map/all_to_all | solution.py:447
  38.8 1.0 %collective-permute-start.8 = (f32[40,128]{1,0:T(8,128)S(1)}, f32[40,128]{1,0:T(8,128)S(1)}, u32[]{:S(2)}, u32[]{:S(2)}) collective-permute-start(f32[40,128]{1,0:T(8,128)S(1)} %reduce_sum.9), channel_id=1, source_target_pairs={{0,48},{1,49},{2,50},{3,51},{4,52},{5,53},{6,54},{7,55},{8,56},{9,... | collective-permute-start | bytes 61448 | tf_op jit(solution)/shard_map/ppermute | solution.py:453
  39.8 1.2 %collective-permute-start.7 = (f32[40,128]{1,0:T(8,128)S(1)}, f32[40,128]{1,0:T(8,128)S(1)}, u32[]{:S(2)}, u32[]{:S(2)}) collective-permute-start(f32[40,128]{1,0:T(8,128)S(1)} %reduce_sum.9), channel_id=1, source_target_pairs={{0,40},{1,41},{2,42},{3,43},{4,44},{5,45},{6,46},{7,47},{8,32},{9,... | collective-permute-start | bytes 61448 | tf_op jit(solution)/shard_map/ppermute | solution.py:453
  41.0 1.3 %collective-permute-start.6 = (f32[40,128]{1,0:T(8,128)S(1)}, f32[40,128]{1,0:T(8,128)S(1)}, u32[]{:S(2)}, u32[]{:S(2)}) collective-permute-start(f32[40,128]{1,0:T(8,128)S(1)} %reduce_sum.9), channel_id=1, source_target_pairs={{0,16},{1,17},{2,18},{3,19},{4,20},{5,21},{6,22},{7,23},{8,24},{9,... | collective-permute-start | bytes 61448 | tf_op jit(solution)/shard_map/ppermute | solution.py:453
  42.3 2.5 %collective-permute-done.8 = f32[40,128]{1,0:T(8,128)S(1)} collective-permute-done((f32[40,128]{1,0:T(8,128)S(1)}, f32[40,128]{1,0:T(8,128)S(1)}, u32[]{:S(2)}, u32[]{:S(2)}) %collective-permute-start.8) | collective-permute-done | bytes 20512 | tf_op jit(solution)/shard_map/ppermute | solution.py:453
  44.8 1.8 %collective-permute-done.7 = f32[40,128]{1,0:T(8,128)S(1)} collective-permute-done((f32[40,128]{1,0:T(8,128)S(1)}, f32[40,128]{1,0:T(8,128)S(1)}, u32[]{:S(2)}, u32[]{:S(2)}) %collective-permute-start.7) | collective-permute-done | bytes 20512 | tf_op jit(solution)/shard_map/ppermute | solution.py:453
  46.6 0.0 collective-permute-done.6
  46.6 2.8 %collective-permute-start.11 = (f32[40,128]{1,0:T(8,128)S(1)}, f32[40,128]{1,0:T(8,128)S(1)}, u32[]{:S(2)}, u32[]{:S(2)}) collective-permute-start(f32[40,128]{1,0:T(8,128)S(1)} %add_add_fusion.1), channel_id=1, source_target_pairs={{0,12},{1,13},{2,14},{3,15},{4,8},{5,9},{6,10},{7,11},{8,4},{9,5},... | collective-permute-start | bytes 61448 | tf_op jit(solution)/shard_map/ppermute | solution.py:453
  49.5 0.0 collective-permute-start.10
  49.5 0.2 collective-permute-start.9
  49.7 1.3 %collective-permute-done.11 = f32[40,128]{1,0:T(8,128)S(1)} collective-permute-done((f32[40,128]{1,0:T(8,128)S(1)}, f32[40,128]{1,0:T(8,128)S(1)}, u32[]{:S(2)}, u32[]{:S(2)}) %collective-permute-start.11) | collective-permute-done | bytes 20512 | tf_op jit(solution)/shard_map/ppermute | solution.py:453
  50.9 2.3 %collective-permute-done.10 = f32[40,128]{1,0:T(8,128)S(1)} collective-permute-done((f32[40,128]{1,0:T(8,128)S(1)}, f32[40,128]{1,0:T(8,128)S(1)}, u32[]{:S(2)}, u32[]{:S(2)}) %collective-permute-start.10) | collective-permute-done | bytes 20512 | tf_op jit(solution)/shard_map/ppermute | solution.py:453
  53.2 0.0 collective-permute-done.9
  53.3 0.0 copy-done
  53.3 5.0 %shard_map.63 = (f32[2,32,6,8,128]{4,3,2,1,0:T(8,128)}, f32[2,2,32,32]{3,2,1,0:T(8,128)}) custom-call(f32[4]{0:T(128)S(1)} %copy-done, f32[40,128]{1,0:T(8,128)S(1)} %add_add_fusion.moments, bf16[24,192,256]{2,1,0:T(8,128)(2,1)S(1)} %get-tuple-element.27.basis), custom_call_target="tpu_custom_call" | custom-call | tf_op jit(solution)/shard_map/pallas_call | solution.py:25
  (5 shorter events, 0.1 us)
Async XLA Ops:
  2.0 22.6 %collective-permute-start.2 = (f32[1544,128]{1,0:T(8,128)S(1)}, f32[1544,128]{1,0:T(8,128)S(1)}, u32[]{:S(2)}, u32[]{:S(2)}) collective-permute-start(f32[1544,128]{1,0:T(8,128)S(1)} %get-tuple-element.22), channel_id=1, source_target_pairs={{0,4},{1,5},{2,6},{3,7},{4,8},{5,9},{6,10},{7,11},{8,12},{9,13},{1... | collective-permute-start | bytes 2371592 | tf_op jit(solution)/shard_map/ppermute | solution.py:441
  2.1 22.5 %collective-permute-start.3 = (f32[1288,128]{1,0:T(8,128)S(1)}, f32[1288,128]{1,0:T(8,128)S(1)}, u32[]{:S(2)}, u32[]{:S(2)}) collective-permute-start(f32[1288,128]{1,0:T(8,128)S(1)} %get-tuple-element.23), channel_id=1, source_target_pairs={{0,252},{1,253},{2,254},{3,255},{4,0},{5,1},{6,2},{7,3},{8,4},{9,5... | collective-permute-start | bytes 1978376 | tf_op jit(solution)/shard_map/ppermute | solution.py:441
  9.9 6.9 %collective-permute-start = (f32[392,128]{1,0:T(8,128)S(1)}, f32[392,128]{1,0:T(8,128)S(1)}, u32[]{:S(2)}, u32[]{:S(2)}) collective-permute-start(f32[392,128]{1,0:T(8,128)S(1)} %get-tuple-element.20), channel_id=1, source_target_pairs={{0,1},{1,2},{2,3},{3,0},{4,5},{5,6},{6,7},{7,4},{8,9},{9,10},{10,1... | collective-permute-start | bytes 602120 | tf_op jit(solution)/shard_map/ppermute | solution.py:441
  11.4 5.4 %collective-permute-start.1 = (f32[328,128]{1,0:T(8,128)S(1)}, f32[328,128]{1,0:T(8,128)S(1)}, u32[]{:S(2)}, u32[]{:S(2)}) collective-permute-start(f32[328,128]{1,0:T(8,128)S(1)} %get-tuple-element.21), channel_id=1, source_target_pairs={{0,3},{1,0},{2,1},{3,2},{4,7},{5,4},{6,5},{7,6},{8,11},{9,8},{10,9... | collective-permute-start | bytes 503816 | tf_op jit(solution)/shard_map/ppermute | solution.py:441
  16.8 7.8 %collective-permute-start.4 = (f32[264,128]{1,0:T(8,128)S(1)}, f32[264,128]{1,0:T(8,128)S(1)}, u32[]{:S(2)}, u32[]{:S(2)}) collective-permute-start(f32[264,128]{1,0:T(8,128)S(1)} %get-tuple-element.24), channel_id=1, source_target_pairs={{0,4},{1,5},{2,6},{3,7},{4,8},{5,9},{6,10},{7,11},{8,12},{9,13},{1... | collective-permute-start | bytes 405512 | tf_op jit(solution)/shard_map/ppermute | solution.py:441
  16.9 7.7 %collective-permute-start.5 = (f32[264,128]{1,0:T(8,128)S(1)}, f32[264,128]{1,0:T(8,128)S(1)}, u32[]{:S(2)}, u32[]{:S(2)}) collective-permute-start(f32[264,128]{1,0:T(8,128)S(1)} %get-tuple-element.25), channel_id=1, source_target_pairs={{0,252},{1,253},{2,254},{3,255},{4,0},{5,1},{6,2},{7,3},{8,4},{9,5... | collective-permute-start | bytes 405512 | tf_op jit(solution)/shard_map/ppermute | solution.py:441
  24.7 28.6 %copy-start = (f32[4]{0:T(128)S(1)}, f32[4]{0:T(128)}, u32[]{:S(2)}) copy-start(f32[4]{0:T(128)} %eps.3) | copy-start | bytes 52
  38.8 6.0 %collective-permute-start.8 = (f32[40,128]{1,0:T(8,128)S(1)}, f32[40,128]{1,0:T(8,128)S(1)}, u32[]{:S(2)}, u32[]{:S(2)}) collective-permute-start(f32[40,128]{1,0:T(8,128)S(1)} %reduce_sum.9), channel_id=1, source_target_pairs={{0,48},{1,49},{2,50},{3,51},{4,52},{5,53},{6,54},{7,55},{8,56},{9,... | collective-permute-start | bytes 61448 | tf_op jit(solution)/shard_map/ppermute | solution.py:453
  39.8 6.8 %collective-permute-start.7 = (f32[40,128]{1,0:T(8,128)S(1)}, f32[40,128]{1,0:T(8,128)S(1)}, u32[]{:S(2)}, u32[]{:S(2)}) collective-permute-start(f32[40,128]{1,0:T(8,128)S(1)} %reduce_sum.9), channel_id=1, source_target_pairs={{0,40},{1,41},{2,42},{3,43},{4,44},{5,45},{6,46},{7,47},{8,32},{9,... | collective-permute-start | bytes 61448 | tf_op jit(solution)/shard_map/ppermute | solution.py:453
  41.0 5.6 %collective-permute-start.6 = (f32[40,128]{1,0:T(8,128)S(1)}, f32[40,128]{1,0:T(8,128)S(1)}, u32[]{:S(2)}, u32[]{:S(2)}) collective-permute-start(f32[40,128]{1,0:T(8,128)S(1)} %reduce_sum.9), channel_id=1, source_target_pairs={{0,16},{1,17},{2,18},{3,19},{4,20},{5,21},{6,22},{7,23},{8,24},{9,... | collective-permute-start | bytes 61448 | tf_op jit(solution)/shard_map/ppermute | solution.py:453
  46.6 4.3 %collective-permute-start.11 = (f32[40,128]{1,0:T(8,128)S(1)}, f32[40,128]{1,0:T(8,128)S(1)}, u32[]{:S(2)}, u32[]{:S(2)}) collective-permute-start(f32[40,128]{1,0:T(8,128)S(1)} %add_add_fusion.1), channel_id=1, source_target_pairs={{0,12},{1,13},{2,14},{3,15},{4,8},{5,9},{6,10},{7,11},{8,4},{9,5},... | collective-permute-start | bytes 61448 | tf_op jit(solution)/shard_map/ppermute | solution.py:453
  49.5 3.8 %collective-permute-start.10 = (f32[40,128]{1,0:T(8,128)S(1)}, f32[40,128]{1,0:T(8,128)S(1)}, u32[]{:S(2)}, u32[]{:S(2)}) collective-permute-start(f32[40,128]{1,0:T(8,128)S(1)} %add_add_fusion.1), channel_id=1, source_target_pairs={{0,8},{1,9},{2,10},{3,11},{4,12},{5,13},{6,14},{7,15},{8,0},{9,1},... | collective-permute-start | bytes 61448 | tf_op jit(solution)/shard_map/ppermute | solution.py:453
  49.5 3.8 %collective-permute-start.9 = (f32[40,128]{1,0:T(8,128)S(1)}, f32[40,128]{1,0:T(8,128)S(1)}, u32[]{:S(2)}, u32[]{:S(2)}) collective-permute-start(f32[40,128]{1,0:T(8,128)S(1)} %add_add_fusion.1), channel_id=1, source_target_pairs={{0,4},{1,5},{2,6},{3,7},{4,0},{5,1},{6,2},{7,3},{8,12},{9,13},{10,... | collective-permute-start | bytes 61448 | tf_op jit(solution)/shard_map/ppermute | solution.py:453
